TPU v7x, 32 devices: a whole 2x2x4 slice. The times are simulated.
32 devices in a mesh: dp: 32 (over z, y, x, core).
Axes of the slice: x: 2, y: 2, z: 4, core: 2. Of those that a mesh axis runs over, the one named last changes fastest.
Arguments:
- bin_index: int32 [65536, 256], P('dp'), may hold values from 0 to 63
- node_ids: int32 [65536], P('dp'), may hold values from 0 to 1
- gradients: bfloat16 [65536, 32], P('dp'), may hold values from -6 to 6
- hessians: bfloat16 [65536, 32], P('dp'), may hold values from 0.02 to 0.25
Outputs:
- gains: float32 [256, 2, 64], replicated
- weights: float32 [256, 2, 64, 32], replicated
All inputs are finite; a program needn't handle non-finite values.
Results may differ from a plain program's by a relative error of at most 0.0003.
Values sent between devices are 32-bit elements; how exact they have to be, the bound alone decides.
No kernel may reach another device: no remote copies, remote signals or barrier semaphores. Data moves between devices by JAX's collectives and lax.ppermute only.
A program may use at most 128 MiB of HBM per device.

v0:
```python
import math

import jax
import jax.numpy as jnp
from jax import lax
from jax.sharding import PartitionSpec as P

B = 64
K = 32
NODES = 2


RIDGE = 1.0


def curves(hist):
    width = hist.shape[-1] // 2
    running = jnp.cumsum(hist, axis=2)
    totals = running[:, :, -1:, :]
    right_side = totals - running

    def score(part):
        return part[..., :width] * part[..., :width] / (part[..., width:] + RIDGE)

    gains = jnp.mean(score(running) + score(right_side) - score(totals), axis=-1)
    weights = -running[..., :width] / (running[..., width:] + RIDGE)
    return (gains, weights)


def arrange(hist):
    return jnp.transpose(hist.reshape(-1, B, NODES, 2 * K), (0, 2, 1, 3))


def on_device(bin_index, node_ids, gradients, hessians):
    devices = lax.axis_size("dp")
    rows_here = bin_index.shape[0]
    features = bin_index.shape[1]
    paired = jnp.concatenate([gradients, hessians], axis=1)
    select = (node_ids[:, None] == jnp.arange(NODES, dtype=jnp.int32)[None, :]).astype(jnp.bfloat16)
    spread = (select[:, :, None] * paired[:, None, :]).reshape(rows_here, NODES * 2 * K)
    row_step = math.gcd(rows_here, 256)
    levels = jnp.arange(B, dtype=jnp.int32)

    def add_block(index, total):
        start = index * row_step
        block_bins = lax.dynamic_slice_in_dim(bin_index, start, row_step, 0)
        block_spread = lax.dynamic_slice_in_dim(spread, start, row_step, 0)
        onehot = (block_bins[:, :, None] == levels[None, None, :]).astype(jnp.bfloat16)
        onehot = onehot.reshape(row_step, features // devices * B * lax.axis_size("dp"))
        return total + lax.dot_general(
            onehot, block_spread, (((0,), (0,)), ((), ())), preferred_element_type=jnp.float32
        )

    empty = jnp.zeros((features // devices * B * lax.axis_size("dp"), NODES * 2 * K), jnp.float32)
    owned = lax.psum_scatter(
        lax.fori_loop(0, rows_here // row_step, add_block, empty),
        "dp",
        scatter_dimension=0,
        tiled=True,
    )
    whole = lax.all_gather(owned, "dp", axis=0, tiled=True)
    gains, weights = curves(arrange(whole))
    return (gains, weights)


def solution(mesh):
    return jax.shard_map(
        on_device,
        mesh=mesh,
        in_specs=(P("dp", None), P("dp"), P("dp", None), P("dp", None)),
        out_specs=(P(), P()),
        check_vma=False,
    )
```

profile of v0, /device:TPU:0, one launch (start us, length us, event | category | flops | bytes accessed | tf_op | source)
XLA Modules:
  0.0 400.9 jit_solution(14070880033185225603)
XLA Ops:
  7.2 0.0 reduce-scatter.2.cloned.1.call-start
  7.2 0.7 compare_convert_fusion
  7.9 1.0 pad_maximum_fusion
  9.0 101.4 %while.14 = (s32[]{:T(128)}, f32[16384,128]{1,0:T(8,128)}, s32[2048,256]{1,0:T(8,128)}, bf16[2048,128]{0,1:T(8,128)(2,1)S(1)}, s32[]{:T(128)}, /*index=5*/s32[]{:T(128)}, s32[]{:T(128)}, s32[]{:T(128)}) while((s32[]{:T(128)}, f32[16384,128]{1,0:T(8,128)}, s32[2048,256]{1,0:T(8,128)}, bf16[2048,128]{0,1:T(8,128)(2,1)S(1)}, ...), condition=%wide.region_1.0_spmd.clone, body=%wide.region_0.0_spmd.clone.sunk | while | flops 1082130432 | bytes 26804380 | solution.py:56
  9.0 0.1 eq.75
  9.1 1.0 constant_dynamic-slice_fusion.2
  10.1 0.1 copy.23
  10.2 2.8 bitcast_compare_fusion.2
  13.1 5.7 %convolution_add_fusion.2 = f32[16384,128]{1,0:T(8,128)} fusion(pred[256,16384]{0,1:T(32,128)(4,1)S(1)} %bitcast_compare_fusion.2, f32[16384,128]{1,0:T(8,128)} %get-tuple-element.172, pred[]{:T(512)S(6)} %compare.3, bf16[2048,128]{0,1:T(8,128)(2,1)S(1)} %get-tuple-element.182, s32[]{:T(128)S(6)} %select_n.10), kind=kOutput, calls=%fused_computation.1.clone.1 | convolution fusion | flops 1077936128 | bytes 21037060 | tf_op jit(solution)/shard_map/while/body/eval_jaxpr/dot_general | solution.py:50
  18.7 0.1 eq.75
  18.8 1.0 constant_dynamic-slice_fusion.2
  19.8 0.1 copy.23
  19.9 2.8 bitcast_compare_fusion.2
  22.8 9.0 %convolution_add_fusion.2 = f32[16384,128]{1,0:T(8,128)} fusion(pred[256,16384]{0,1:T(32,128)(4,1)S(1)} %bitcast_compare_fusion.2, f32[16384,128]{1,0:T(8,128)} %get-tuple-element.172, pred[]{:T(512)S(6)} %compare.3, bf16[2048,128]{0,1:T(8,128)(2,1)S(1)} %get-tuple-element.182, s32[]{:T(128)S(6)} %select_n.10), kind=kOutput, calls=%fused_computation.1.clone.1 | convolution fusion | flops 1077936128 | bytes 21037060 | tf_op jit(solution)/shard_map/while/body/eval_jaxpr/dot_general | solution.py:50
  31.8 0.1 eq.75
  31.9 1.0 constant_dynamic-slice_fusion.2
  32.9 0.1 copy.23
  33.0 2.8 bitcast_compare_fusion.2
  35.9 9.0 %convolution_add_fusion.2 = f32[16384,128]{1,0:T(8,128)} fusion(pred[256,16384]{0,1:T(32,128)(4,1)S(1)} %bitcast_compare_fusion.2, f32[16384,128]{1,0:T(8,128)} %get-tuple-element.172, pred[]{:T(512)S(6)} %compare.3, bf16[2048,128]{0,1:T(8,128)(2,1)S(1)} %get-tuple-element.182, s32[]{:T(128)S(6)} %select_n.10), kind=kOutput, calls=%fused_computation.1.clone.1 | convolution fusion | flops 1077936128 | bytes 21037060 | tf_op jit(solution)/shard_map/while/body/eval_jaxpr/dot_general | solution.py:50
  44.9 0.1 eq.75
  45.0 1.0 constant_dynamic-slice_fusion.2
  46.0 0.1 copy.23
  46.1 2.8 bitcast_compare_fusion.2
  49.0 9.0 %convolution_add_fusion.2 = f32[16384,128]{1,0:T(8,128)} fusion(pred[256,16384]{0,1:T(32,128)(4,1)S(1)} %bitcast_compare_fusion.2, f32[16384,128]{1,0:T(8,128)} %get-tuple-element.172, pred[]{:T(512)S(6)} %compare.3, bf16[2048,128]{0,1:T(8,128)(2,1)S(1)} %get-tuple-element.182, s32[]{:T(128)S(6)} %select_n.10), kind=kOutput, calls=%fused_computation.1.clone.1 | convolution fusion | flops 1077936128 | bytes 21037060 | tf_op jit(solution)/shard_map/while/body/eval_jaxpr/dot_general | solution.py:50
  58.0 0.1 eq.75
  58.1 1.0 constant_dynamic-slice_fusion.2
  59.1 0.1 copy.23
  59.2 2.8 bitcast_compare_fusion.2
  62.1 9.0 %convolution_add_fusion.2 = f32[16384,128]{1,0:T(8,128)} fusion(pred[256,16384]{0,1:T(32,128)(4,1)S(1)} %bitcast_compare_fusion.2, f32[16384,128]{1,0:T(8,128)} %get-tuple-element.172, pred[]{:T(512)S(6)} %compare.3, bf16[2048,128]{0,1:T(8,128)(2,1)S(1)} %get-tuple-element.182, s32[]{:T(128)S(6)} %select_n.10), kind=kOutput, calls=%fused_computation.1.clone.1 | convolution fusion | flops 1077936128 | bytes 21037060 | tf_op jit(solution)/shard_map/while/body/eval_jaxpr/dot_general | solution.py:50
  71.1 0.1 eq.75
  71.2 1.0 constant_dynamic-slice_fusion.2
  72.2 0.1 copy.23
  72.3 2.8 bitcast_compare_fusion.2
  75.2 9.0 %convolution_add_fusion.2 = f32[16384,128]{1,0:T(8,128)} fusion(pred[256,16384]{0,1:T(32,128)(4,1)S(1)} %bitcast_compare_fusion.2, f32[16384,128]{1,0:T(8,128)} %get-tuple-element.172, pred[]{:T(512)S(6)} %compare.3, bf16[2048,128]{0,1:T(8,128)(2,1)S(1)} %get-tuple-element.182, s32[]{:T(128)S(6)} %select_n.10), kind=kOutput, calls=%fused_computation.1.clone.1 | convolution fusion | flops 1077936128 | bytes 21037060 | tf_op jit(solution)/shard_map/while/body/eval_jaxpr/dot_general | solution.py:50
  84.2 0.1 eq.75
  84.3 1.0 constant_dynamic-slice_fusion.2
  85.3 0.1 copy.23
  85.4 2.8 bitcast_compare_fusion.2
  88.3 9.0 %convolution_add_fusion.2 = f32[16384,128]{1,0:T(8,128)} fusion(pred[256,16384]{0,1:T(32,128)(4,1)S(1)} %bitcast_compare_fusion.2, f32[16384,128]{1,0:T(8,128)} %get-tuple-element.172, pred[]{:T(512)S(6)} %compare.3, bf16[2048,128]{0,1:T(8,128)(2,1)S(1)} %get-tuple-element.182, s32[]{:T(128)S(6)} %select_n.10), kind=kOutput, calls=%fused_computation.1.clone.1 | convolution fusion | flops 1077936128 | bytes 21037060 | tf_op jit(solution)/shard_map/while/body/eval_jaxpr/dot_general | solution.py:50
  97.3 0.1 eq.75
  97.4 1.0 constant_dynamic-slice_fusion.2
  98.4 0.1 copy.23
  98.5 2.8 bitcast_compare_fusion.2
  101.4 9.0 %convolution_add_fusion.2 = f32[16384,128]{1,0:T(8,128)} fusion(pred[256,16384]{0,1:T(32,128)(4,1)S(1)} %bitcast_compare_fusion.2, f32[16384,128]{1,0:T(8,128)} %get-tuple-element.172, pred[]{:T(512)S(6)} %compare.3, bf16[2048,128]{0,1:T(8,128)(2,1)S(1)} %get-tuple-element.182, s32[]{:T(128)S(6)} %select_n.10), kind=kOutput, calls=%fused_computation.1.clone.1 | convolution fusion | flops 1077936128 | bytes 21037060 | tf_op jit(solution)/shard_map/while/body/eval_jaxpr/dot_general | solution.py:50
  110.4 0.0 reduce-scatter.2.cloned.1.call-update
  110.4 0.0 all-gather.2.cloned.1.call-start
  110.5 151.5 %reduce-scatter.2.cloned.1.call-done = f32[512,128]{1,0:T(8,128)} async-done(((f32[16384,128]{1,0:T(8,128)}), f32[512,128]{1,0:T(8,128)}) %reduce-scatter.2.cloned.1.call-update) | async-done | bytes 262160 | tf_op jit(solution)/shard_map/reduce_scatter | solution.py:55
  262.0 0.0 all-gather.2.cloned.1.call-update
  262.0 76.2 %all-gather.2.cloned.1.call-done = f32[16384,128]{1,0:T(8,128)} async-done(((f32[512,128]{1,0:T(8,128)}), f32[16384,128]{1,0:T(8,128)}) %all-gather.2.cloned.1.call-update) | async-done | bytes 8388624 | tf_op jit(solution)/shard_map/all_gather | solution.py:61
  338.2 9.0 %copy.16 = f32[16384,128]{0,1:T(8,128)} copy(f32[16384,128]{1,0:T(8,128)} %all-gather.2.cloned.1.call-done) | data formatting | bytes 16777216 | tf_op jit(solution)/shard_map/all_gather | solution.py:61
  347.2 13.1 %reshape.45 = f32[256,64,2,64]{1,0,3,2:T(8,128)} reshape(f32[16384,128]{0,1:T(8,128)} %copy.16) | data formatting | bytes 16777216 | tf_op jit(solution)/shard_map/reshape | solution.py:31
  360.4 13.6 %copy.17 = f32[256,2,64,64]{0,3,1,2:T(8,128)} copy(f32[256,2,64,64]{2,0,3,1:T(8,128)} %bitcast.18) | data formatting | bytes 16777216 | tf_op jit(solution)/shard_map/transpose | solution.py:31
  374.0 7.4 %fusion.10 = f32[256,2,64,64]{0,3,1,2:T(8,128)} fusion(f32[256,2,64,64]{0,3,1,2:T(8,128)} %copy.17), kind=kOutput, calls=%fused_computation.24 | output fusion | flops 132120576 | bytes 16777216 | tf_op jit(solution)/shard_map/jit(cumsum)/reduce_window_sum | solution.py:18
  381.4 0.9 fusion.9
  382.3 0.0 slice-start
  382.3 1.1 slice_bitcast_fusion
  383.4 0.0 slice-start.1
  383.4 4.5 %broadcast_subtract_fusion = f32[256,2,64,64]{0,3,1,2:T(8,128)S(1)} fusion(f32[256,2,64,64]{0,3,1,2:T(8,128)} %fusion.10, f32[256,2,64]{0,2,1:T(8,128)S(1)} %slice_bitcast_fusion), kind=kLoop, calls=%fused_computation.13 | loop fusion | flops 2097152 | bytes 16908288 | tf_op jit(solution)/shard_map/sub | solution.py:20
  387.9 0.0 slice-done
  387.9 0.5 slice-done.1
  388.4 2.6 negate_divide_fusion
  391.0 2.3 copy.19
  393.3 0.1 broadcast_multiply_fusion.1
  393.4 0.7 copy.18
  (11 shorter events, 0.1 us)
Async XLA Ops:
  7.2 254.8 %reduce-scatter.2.cloned.1.call-start = ((), (), s32[]{:S(2)}) async-start(), calls=%async_computation.1 | async-start | bytes 8650752 | tf_op jit(solution)/shard_map/reduce_scatter | solution.py:55
  110.4 227.8 %all-gather.2.cloned.1.call-start = ((), (), s32[]{:S(2)}) async-start(), calls=%async_computation.2 | async-start | bytes 8650752 | tf_op jit(solution)/shard_map/all_gather | solution.py:61
  382.3 5.6 %slice-start = ((s8[8388608]{0:T(1024)(128)(4,1)}), s8[4194304]{0:T(1024)(128)(4,1)S(1)}, s32[]{:S(2)}) async-start(s8[8388608]{0:T(1024)(128)(4,1)} %bitcast.16), calls=%async_computation.3 | async-start | bytes 8388608
  383.4 5.1 %slice-start.1 = ((s8[8388608]{0:T(1024)(128)(4,1)}), s8[4194304]{0:T(1024)(128)(4,1)S(1)}, s32[]{:S(2)}) async-start(s8[8388608]{0:T(1024)(128)(4,1)} %bitcast.16), calls=%async_computation.4 | async-start | bytes 8388608
Sparse Core Ops, SparseCore 0:
  110.6 151.3 reduce-scatter.1
  264.9 73.3 all-gather.1
where the time goes:
time: 402 us; the launch traced here: 401 us
  waiting for transfers between devices  228 us (57%)
  matrix products  68.9 us (17%)
  local copies, waits for them, and re-layouts  49.9 us (12%)
  other arithmetic  39.9 us (10%)
  between operations  14.1 us (4%)
    reduce_scatter x1, waiting for transfers between devices, on_device(): lax.psum_scatter(lax.fori_loop(0, rows_here // row_step, add_block, empty...  152 us
    all_gather x1, waiting for transfers between devices, on_device(): whole = lax.all_gather(owned, 'dp', axis=0, tiled=True)  76.2 us
    dot_general x8, matrix products, add_block(): lax.dot_general(onehot, block_spread, (((0,), (0,)), ((), ())), preferred...  68.9 us
    eq x8, other arithmetic, add_block(): block_bins[:, :, None] == levels[None, None, :]  22.7 us
    transpose x1, local copies, waits for them, and re-layouts, arrange(): return jnp.transpose(hist.reshape(-1, B, NODES, 2 * K), (0, 2, 1, 3))  13.6 us
    reshape x1, local copies, waits for them, and re-layouts, arrange(): return jnp.transpose(hist.reshape(-1, B, NODES, 2 * K), (0, 2, 1, 3))  13.1 us
    all_gather x1, local copies, waits for them, and re-layouts, on_device(): whole = lax.all_gather(owned, 'dp', axis=0, tiled=True)  9.01 us
    dynamic_slice x16, local copies, waits for them, and re-layouts, add_block(): block_bins = lax.dynamic_slice_in_dim(bin_index, start, row_step, 0)  8.82 us
  transfers between devices with their start and end apart: 2, of which 2 were waited for; matrix products, arithmetic and copies ran while one was open for 0% of the time, Pallas kernels for 0%

commit v1 on v0

v1 whole, which is shorter than its diff:
```python
import functools

import jax
import jax.numpy as jnp
from jax import lax
from jax.experimental import pallas as pl
from jax.experimental.pallas import tpu as pltpu
from jax.sharding import PartitionSpec as P

B = 64
K = 32
NODES = 2
RIDGE = 1.0
LANES = 128
EXTRA = 8
VMEM_LIMIT = 48 * 2**20


class Plan:
    def __init__(self, devices):
        bits = devices.bit_length() - 1
        assert devices == 1 << bits and bits >= 4
        self.items = devices // 2
        self.bin_bits = bits - 2
        self.unit = 1 << self.bin_bits
        self.units = B // self.unit
        assert self.units >= 1
        first = [((2,), (4,)), ((4,), (2,))]
        rest = list(range(3, bits))
        later = []
        while rest:
            now, rest = rest[:2], rest[2:]
            masks = tuple(1 << b for b in now)
            later.append((masks, masks))
        self.stages = first + later
        self.flips = [[], []]
        for core in (0, 1):
            for stage in reversed(self.stages):
                self.flips[core].extend(stage[core])
        self.half_at = self.flips[0].index(devices // 2)
        assert self.flips[1][self.half_at] == devices // 2

    def mirrored(self, item):
        top = len(self.flips[0]) - 1
        differ = ((item >> top) ^ (item >> (top - 1))) & 1
        return item ^ (differ * (3 << (top - 1)))

    def sizes(self):
        share = self.units // 4
        return [share] * 4 if share else [1] * self.units

    def groups(self, stage):
        return 1 << len(self.stages[stage][0])

    def partner(self, stage, group, device):
        flip = 0
        for i, mask in enumerate(self.stages[stage][device & 1]):
            flip ^= mask * ((group >> i) & 1)
        return device ^ flip

    def mask(self, item, core):
        total = 0
        for i, (even, odd) in enumerate(zip(*self.flips, strict=True)):
            total = total ^ (((item >> i) & 1) * (even + core * (odd - even)))
        return total


def hist_body(plan, first_unit, count, has_totals, bins, spread, keep, send):
    me = lax.axis_index("dp")
    core = me & 1
    rows = bins.shape[0]
    step = min(rows, 256)
    half_at = plan.half_at
    low = (1 << half_at) - 1

    @pl.loop(0, plan.items // 2)
    def _(slot):
        item = ((slot >> half_at) << (half_at + 1)) | (slot & low)
        other = item | (1 << half_at)
        owner = (me ^ plan.mask(item, core)) >> 1
        low_bin = owner & (plan.unit - 1)
        for u in range(count):
            level = (first_unit + u) * plan.unit + low_bin
            level = level.astype(jnp.float32).astype(jnp.bfloat16)
            total = jnp.zeros((spread.shape[0], bins.shape[1]), jnp.float32)
            for start in range(0, rows, step):
                below = jnp.where(
                    bins[start : start + step, :] <= level, jnp.bfloat16(1), jnp.bfloat16(0)
                )
                total += jnp.dot(
                    spread[:, start : start + step], below, preferred_element_type=jnp.float32
                )
            at = pl.ds(u * 2 * K, 2 * K)
            keep[item, at, :] = total[: 2 * K, :LANES]
            keep[other, at, :] = total[: 2 * K, LANES:]
            send[plan.mirrored(item), at, :] = total[2 * K :, :LANES]
            send[plan.mirrored(other), at, :] = total[2 * K :, LANES:]
    if has_totals:
        sums = jnp.sum(spread[...].astype(jnp.float32), axis=1, keepdims=True)
        lane = lax.broadcasted_iota(jnp.int32, (EXTRA, LANES), 1)
        for target, base in ((keep, 0), (send, 2 * K)):
            packed = jnp.zeros((EXTRA, LANES), jnp.float32)
            for i in range(2 * K // EXTRA):
                part = sums[base + i * EXTRA : base + (i + 1) * EXTRA, :]
                packed = jnp.where(lane == i, part, packed)
            for item in range(plan.items):
                target[item, pl.ds(count * 2 * K, EXTRA), :] = packed


def first_kernel(plan, count, bins_ref, node_ref, grad_ref, hess_ref, keep, send, bins, spread):
    me = lax.axis_index("dp")
    core = me & 1
    half = me >> (plan.bin_bits + 1)
    raw = bins_ref[...].astype(jnp.float32).astype(jnp.bfloat16)
    swapped = jnp.concatenate([raw[:, LANES:], raw[:, :LANES]], axis=1)
    bins[...] = jnp.where(half == 0, raw, swapped)
    paired = jnp.concatenate([grad_ref[...], hess_ref[...]], axis=0).astype(jnp.float32)
    node = node_ref[...]
    for slot in range(NODES):
        here = (node == (core ^ slot)).astype(jnp.float32)
        spread[slot * 2 * K : (slot + 1) * 2 * K, :] = (paired * here).astype(jnp.bfloat16)
    hist_body(plan, 0, count, True, bins, spread, keep, send)


def next_kernel(plan, first_unit, count, bins, spread, keep, send):
    hist_body(plan, first_unit, count, False, bins, spread, keep, send)


def vmem(n):
    return [pl.BlockSpec(memory_space=pltpu.VMEM)] * n


def call(body, out_shape, n_in, flops=0, moved=0):
    return pl.pallas_call(
        body,
        out_shape=out_shape,
        in_specs=vmem(n_in),
        out_specs=vmem(len(out_shape)),
        compiler_params=pltpu.CompilerParams(vmem_limit_bytes=VMEM_LIMIT),
        cost_estimate=pl.CostEstimate(flops=flops, bytes_accessed=moved, transcendentals=0),
    )


def f32(*shape):
    return jax.ShapeDtypeStruct(shape, jnp.float32)


def add_body(mine, theirs, *outs):
    each = outs[0].shape[0]
    for i, out in enumerate(outs):
        out[...] = mine[i * each : (i + 1) * each] + theirs[i * each : (i + 1) * each]


def add_split(mine, theirs, groups):
    items, rows, lanes = mine.shape
    return call(
        add_body, [f32(items // groups, rows, lanes)] * groups, 2, moved=mine.size * 12
    )(mine, theirs)


def score(g, h):
    return g * g / (h + RIDGE)


def curves_body(count, first_unit, has_totals, last, n_parts, *refs):
    parts, refs = refs[:n_parts], refs[n_parts:]
    if has_totals:
        weights, totals, gains = refs
    elif last:
        packed, old_gains, weights = refs
    else:
        packed, old_gains, weights, gains = refs

    def summed(start, size):
        total = parts[0][0, start : start + size, :]
        for part in parts[1:]:
            total += part[0, start : start + size, :]
        return total

    if has_totals:
        block = summed(count * 2 * K, EXTRA)
        totals[...] = block
        gain_rows = jnp.zeros((EXTRA, LANES), jnp.float32)
    else:
        block = packed[...]
        gain_rows = old_gains[...]
    columns = [
        jnp.broadcast_to(block[:, i : i + 1], (EXTRA, LANES)) for i in range(2 * K // EXTRA)
    ]
    row = lax.broadcasted_iota(jnp.int32, (EXTRA, LANES), 0)
    for u in range(count):
        gain = jnp.zeros((EXTRA, LANES), jnp.float32)
        for i in range(K // EXTRA):
            gl = summed(u * 2 * K + i * EXTRA, EXTRA)
            hl = summed(u * 2 * K + K + i * EXTRA, EXTRA)
            g, h = columns[i], columns[K // EXTRA + i]
            gain += score(gl, hl) + score(g - gl, h - hl) - score(g, h)
            weights[0, u * K + i * EXTRA : u * K + (i + 1) * EXTRA, :] = -gl / (hl + RIDGE)
        mean = jnp.sum(gain, axis=0, keepdims=True) / K
        gain_rows = jnp.where(row == first_unit + u, mean, gain_rows)
    if last:
        weights[0, count * K : count * K + EXTRA, :] = gain_rows
    else:
        gains[...] = gain_rows


def place_body(plan, first_unit, count, last, first, *refs):
    if not first:
        refs = refs[1:]
    mine, theirs, weights = refs[:3]
    if last:
        gains, held, lines, sems, held_sems = refs[3:]
    else:
        (sems,) = refs[3:]
    me = lax.axis_index("dp")
    copies = []
    fetched = []
    for side, source in enumerate((mine, theirs)):
        who = me ^ side
        core = who & 1
        if last:
            fetch = pltpu.make_async_copy(
                source.at[:, pl.ds(count * K, EXTRA), :], held.at[side], held_sems.at[side]
            )
            fetch.start()
            fetched.append(fetch)
        for item in range(plan.items):
            owner = (who ^ plan.mask(item, core)) >> 1
            low_bin = owner & (plan.unit - 1)
            half = owner >> plan.bin_bits
            at = pl.multiple_of(half * LANES, LANES)
            for u in range(count):
                copy = pltpu.make_async_copy(
                    source.at[item, pl.ds(u * K, K), :],
                    weights.at[core, (first_unit + u) * plan.unit + low_bin, :, pl.ds(at, LANES)],
                    sems.at[(side * plan.items + item) * count + u],
                )
                copy.start()
                copies.append(copy)
    if last:
        for side in range(2):
            fetched[side].wait()
        for side in range(2):
            who = me ^ side
            core = who & 1
            for item in range(plan.items):
                owner = (who ^ plan.mask(item, core)) >> 1
                low_bin = owner & (plan.unit - 1)
                half = owner >> plan.bin_bits
                for u in range(plan.units):
                    value = held[side, item, u : u + 1, :]
                    lines[core, half, pl.ds(u * plan.unit + low_bin, 1), :] = value
        for h in range(2):
            gains[:, :, h * LANES : (h + 1) * LANES] = lines[:, h]
    for copy in copies:
        copy.wait()


def place(plan, first_unit, count, last, buffer, mine, theirs, features):
    first = buffer is None
    out_shape = [f32(NODES, B, K, features)]
    out_specs = [pl.BlockSpec(memory_space=pl.ANY)]
    scratch = [pltpu.SemaphoreType.DMA((2 * plan.items * count,))]
    if last:
        out_shape.append(f32(NODES, B, features))
        out_specs.append(pl.BlockSpec(memory_space=pltpu.VMEM))
        scratch = [
            pltpu.VMEM((2, plan.items, EXTRA, LANES), jnp.float32),
            pltpu.VMEM((NODES, 2, B, LANES), jnp.float32),
            *scratch,
            pltpu.SemaphoreType.DMA((2,)),
        ]
    operands = [mine, theirs] if first else [buffer, mine, theirs]
    return pl.pallas_call(
        functools.partial(place_body, plan, first_unit, count, last, first),
        out_shape=out_shape,
        in_specs=[pl.BlockSpec(memory_space=pl.ANY)] * len(operands),
        out_specs=out_specs,
        scratch_shapes=scratch,
        input_output_aliases={} if first else {0: 0},
        compiler_params=pltpu.CompilerParams(vmem_limit_bytes=VMEM_LIMIT),
        cost_estimate=pl.CostEstimate(flops=0, bytes_accessed=mine.size * 16, transcendentals=0),
    )(*operands)


def on_device(bin_index, node_ids, gradients, hessians):
    devices = lax.axis_size("dp")
    plan = Plan(devices)
    rows, features = bin_index.shape
    assert features == 2 * LANES

    def swap(x, stage, group):
        pairs = [(d, plan.partner(stage, group, d)) for d in range(devices)]
        return lax.ppermute(x, "dp", pairs)

    def swap_cores(x):
        return lax.ppermute(x, "dp", [(d, d ^ 1) for d in range(devices)])

    sizes = plan.sizes()
    starts = [sum(sizes[:i]) for i in range(len(sizes))]
    totals = gains = buffer = gains_out = None
    bins = spread = None
    for number, (first_unit, count) in enumerate(zip(starts, sizes, strict=True)):
        last = number == len(sizes) - 1
        depth = count * 2 * K + (EXTRA if number == 0 else 0)
        halves = [f32(plan.items, depth, LANES)] * 2
        work = 2 * rows * features * 4 * K * plan.items // 2 * count
        if number == 0:
            keep, send, bins, spread = call(
                functools.partial(first_kernel, plan, count),
                [
                    *halves,
                    jax.ShapeDtypeStruct((rows, features), jnp.bfloat16),
                    jax.ShapeDtypeStruct((NODES * 2 * K, rows), jnp.bfloat16),
                ],
                4,
                flops=3 * work,
            )(bin_index, node_ids.reshape(1, rows), gradients.T, hessians.T)
        else:
            keep, send = call(
                functools.partial(next_kernel, plan, first_unit, count), halves, 2, flops=3 * work
            )(bins, spread)
        held = add_split(keep, swap_cores(send), plan.groups(0))
        for stage in range(len(plan.stages)):
            got = [swap(held[g], stage, g) for g in range(1, plan.groups(stage))]
            if stage == len(plan.stages) - 1:
                break
            mine = held[0]
            for extra in got[:-1]:
                mine = mine + extra
            held = add_split(mine, got[-1], plan.groups(stage + 1))
        parts = [held[0], *got]
        body = functools.partial(
            curves_body, count, first_unit, number == 0, last and number > 0, len(parts)
        )
        tile = f32(EXTRA, LANES)
        if number == 0:
            weights, totals, gains = call(body, [f32(1, count * K, LANES), tile, tile], len(parts))(
                *parts
            )
            if last:
                weights = jnp.concatenate([weights, gains[None]], axis=1)
        elif last:
            (weights,) = call(body, [f32(1, count * K + EXTRA, LANES)], len(parts) + 2)(
                *parts, totals, gains
            )
        else:
            weights, gains = call(body, [f32(1, count * K, LANES), tile], len(parts) + 2)(
                *parts, totals, gains
            )
        for stage in reversed(range(len(plan.stages))):
            weights = jnp.concatenate(
                [weights, *(swap(weights, stage, g) for g in range(1, plan.groups(stage)))], axis=0
            )
        placed = place(
            plan, first_unit, count, last, buffer, weights, swap_cores(weights), features
        )
        buffer = placed[0]
        if last:
            gains_out = placed[1]
    return gains_out.transpose(2, 0, 1), buffer.transpose(3, 0, 1, 2)


def solution(mesh):
    return jax.shard_map(
        on_device,
        mesh=mesh,
        in_specs=(P("dp", None), P("dp"), P("dp", None), P("dp", None)),
        out_specs=(P(), P()),
        check_vma=False,
    )
```

time: 402 us -> 133 us (0.33)
  waiting for transfers between devices: 228 us -> 43.6 us
  matrix products: 68.9 us -> 0 us
  starting transfers between devices: 0.08 us -> 60.3 us
  local copies, waits for them, and re-layouts: 49.9 us -> 4.36 us
  other arithmetic: 39.9 us -> 0.05 us
  Pallas kernels: 0 us -> 23.4 us
  between operations: 14.1 us -> 1.1 us
    reduce_scatter x1 -> x0, waiting for transfers between devices: 152 us -> none  [on_device(): lax.psum_scatter(lax.fori_loop(0, rows_here // row_step, add_block, empty...]
    all_gather x1 -> x0, waiting for transfers between devices: 76.2 us -> none  [on_device(): whole = lax.all_gather(owned, 'dp', axis=0, tiled=True)]
    dot_general x8 -> x0, matrix products: 68.9 us -> none  [add_block(): lax.dot_general(onehot, block_spread, (((0,), (0,)), ((), ())), preferred...]
    ppermute x0 -> x48, starting transfers between devices: none -> 60.3 us  [the longest x40 58.2 us: swap(): return lax.ppermute(x, 'dp', pairs)]
    ppermute x0 -> x48, waiting for transfers between devices: none -> 43.6 us  [the longest x40 43.6 us: swap(): return lax.ppermute(x, 'dp', pairs)]
    pallas_call x0 -> x24, Pallas kernels: none -> 23.4 us  [the longest x3 11.2 us: on_device(): call(functools.partial(next_kernel, plan, first_unit, count), halves, 2,...]
    eq x8 -> x0, other arithmetic: 22.7 us -> none  [add_block(): block_bins[:, :, None] == levels[None, None, :]]
    transpose x1 -> x0, local copies, waits for them, and re-layouts: 13.6 us -> none  [arrange(): return jnp.transpose(hist.reshape(-1, B, NODES, 2 * K), (0, 2, 1, 3))]
  transfers between devices with their start and end apart: 2 -> 48, of which waited for: 2 -> 14; matrix products, arithmetic and copies ran while one was open for 0% -> 0% of each run, Pallas kernels for 0% -> 13%
where the time goes in v1:
time: 133 us
  starting transfers between devices  60.3 us (45%)
  waiting for transfers between devices  43.6 us (33%)
  Pallas kernels  23.4 us (18%)
  local copies, waits for them, and re-layouts  4.36 us (3%)
    ppermute x40, starting transfers between devices, swap(): return lax.ppermute(x, 'dp', pairs)  58.2 us
    ppermute x40, waiting for transfers between devices, swap(): return lax.ppermute(x, 'dp', pairs)  43.6 us
    pallas_call x3, Pallas kernels, on_device(): call(functools.partial(next_kernel, plan, first_unit, count), halves, 2,...  11.2 us
    pallas_call x4, Pallas kernels, place(): pl.pallas_call(functools.partial(place_body, plan, first_unit, count, las...  6.77 us
    unnamed x24, local copies, waits for them, and re-layouts  4.21 us
    pallas_call x1, Pallas kernels, on_device(): call(functools.partial(first_kernel, plan, count), [*halves, jax.ShapeDty...  4.2 us
  transfers between devices with their start and end apart: 48, of which 14 were waited for; matrix products, arithmetic and copies ran while one was open for 0% of the time, Pallas kernels for 13%

profile of v1, /device:TPU:0, one launch (start us, length us, event | category | flops | bytes accessed | tf_op | source)
XLA Modules:
  0.0 132.8 jit_solution(13367376863656065739)
XLA Ops:
  0.6 1.6 %copy-done = s32[2048,256]{1,0:T(8,128)S(1)} copy-done((s32[2048,256]{1,0:T(8,128)S(1)}, s32[2048,256]{1,0:T(8,128)}, u32[]{:S(2)}) %copy-start) | copy-done | bytes 2097176
  2.2 0.9 copy-done.1
  3.1 0.9 copy-done.2
  4.0 0.7 copy-done.3
  4.7 4.2 %shard_map.59 = (f32[16,136,128]{2,1,0:T(8,128)S(1)}, f32[16,136,128]{2,1,0:T(8,128)S(1)}, bf16[2048,256]{1,0:T(8,128)(2,1)S(1)}, bf16[128,2048]{1,0:T(8,128)(2,1)S(1)}) custom-call(s32[2048,256]{1,0:T(8,128)S(1)} %copy-done, s32[1,2048]{1,0:T(1,128)S(1)} %bitcast.7, bf16[32,2048]{1,0:T(8,128)(2,1)S(1)} %bitcast.5, bf16[32,2048]{1,0:T(8,128)(2,1)S(1)} %bitcast.6), custom_call_target="tpu_custom_call" | custom-call | flops 6442450944 | tf_op jit(solution)/shard_map/pallas_call | solution.py:309
  8.9 0.5 collective-permute-start
  9.5 3.8 %shard_map.65 = (f32[16,128,128]{2,1,0:T(8,128)S(1)}, f32[16,128,128]{2,1,0:T(8,128)S(1)}) custom-call(bf16[2048,256]{1,0:T(8,128)(2,1)S(1)} %get-tuple-element.64.bins, bf16[128,2048]{1,0:T(8,128)(2,1)S(1)} %get-tuple-element.65.spread), custom_call_target="tpu_custom_call" | custom-call | flops 6442450944 | tf_op jit(solution)/shard_map/pallas_call | solution.py:320
  13.3 3.7 %shard_map.71 = (f32[16,128,128]{2,1,0:T(8,128)S(1)}, f32[16,128,128]{2,1,0:T(8,128)S(1)}) custom-call(bf16[2048,256]{1,0:T(8,128)(2,1)S(1)} %get-tuple-element.64.bins, bf16[128,2048]{1,0:T(8,128)(2,1)S(1)} %get-tuple-element.65.spread), custom_call_target="tpu_custom_call" | custom-call | flops 6442450944 | tf_op jit(solution)/shard_map/pallas_call | solution.py:320
  17.0 0.5 collective-permute-start.24
  17.6 3.7 %shard_map.77 = (f32[16,128,128]{2,1,0:T(8,128)S(1)}, f32[16,128,128]{2,1,0:T(8,128)S(1)}) custom-call(bf16[2048,256]{1,0:T(8,128)(2,1)S(1)} %get-tuple-element.64.bins, bf16[128,2048]{1,0:T(8,128)(2,1)S(1)} %get-tuple-element.65.spread), custom_call_target="tpu_custom_call" | custom-call | flops 6442450944 | tf_op jit(solution)/shard_map/pallas_call | solution.py:320
  21.3 0.1 collective-permute-start.36
  21.5 0.1 shard_map.60
  21.6 2.9 %collective-permute-start.1 = (f32[8,136,128]{2,1,0:T(8,128)S(1)}, f32[8,136,128]{2,1,0:T(8,128)S(1)}, u32[]{:S(2)}, u32[]{:S(2)}) collective-permute-start(f32[8,136,128]{2,1,0:T(8,128)S(1)} %get-tuple-element.56), channel_id=1, source_target_pairs={{0,2},{1,5},{2,0},{3,7},{4,6},{5,1},{6,4},{7,3},{8,10},{9,13},{10,... | collective-permute-start | bytes 1671176 | tf_op jit(solution)/shard_map/ppermute | solution.py:294
  24.6 0.1 shard_map.66
  24.8 0.1 shard_map.72
  24.9 2.1 %collective-permute-start.25 = (f32[8,128,128]{2,1,0:T(8,128)S(1)}, f32[8,128,128]{2,1,0:T(8,128)S(1)}, u32[]{:S(2)}, u32[]{:S(2)}) collective-permute-start(f32[8,128,128]{2,1,0:T(8,128)S(1)} %get-tuple-element.82), channel_id=1, source_target_pairs={{0,2},{1,5},{2,0},{3,7},{4,6},{5,1},{6,4},{7,3},{8,10},{9,13},{10,... | collective-permute-start | bytes 1572872 | tf_op jit(solution)/shard_map/ppermute | solution.py:294
  26.9 0.1 shard_map.78
  27.2 4.9 %collective-permute-done.1.theirs = f32[8,136,128]{2,1,0:T(8,128)S(1)} collective-permute-done((f32[8,136,128]{2,1,0:T(8,128)S(1)}, f32[8,136,128]{2,1,0:T(8,128)S(1)}, u32[]{:S(2)}, u32[]{:S(2)}) %collective-permute-start.1) | collective-permute-done | bytes 557088 | tf_op jit(solution)/shard_map/ppermute | solution.py:294
  32.1 2.2 %collective-permute-start.2 = (f32[4,136,128]{2,1,0:T(8,128)S(1)}, f32[4,136,128]{2,1,0:T(8,128)S(1)}, u32[]{:S(2)}, u32[]{:S(2)}) collective-permute-start(f32[4,136,128]{2,1,0:T(8,128)S(1)} %get-tuple-element.58), channel_id=1, source_target_pairs={{0,4},{1,3},{2,6},{3,1},{4,0},{5,7},{6,2},{7,5},{8,12},{9,11},{10,... | collective-permute-start | bytes 835592 | tf_op jit(solution)/shard_map/ppermute | solution.py:294
  34.3 6.4 %collective-permute-done.13.theirs = f32[8,128,128]{2,1,0:T(8,128)S(1)} collective-permute-done((f32[8,128,128]{2,1,0:T(8,128)S(1)}, f32[8,128,128]{2,1,0:T(8,128)S(1)}, u32[]{:S(2)}, u32[]{:S(2)}) %collective-permute-start.13) | collective-permute-done | bytes 524320 | tf_op jit(solution)/shard_map/ppermute | solution.py:294
  40.7 2.3 %collective-permute-start.14 = (f32[4,128,128]{2,1,0:T(8,128)S(1)}, f32[4,128,128]{2,1,0:T(8,128)S(1)}, u32[]{:S(2)}, u32[]{:S(2)}) collective-permute-start(f32[4,128,128]{2,1,0:T(8,128)S(1)} %get-tuple-element.71), channel_id=1, source_target_pairs={{0,4},{1,3},{2,6},{3,1},{4,0},{5,7},{6,2},{7,5},{8,12},{9,11},{10,... | collective-permute-start | bytes 786440 | tf_op jit(solution)/shard_map/ppermute | solution.py:294
  43.0 6.1 %collective-permute-done.25.theirs = f32[8,128,128]{2,1,0:T(8,128)S(1)} collective-permute-done((f32[8,128,128]{2,1,0:T(8,128)S(1)}, f32[8,128,128]{2,1,0:T(8,128)S(1)}, u32[]{:S(2)}, u32[]{:S(2)}) %collective-permute-start.25) | collective-permute-done | bytes 524320 | tf_op jit(solution)/shard_map/ppermute | solution.py:294
  49.1 2.2 %collective-permute-start.26 = (f32[4,128,128]{2,1,0:T(8,128)S(1)}, f32[4,128,128]{2,1,0:T(8,128)S(1)}, u32[]{:S(2)}, u32[]{:S(2)}) collective-permute-start(f32[4,128,128]{2,1,0:T(8,128)S(1)} %get-tuple-element.84), channel_id=1, source_target_pairs={{0,4},{1,3},{2,6},{3,1},{4,0},{5,7},{6,2},{7,5},{8,12},{9,11},{10,... | collective-permute-start | bytes 786440 | tf_op jit(solution)/shard_map/ppermute | solution.py:294
  51.3 6.2 %collective-permute-done.37.theirs = f32[8,128,128]{2,1,0:T(8,128)S(1)} collective-permute-done((f32[8,128,128]{2,1,0:T(8,128)S(1)}, f32[8,128,128]{2,1,0:T(8,128)S(1)}, u32[]{:S(2)}, u32[]{:S(2)}) %collective-permute-start.37) | collective-permute-done | bytes 524320 | tf_op jit(solution)/shard_map/ppermute | solution.py:294
  57.6 2.2 %collective-permute-start.38 = (f32[4,128,128]{2,1,0:T(8,128)S(1)}, f32[4,128,128]{2,1,0:T(8,128)S(1)}, u32[]{:S(2)}, u32[]{:S(2)}) collective-permute-start(f32[4,128,128]{2,1,0:T(8,128)S(1)} %get-tuple-element.96), channel_id=1, source_target_pairs={{0,4},{1,3},{2,6},{3,1},{4,0},{5,7},{6,2},{7,5},{8,12},{9,11},{10,... | collective-permute-start | bytes 786440 | tf_op jit(solution)/shard_map/ppermute | solution.py:294
  59.8 1.7 %collective-permute-start.3 = (f32[1,136,128]{2,1,0:T(8,128)S(1)}, f32[1,136,128]{2,1,0:T(8,128)S(1)}, u32[]{:S(2)}, u32[]{:S(2)}) collective-permute-start(f32[1,136,128]{2,1,0:T(8,128)S(1)} %get-tuple-element.60), channel_id=1, source_target_pairs={{0,8},{1,9},{2,10},{3,11},{4,12},{5,13},{6,14},{7,15},{8,0},{9,1},... | collective-permute-start | bytes 208904 | tf_op jit(solution)/shard_map/ppermute | solution.py:294
  61.5 2.5 %collective-permute-start.4 = (f32[1,136,128]{2,1,0:T(8,128)S(1)}, f32[1,136,128]{2,1,0:T(8,128)S(1)}, u32[]{:S(2)}, u32[]{:S(2)}) collective-permute-start(f32[1,136,128]{2,1,0:T(8,128)S(1)} %get-tuple-element.61), channel_id=1, source_target_pairs={{0,16},{1,17},{2,18},{3,19},{4,20},{5,21},{6,22},{7,23},{8,24},{9,... | collective-permute-start | bytes 208904 | tf_op jit(solution)/shard_map/ppermute | solution.py:294
  64.0 0.3 collective-permute-start.5
  64.3 0.8 collective-permute-start.15
  65.1 3.4 %collective-permute-start.16 = (f32[1,128,128]{2,1,0:T(8,128)S(1)}, f32[1,128,128]{2,1,0:T(8,128)S(1)}, u32[]{:S(2)}, u32[]{:S(2)}) collective-permute-start(f32[1,128,128]{2,1,0:T(8,128)S(1)} %get-tuple-element.74), channel_id=1, source_target_pairs={{0,16},{1,17},{2,18},{3,19},{4,20},{5,21},{6,22},{7,23},{8,24},{9,... | collective-permute-start | bytes 196616 | tf_op jit(solution)/shard_map/ppermute | solution.py:294
  68.5 0.7 collective-permute-start.17
  69.3 0.5 collective-permute-done.4.refs_2_
  69.7 1.2 collective-permute-done.5.refs_3_
  70.9 5.2 %collective-permute-start.28 = (f32[1,128,128]{2,1,0:T(8,128)S(1)}, f32[1,128,128]{2,1,0:T(8,128)S(1)}, u32[]{:S(2)}, u32[]{:S(2)}) collective-permute-start(f32[1,128,128]{2,1,0:T(8,128)S(1)} %get-tuple-element.87), channel_id=1, source_target_pairs={{0,16},{1,17},{2,18},{3,19},{4,20},{5,21},{6,22},{7,23},{8,24},{9,... | collective-permute-start | bytes 196616 | tf_op jit(solution)/shard_map/ppermute | solution.py:294
  76.1 0.1 shard_map.63
  76.2 0.8 collective-permute-start.29
  77.0 3.7 %collective-permute-start.40 = (f32[1,128,128]{2,1,0:T(8,128)S(1)}, f32[1,128,128]{2,1,0:T(8,128)S(1)}, u32[]{:S(2)}, u32[]{:S(2)}) collective-permute-start(f32[1,128,128]{2,1,0:T(8,128)S(1)} %get-tuple-element.99), channel_id=1, source_target_pairs={{0,16},{1,17},{2,18},{3,19},{4,20},{5,21},{6,22},{7,23},{8,24},{9,... | collective-permute-start | bytes 196616 | tf_op jit(solution)/shard_map/ppermute | solution.py:294
  80.8 1.8 %collective-permute-start.41 = (f32[1,128,128]{2,1,0:T(8,128)S(1)}, f32[1,128,128]{2,1,0:T(8,128)S(1)}, u32[]{:S(2)}, u32[]{:S(2)}) collective-permute-start(f32[1,128,128]{2,1,0:T(8,128)S(1)} %get-tuple-element.100), channel_id=1, source_target_pairs={{0,24},{1,25},{2,26},{3,27},{4,28},{5,29},{6,30},{7,31},{8,16},{9,... | collective-permute-start | bytes 196616 | tf_op jit(solution)/shard_map/ppermute | solution.py:294
  82.6 0.2 collective-permute-done.29.refs_3_
  82.8 3.0 %collective-permute-start.7 = (f32[1,64,128]{2,1,0:T(8,128)S(1)}, f32[1,64,128]{2,1,0:T(8,128)S(1)}, u32[]{:S(2)}, u32[]{:S(2)}) collective-permute-start(f32[1,64,128]{2,1,0:T(8,128)S(1)} %get-tuple-element.63), channel_id=1, source_target_pairs={{0,16},{1,17},{2,18},{3,19},{4,20},{5,21},{6,22},{7,23},{8,24},{9,... | collective-permute-start | bytes 98312 | tf_op jit(solution)/shard_map/ppermute | solution.py:294
  85.9 1.3 collective-permute-start.8
  87.2 3.1 %collective-permute-start.19 = (f32[1,64,128]{2,1,0:T(8,128)S(1)}, f32[1,64,128]{2,1,0:T(8,128)S(1)}, u32[]{:S(2)}, u32[]{:S(2)}) collective-permute-start(f32[1,64,128]{2,1,0:T(8,128)S(1)} %get-tuple-element.78), channel_id=1, source_target_pairs={{0,16},{1,17},{2,18},{3,19},{4,20},{5,21},{6,22},{7,23},{8,24},{9,... | collective-permute-start | bytes 98312 | tf_op jit(solution)/shard_map/ppermute | solution.py:294
  90.5 1.3 collective-permute-start.20
  91.9 3.1 %collective-permute-start.31 = (f32[1,64,128]{2,1,0:T(8,128)S(1)}, f32[1,64,128]{2,1,0:T(8,128)S(1)}, u32[]{:S(2)}, u32[]{:S(2)}) collective-permute-start(f32[1,64,128]{2,1,0:T(8,128)S(1)} %get-tuple-element.90), channel_id=1, source_target_pairs={{0,16},{1,17},{2,18},{3,19},{4,20},{5,21},{6,22},{7,23},{8,24},{9,... | collective-permute-start | bytes 98312 | tf_op jit(solution)/shard_map/ppermute | solution.py:294
  95.1 1.3 collective-permute-start.32
  96.5 3.1 %collective-permute-start.43 = (f32[1,72,128]{2,1,0:T(8,128)S(1)}, f32[1,72,128]{2,1,0:T(8,128)S(1)}, u32[]{:S(2)}, u32[]{:S(2)}) collective-permute-start(f32[1,72,128]{2,1,0:T(8,128)S(1)} %shard_map.81), channel_id=1, source_target_pairs={{0,16},{1,17},{2,18},{3,19},{4,20},{5,21},{6,22},{7,23},{8,24},{9,... | collective-permute-start | bytes 110600 | tf_op jit(solution)/shard_map/ppermute | solution.py:294
  99.7 1.3 collective-permute-start.44
  101.0 1.2 collective-permute-start.9
  102.2 0.9 collective-permute-start.21
  103.2 1.2 collective-permute-start.33
  104.4 1.1 collective-permute-done.44
  105.6 1.9 %collective-permute-done.9 = f32[4,64,128]{2,1,0:T(8,128)S(1)} collective-permute-done((f32[4,64,128]{2,1,0:T(8,128)S(1)}, f32[4,64,128]{2,1,0:T(8,128)S(1)}, u32[]{:S(2)}, u32[]{:S(2)}) %collective-permute-start.9) | collective-permute-done | bytes 131104 | tf_op jit(solution)/shard_map/ppermute | solution.py:294
  107.5 0.1 collective-permute-start.10
  107.6 2.7 %collective-permute-done.21 = f32[4,64,128]{2,1,0:T(8,128)S(1)} collective-permute-done((f32[4,64,128]{2,1,0:T(8,128)S(1)}, f32[4,64,128]{2,1,0:T(8,128)S(1)}, u32[]{:S(2)}, u32[]{:S(2)}) %collective-permute-start.21) | collective-permute-done | bytes 131104 | tf_op jit(solution)/shard_map/ppermute | solution.py:294
  110.3 0.1 collective-permute-start.22
  110.4 5.8 %collective-permute-done.45 = f32[4,72,128]{2,1,0:T(8,128)S(1)} collective-permute-done((f32[4,72,128]{2,1,0:T(8,128)S(1)}, f32[4,72,128]{2,1,0:T(8,128)S(1)}, u32[]{:S(2)}, u32[]{:S(2)}) %collective-permute-start.45) | collective-permute-done | bytes 147488 | tf_op jit(solution)/shard_map/ppermute | solution.py:294
  116.4 2.1 %collective-permute-start.34 = (f32[8,64,128]{2,1,0:T(8,128)S(1)}, f32[8,64,128]{2,1,0:T(8,128)S(1)}, u32[]{:S(2)}, u32[]{:S(2)}) collective-permute-start(f32[8,64,128]{2,1,0:T(8,128)S(1)} %get-tuple-element.106), channel_id=1, source_target_pairs={{0,2},{1,5},{2,0},{3,7},{4,6},{5,1},{6,4},{7,3},{8,10},{9,13},{10,... | collective-permute-start | bytes 786440 | tf_op jit(solution)/shard_map/ppermute | solution.py:294
  118.6 0.5 collective-permute-start.23
  119.2 3.9 %collective-permute-done.46 = f32[8,72,128]{2,1,0:T(8,128)S(1)} collective-permute-done((f32[8,72,128]{2,1,0:T(8,128)S(1)}, f32[8,72,128]{2,1,0:T(8,128)S(1)}, u32[]{:S(2)}, u32[]{:S(2)}) %collective-permute-start.46) | collective-permute-done | bytes 294944 | tf_op jit(solution)/shard_map/ppermute | solution.py:294
  123.2 2.7 %collective-permute-done.34 = f32[8,64,128]{2,1,0:T(8,128)S(1)} collective-permute-done((f32[8,64,128]{2,1,0:T(8,128)S(1)}, f32[8,64,128]{2,1,0:T(8,128)S(1)}, u32[]{:S(2)}, u32[]{:S(2)}) %collective-permute-start.34) | collective-permute-done | bytes 262176 | tf_op jit(solution)/shard_map/ppermute | solution.py:294
  126.0 1.5 %shard_map.64.refs_0_ = f32[2,64,32,256]{3,2,1,0:T(8,128)} custom-call(f32[16,64,128]{2,1,0:T(8,128)S(1)} %constant_dynamic-update-slice_fusion.5.refs_0_, f32[16,64,128]{2,1,0:T(8,128)S(1)} %collective-permute-done.11.refs_1_), custom_call_target="tpu_custom_call" | custom-call | bytes 2097152 | tf_op jit(solution)/shard_map/pallas_call | solution.py:274
  127.6 1.5 %shard_map.70.refs_0_ = f32[2,64,32,256]{3,2,1,0:T(8,128)} custom-call(f32[2,64,32,256]{3,2,1,0:T(8,128)} %shard_map.64.refs_0_, f32[16,64,128]{2,1,0:T(8,128)S(1)} %constant_dynamic-update-slice_fusion.16.refs_1_, f32[16,64,128]{2,1,0:T(8,128)S(1)} %collective-permute-done.23.refs_2_), custom_call_target="tpu_custom_call", output_to_operand_aliasing={{}: (0, {})} | custom-call | bytes 2097152 | tf_op jit(solution)/shard_map/pallas_call | solution.py:274
  129.1 1.5 %shard_map.76.refs_0_ = f32[2,64,32,256]{3,2,1,0:T(8,128)} custom-call(f32[2,64,32,256]{3,2,1,0:T(8,128)} %shard_map.70.refs_0_, f32[16,64,128]{2,1,0:T(8,128)S(1)} %constant_dynamic-update-slice_fusion.27.refs_1_, f32[16,64,128]{2,1,0:T(8,128)S(1)} %collective-permute-done.35.refs_2_), custom_call_target="tpu_custom_call", output_to_operand_aliasing={{}: (0, {})} | custom-call | bytes 2097152 | tf_op jit(solution)/shard_map/pallas_call | solution.py:274
  130.6 2.2 %shard_map.82 = (f32[2,64,32,256]{3,2,1,0:T(8,128)}, f32[2,64,256]{2,1,0:T(8,128)}) custom-call(f32[2,64,32,256]{3,2,1,0:T(8,128)} %shard_map.76.refs_0_, f32[16,72,128]{2,1,0:T(8,128)S(1)} %constant_dynamic-update-slice_fusion.38.refs_1_, f32[16,72,128]{2,1,0:T(8,128)S(1)} %collective-permute-done.47.refs_2_), custom_call_target="tpu_custom_call", output_to_operand_aliasing={{0}: (0, {})} | custom-call | bytes 2359296 | tf_op jit(solution)/shard_map/pallas_call | solution.py:274
  (92 shorter events, 1.9 us)
Async XLA Ops:
  0.6 1.6 %copy-start = (s32[2048,256]{1,0:T(8,128)S(1)}, s32[2048,256]{1,0:T(8,128)}, u32[]{:S(2)}) copy-start(s32[2048,256]{1,0:T(8,128)} %bins_ref.1) | copy-start | bytes 6291460
  2.2 0.9 copy-start.1
  3.1 0.9 copy-start.2
  4.0 0.7 copy-start.3
  8.9 12.5 %collective-permute-start = (f32[16,136,128]{2,1,0:T(8,128)S(1)}, f32[16,136,128]{2,1,0:T(8,128)S(1)}, u32[]{:S(2)}, u32[]{:S(2)}) collective-permute-start(f32[16,136,128]{2,1,0:T(8,128)S(1)} %get-tuple-element.54), channel_id=1, source_target_pairs={{0,1},{1,0},{2,3},{3,2},{4,5},{5,4},{6,7},{7,6},{8,9},{9,8},{10,11... | collective-permute-start | bytes 3342344 | tf_op jit(solution)/shard_map/ppermute | solution.py:297
  13.2 11.3 %collective-permute-start.12 = (f32[16,128,128]{2,1,0:T(8,128)S(1)}, f32[16,128,128]{2,1,0:T(8,128)S(1)}, u32[]{:S(2)}, u32[]{:S(2)}) collective-permute-start(f32[16,128,128]{2,1,0:T(8,128)S(1)} %get-tuple-element.67), channel_id=1, source_target_pairs={{0,1},{1,0},{2,3},{3,2},{4,5},{5,4},{6,7},{7,6},{8,9},{9,8},{10,11... | collective-permute-start | bytes 3145736 | tf_op jit(solution)/shard_map/ppermute | solution.py:297
  17.0 7.7 %collective-permute-start.24 = (f32[16,128,128]{2,1,0:T(8,128)S(1)}, f32[16,128,128]{2,1,0:T(8,128)S(1)}, u32[]{:S(2)}, u32[]{:S(2)}) collective-permute-start(f32[16,128,128]{2,1,0:T(8,128)S(1)} %get-tuple-element.80), channel_id=1, source_target_pairs={{0,1},{1,0},{2,3},{3,2},{4,5},{5,4},{6,7},{7,6},{8,9},{9,8},{10,11... | collective-permute-start | bytes 3145736 | tf_op jit(solution)/shard_map/ppermute | solution.py:297
  21.3 5.6 %collective-permute-start.36 = (f32[16,128,128]{2,1,0:T(8,128)S(1)}, f32[16,128,128]{2,1,0:T(8,128)S(1)}, u32[]{:S(2)}, u32[]{:S(2)}) collective-permute-start(f32[16,128,128]{2,1,0:T(8,128)S(1)} %get-tuple-element.92), channel_id=1, source_target_pairs={{0,1},{1,0},{2,3},{3,2},{4,5},{5,4},{6,7},{7,6},{8,9},{9,8},{10,11... | collective-permute-start | bytes 3145736 | tf_op jit(solution)/shard_map/ppermute | solution.py:297
  21.6 10.4 %collective-permute-start.1 = (f32[8,136,128]{2,1,0:T(8,128)S(1)}, f32[8,136,128]{2,1,0:T(8,128)S(1)}, u32[]{:S(2)}, u32[]{:S(2)}) collective-permute-start(f32[8,136,128]{2,1,0:T(8,128)S(1)} %get-tuple-element.56), channel_id=1, source_target_pairs={{0,2},{1,5},{2,0},{3,7},{4,6},{5,1},{6,4},{7,3},{8,10},{9,13},{10,... | collective-permute-start | bytes 1671176 | tf_op jit(solution)/shard_map/ppermute | solution.py:294
  24.7 16.0 %collective-permute-start.13 = (f32[8,128,128]{2,1,0:T(8,128)S(1)}, f32[8,128,128]{2,1,0:T(8,128)S(1)}, u32[]{:S(2)}, u32[]{:S(2)}) collective-permute-start(f32[8,128,128]{2,1,0:T(8,128)S(1)} %get-tuple-element.69), channel_id=1, source_target_pairs={{0,2},{1,5},{2,0},{3,7},{4,6},{5,1},{6,4},{7,3},{8,10},{9,13},{10,... | collective-permute-start | bytes 1572872 | tf_op jit(solution)/shard_map/ppermute | solution.py:294
  24.9 24.2 %collective-permute-start.25 = (f32[8,128,128]{2,1,0:T(8,128)S(1)}, f32[8,128,128]{2,1,0:T(8,128)S(1)}, u32[]{:S(2)}, u32[]{:S(2)}) collective-permute-start(f32[8,128,128]{2,1,0:T(8,128)S(1)} %get-tuple-element.82), channel_id=1, source_target_pairs={{0,2},{1,5},{2,0},{3,7},{4,6},{5,1},{6,4},{7,3},{8,10},{9,13},{10,... | collective-permute-start | bytes 1572872 | tf_op jit(solution)/shard_map/ppermute | solution.py:294
  27.1 30.4 %collective-permute-start.37 = (f32[8,128,128]{2,1,0:T(8,128)S(1)}, f32[8,128,128]{2,1,0:T(8,128)S(1)}, u32[]{:S(2)}, u32[]{:S(2)}) collective-permute-start(f32[8,128,128]{2,1,0:T(8,128)S(1)} %get-tuple-element.94), channel_id=1, source_target_pairs={{0,2},{1,5},{2,0},{3,7},{4,6},{5,1},{6,4},{7,3},{8,10},{9,13},{10,... | collective-permute-start | bytes 1572872 | tf_op jit(solution)/shard_map/ppermute | solution.py:294
  32.1 27.6 %collective-permute-start.2 = (f32[4,136,128]{2,1,0:T(8,128)S(1)}, f32[4,136,128]{2,1,0:T(8,128)S(1)}, u32[]{:S(2)}, u32[]{:S(2)}) collective-permute-start(f32[4,136,128]{2,1,0:T(8,128)S(1)} %get-tuple-element.58), channel_id=1, source_target_pairs={{0,4},{1,3},{2,6},{3,1},{4,0},{5,7},{6,2},{7,5},{8,12},{9,11},{10,... | collective-permute-start | bytes 835592 | tf_op jit(solution)/shard_map/ppermute | solution.py:294
  40.7 23.2 %collective-permute-start.14 = (f32[4,128,128]{2,1,0:T(8,128)S(1)}, f32[4,128,128]{2,1,0:T(8,128)S(1)}, u32[]{:S(2)}, u32[]{:S(2)}) collective-permute-start(f32[4,128,128]{2,1,0:T(8,128)S(1)} %get-tuple-element.71), channel_id=1, source_target_pairs={{0,4},{1,3},{2,6},{3,1},{4,0},{5,7},{6,2},{7,5},{8,12},{9,11},{10,... | collective-permute-start | bytes 786440 | tf_op jit(solution)/shard_map/ppermute | solution.py:294
  49.1 15.1 %collective-permute-start.26 = (f32[4,128,128]{2,1,0:T(8,128)S(1)}, f32[4,128,128]{2,1,0:T(8,128)S(1)}, u32[]{:S(2)}, u32[]{:S(2)}) collective-permute-start(f32[4,128,128]{2,1,0:T(8,128)S(1)} %get-tuple-element.84), channel_id=1, source_target_pairs={{0,4},{1,3},{2,6},{3,1},{4,0},{5,7},{6,2},{7,5},{8,12},{9,11},{10,... | collective-permute-start | bytes 786440 | tf_op jit(solution)/shard_map/ppermute | solution.py:294
  57.6 7.5 %collective-permute-start.38 = (f32[4,128,128]{2,1,0:T(8,128)S(1)}, f32[4,128,128]{2,1,0:T(8,128)S(1)}, u32[]{:S(2)}, u32[]{:S(2)}) collective-permute-start(f32[4,128,128]{2,1,0:T(8,128)S(1)} %get-tuple-element.96), channel_id=1, source_target_pairs={{0,4},{1,3},{2,6},{3,1},{4,0},{5,7},{6,2},{7,5},{8,12},{9,11},{10,... | collective-permute-start | bytes 786440 | tf_op jit(solution)/shard_map/ppermute | solution.py:294
  59.8 8.7 %collective-permute-start.3 = (f32[1,136,128]{2,1,0:T(8,128)S(1)}, f32[1,136,128]{2,1,0:T(8,128)S(1)}, u32[]{:S(2)}, u32[]{:S(2)}) collective-permute-start(f32[1,136,128]{2,1,0:T(8,128)S(1)} %get-tuple-element.60), channel_id=1, source_target_pairs={{0,8},{1,9},{2,10},{3,11},{4,12},{5,13},{6,14},{7,15},{8,0},{9,1},... | collective-permute-start | bytes 208904 | tf_op jit(solution)/shard_map/ppermute | solution.py:294
  61.5 8.3 %collective-permute-start.4 = (f32[1,136,128]{2,1,0:T(8,128)S(1)}, f32[1,136,128]{2,1,0:T(8,128)S(1)}, u32[]{:S(2)}, u32[]{:S(2)}) collective-permute-start(f32[1,136,128]{2,1,0:T(8,128)S(1)} %get-tuple-element.61), channel_id=1, source_target_pairs={{0,16},{1,17},{2,18},{3,19},{4,20},{5,21},{6,22},{7,23},{8,24},{9,... | collective-permute-start | bytes 208904 | tf_op jit(solution)/shard_map/ppermute | solution.py:294
  64.0 7.0 %collective-permute-start.5 = (f32[1,136,128]{2,1,0:T(8,128)S(1)}, f32[1,136,128]{2,1,0:T(8,128)S(1)}, u32[]{:S(2)}, u32[]{:S(2)}) collective-permute-start(f32[1,136,128]{2,1,0:T(8,128)S(1)} %get-tuple-element.62), channel_id=1, source_target_pairs={{0,24},{1,25},{2,26},{3,27},{4,28},{5,29},{6,30},{7,31},{8,16},{9,... | collective-permute-start | bytes 208904 | tf_op jit(solution)/shard_map/ppermute | solution.py:294
  64.3 12.0 %collective-permute-start.15 = (f32[1,128,128]{2,1,0:T(8,128)S(1)}, f32[1,128,128]{2,1,0:T(8,128)S(1)}, u32[]{:S(2)}, u32[]{:S(2)}) collective-permute-start(f32[1,128,128]{2,1,0:T(8,128)S(1)} %get-tuple-element.73), channel_id=1, source_target_pairs={{0,8},{1,9},{2,10},{3,11},{4,12},{5,13},{6,14},{7,15},{8,0},{9,1},... | collective-permute-start | bytes 196616 | tf_op jit(solution)/shard_map/ppermute | solution.py:294
  65.1 12.0 %collective-permute-start.16 = (f32[1,128,128]{2,1,0:T(8,128)S(1)}, f32[1,128,128]{2,1,0:T(8,128)S(1)}, u32[]{:S(2)}, u32[]{:S(2)}) collective-permute-start(f32[1,128,128]{2,1,0:T(8,128)S(1)} %get-tuple-element.74), channel_id=1, source_target_pairs={{0,16},{1,17},{2,18},{3,19},{4,20},{5,21},{6,22},{7,23},{8,24},{9,... | collective-permute-start | bytes 196616 | tf_op jit(solution)/shard_map/ppermute | solution.py:294
  68.5 8.6 %collective-permute-start.17 = (f32[1,128,128]{2,1,0:T(8,128)S(1)}, f32[1,128,128]{2,1,0:T(8,128)S(1)}, u32[]{:S(2)}, u32[]{:S(2)}) collective-permute-start(f32[1,128,128]{2,1,0:T(8,128)S(1)} %get-tuple-element.75), channel_id=1, source_target_pairs={{0,24},{1,25},{2,26},{3,27},{4,28},{5,29},{6,30},{7,31},{8,16},{9,... | collective-permute-start | bytes 196616 | tf_op jit(solution)/shard_map/ppermute | solution.py:294
  69.7 11.1 %collective-permute-start.27 = (f32[1,128,128]{2,1,0:T(8,128)S(1)}, f32[1,128,128]{2,1,0:T(8,128)S(1)}, u32[]{:S(2)}, u32[]{:S(2)}) collective-permute-start(f32[1,128,128]{2,1,0:T(8,128)S(1)} %get-tuple-element.86), channel_id=1, source_target_pairs={{0,8},{1,9},{2,10},{3,11},{4,12},{5,13},{6,14},{7,15},{8,0},{9,1},... | collective-permute-start | bytes 196616 | tf_op jit(solution)/shard_map/ppermute | solution.py:294
  70.9 11.7 %collective-permute-start.28 = (f32[1,128,128]{2,1,0:T(8,128)S(1)}, f32[1,128,128]{2,1,0:T(8,128)S(1)}, u32[]{:S(2)}, u32[]{:S(2)}) collective-permute-start(f32[1,128,128]{2,1,0:T(8,128)S(1)} %get-tuple-element.87), channel_id=1, source_target_pairs={{0,16},{1,17},{2,18},{3,19},{4,20},{5,21},{6,22},{7,23},{8,24},{9,... | collective-permute-start | bytes 196616 | tf_op jit(solution)/shard_map/ppermute | solution.py:294
  76.2 6.6 %collective-permute-start.29 = (f32[1,128,128]{2,1,0:T(8,128)S(1)}, f32[1,128,128]{2,1,0:T(8,128)S(1)}, u32[]{:S(2)}, u32[]{:S(2)}) collective-permute-start(f32[1,128,128]{2,1,0:T(8,128)S(1)} %get-tuple-element.88), channel_id=1, source_target_pairs={{0,24},{1,25},{2,26},{3,27},{4,28},{5,29},{6,30},{7,31},{8,16},{9,... | collective-permute-start | bytes 196616 | tf_op jit(solution)/shard_map/ppermute | solution.py:294
  77.0 8.9 %collective-permute-start.39 = (f32[1,128,128]{2,1,0:T(8,128)S(1)}, f32[1,128,128]{2,1,0:T(8,128)S(1)}, u32[]{:S(2)}, u32[]{:S(2)}) collective-permute-start(f32[1,128,128]{2,1,0:T(8,128)S(1)} %get-tuple-element.98), channel_id=1, source_target_pairs={{0,8},{1,9},{2,10},{3,11},{4,12},{5,13},{6,14},{7,15},{8,0},{9,1},... | collective-permute-start | bytes 196616 | tf_op jit(solution)/shard_map/ppermute | solution.py:294
  77.0 10.2 %collective-permute-start.40 = (f32[1,128,128]{2,1,0:T(8,128)S(1)}, f32[1,128,128]{2,1,0:T(8,128)S(1)}, u32[]{:S(2)}, u32[]{:S(2)}) collective-permute-start(f32[1,128,128]{2,1,0:T(8,128)S(1)} %get-tuple-element.99), channel_id=1, source_target_pairs={{0,16},{1,17},{2,18},{3,19},{4,20},{5,21},{6,22},{7,23},{8,24},{9,... | collective-permute-start | bytes 196616 | tf_op jit(solution)/shard_map/ppermute | solution.py:294
  80.8 6.4 %collective-permute-start.41 = (f32[1,128,128]{2,1,0:T(8,128)S(1)}, f32[1,128,128]{2,1,0:T(8,128)S(1)}, u32[]{:S(2)}, u32[]{:S(2)}) collective-permute-start(f32[1,128,128]{2,1,0:T(8,128)S(1)} %get-tuple-element.100), channel_id=1, source_target_pairs={{0,24},{1,25},{2,26},{3,27},{4,28},{5,29},{6,30},{7,31},{8,16},{9,... | collective-permute-start | bytes 196616 | tf_op jit(solution)/shard_map/ppermute | solution.py:294
  82.6 7.8 %collective-permute-start.6 = (f32[1,64,128]{2,1,0:T(8,128)S(1)}, f32[1,64,128]{2,1,0:T(8,128)S(1)}, u32[]{:S(2)}, u32[]{:S(2)}) collective-permute-start(f32[1,64,128]{2,1,0:T(8,128)S(1)} %get-tuple-element.63), channel_id=1, source_target_pairs={{0,8},{1,9},{2,10},{3,11},{4,12},{5,13},{6,14},{7,15},{8,0},{9,1},... | collective-permute-start | bytes 98312 | tf_op jit(solution)/shard_map/ppermute | solution.py:294
  82.8 9.0 %collective-permute-start.7 = (f32[1,64,128]{2,1,0:T(8,128)S(1)}, f32[1,64,128]{2,1,0:T(8,128)S(1)}, u32[]{:S(2)}, u32[]{:S(2)}) collective-permute-start(f32[1,64,128]{2,1,0:T(8,128)S(1)} %get-tuple-element.63), channel_id=1, source_target_pairs={{0,16},{1,17},{2,18},{3,19},{4,20},{5,21},{6,22},{7,23},{8,24},{9,... | collective-permute-start | bytes 98312 | tf_op jit(solution)/shard_map/ppermute | solution.py:294
  85.9 6.0 %collective-permute-start.8 = (f32[1,64,128]{2,1,0:T(8,128)S(1)}, f32[1,64,128]{2,1,0:T(8,128)S(1)}, u32[]{:S(2)}, u32[]{:S(2)}) collective-permute-start(f32[1,64,128]{2,1,0:T(8,128)S(1)} %get-tuple-element.63), channel_id=1, source_target_pairs={{0,24},{1,25},{2,26},{3,27},{4,28},{5,29},{6,30},{7,31},{8,16},{9,... | collective-permute-start | bytes 98312 | tf_op jit(solution)/shard_map/ppermute | solution.py:294
  87.2 7.9 %collective-permute-start.18 = (f32[1,64,128]{2,1,0:T(8,128)S(1)}, f32[1,64,128]{2,1,0:T(8,128)S(1)}, u32[]{:S(2)}, u32[]{:S(2)}) collective-permute-start(f32[1,64,128]{2,1,0:T(8,128)S(1)} %get-tuple-element.78), channel_id=1, source_target_pairs={{0,8},{1,9},{2,10},{3,11},{4,12},{5,13},{6,14},{7,15},{8,0},{9,1},... | collective-permute-start | bytes 98312 | tf_op jit(solution)/shard_map/ppermute | solution.py:294
  87.2 9.2 %collective-permute-start.19 = (f32[1,64,128]{2,1,0:T(8,128)S(1)}, f32[1,64,128]{2,1,0:T(8,128)S(1)}, u32[]{:S(2)}, u32[]{:S(2)}) collective-permute-start(f32[1,64,128]{2,1,0:T(8,128)S(1)} %get-tuple-element.78), channel_id=1, source_target_pairs={{0,16},{1,17},{2,18},{3,19},{4,20},{5,21},{6,22},{7,23},{8,24},{9,... | collective-permute-start | bytes 98312 | tf_op jit(solution)/shard_map/ppermute | solution.py:294
  90.5 6.1 %collective-permute-start.20 = (f32[1,64,128]{2,1,0:T(8,128)S(1)}, f32[1,64,128]{2,1,0:T(8,128)S(1)}, u32[]{:S(2)}, u32[]{:S(2)}) collective-permute-start(f32[1,64,128]{2,1,0:T(8,128)S(1)} %get-tuple-element.78), channel_id=1, source_target_pairs={{0,24},{1,25},{2,26},{3,27},{4,28},{5,29},{6,30},{7,31},{8,16},{9,... | collective-permute-start | bytes 98312 | tf_op jit(solution)/shard_map/ppermute | solution.py:294
  91.8 7.8 %collective-permute-start.30 = (f32[1,64,128]{2,1,0:T(8,128)S(1)}, f32[1,64,128]{2,1,0:T(8,128)S(1)}, u32[]{:S(2)}, u32[]{:S(2)}) collective-permute-start(f32[1,64,128]{2,1,0:T(8,128)S(1)} %get-tuple-element.90), channel_id=1, source_target_pairs={{0,8},{1,9},{2,10},{3,11},{4,12},{5,13},{6,14},{7,15},{8,0},{9,1},... | collective-permute-start | bytes 98312 | tf_op jit(solution)/shard_map/ppermute | solution.py:294
  91.9 9.1 %collective-permute-start.31 = (f32[1,64,128]{2,1,0:T(8,128)S(1)}, f32[1,64,128]{2,1,0:T(8,128)S(1)}, u32[]{:S(2)}, u32[]{:S(2)}) collective-permute-start(f32[1,64,128]{2,1,0:T(8,128)S(1)} %get-tuple-element.90), channel_id=1, source_target_pairs={{0,16},{1,17},{2,18},{3,19},{4,20},{5,21},{6,22},{7,23},{8,24},{9,... | collective-permute-start | bytes 98312 | tf_op jit(solution)/shard_map/ppermute | solution.py:294
  95.1 7.1 %collective-permute-start.32 = (f32[1,64,128]{2,1,0:T(8,128)S(1)}, f32[1,64,128]{2,1,0:T(8,128)S(1)}, u32[]{:S(2)}, u32[]{:S(2)}) collective-permute-start(f32[1,64,128]{2,1,0:T(8,128)S(1)} %get-tuple-element.90), channel_id=1, source_target_pairs={{0,24},{1,25},{2,26},{3,27},{4,28},{5,29},{6,30},{7,31},{8,16},{9,... | collective-permute-start | bytes 98312 | tf_op jit(solution)/shard_map/ppermute | solution.py:294
  96.4 6.7 %collective-permute-start.42 = (f32[1,72,128]{2,1,0:T(8,128)S(1)}, f32[1,72,128]{2,1,0:T(8,128)S(1)}, u32[]{:S(2)}, u32[]{:S(2)}) collective-permute-start(f32[1,72,128]{2,1,0:T(8,128)S(1)} %shard_map.81), channel_id=1, source_target_pairs={{0,8},{1,9},{2,10},{3,11},{4,12},{5,13},{6,14},{7,15},{8,0},{9,1},... | collective-permute-start | bytes 110600 | tf_op jit(solution)/shard_map/ppermute | solution.py:294
  96.5 7.8 %collective-permute-start.43 = (f32[1,72,128]{2,1,0:T(8,128)S(1)}, f32[1,72,128]{2,1,0:T(8,128)S(1)}, u32[]{:S(2)}, u32[]{:S(2)}) collective-permute-start(f32[1,72,128]{2,1,0:T(8,128)S(1)} %shard_map.81), channel_id=1, source_target_pairs={{0,16},{1,17},{2,18},{3,19},{4,20},{5,21},{6,22},{7,23},{8,24},{9,... | collective-permute-start | bytes 110600 | tf_op jit(solution)/shard_map/ppermute | solution.py:294
  99.7 5.8 %collective-permute-start.44 = (f32[1,72,128]{2,1,0:T(8,128)S(1)}, f32[1,72,128]{2,1,0:T(8,128)S(1)}, u32[]{:S(2)}, u32[]{:S(2)}) collective-permute-start(f32[1,72,128]{2,1,0:T(8,128)S(1)} %shard_map.81), channel_id=1, source_target_pairs={{0,24},{1,25},{2,26},{3,27},{4,28},{5,29},{6,30},{7,31},{8,16},{9,... | collective-permute-start | bytes 110600 | tf_op jit(solution)/shard_map/ppermute | solution.py:294
  101.0 6.5 %collective-permute-start.9 = (f32[4,64,128]{2,1,0:T(8,128)S(1)}, f32[4,64,128]{2,1,0:T(8,128)S(1)}, u32[]{:S(2)}, u32[]{:S(2)}) collective-permute-start(f32[4,64,128]{2,1,0:T(8,128)S(1)} %pad_maximum_fusion.1), channel_id=1, source_target_pairs={{0,4},{1,3},{2,6},{3,1},{4,0},{5,7},{6,2},{7,5},{8,12},{9,11},{10,... | collective-permute-start | bytes 393224 | tf_op jit(solution)/shard_map/ppermute | solution.py:294
  102.2 8.1 %collective-permute-start.21 = (f32[4,64,128]{2,1,0:T(8,128)S(1)}, f32[4,64,128]{2,1,0:T(8,128)S(1)}, u32[]{:S(2)}, u32[]{:S(2)}) collective-permute-start(f32[4,64,128]{2,1,0:T(8,128)S(1)} %pad_maximum_fusion.2), channel_id=1, source_target_pairs={{0,4},{1,3},{2,6},{3,1},{4,0},{5,7},{6,2},{7,5},{8,12},{9,11},{10,... | collective-permute-start | bytes 393224 | tf_op jit(solution)/shard_map/ppermute | solution.py:294
  103.2 13.3 %collective-permute-start.33 = (f32[4,64,128]{2,1,0:T(8,128)S(1)}, f32[4,64,128]{2,1,0:T(8,128)S(1)}, u32[]{:S(2)}, u32[]{:S(2)}) collective-permute-start(f32[4,64,128]{2,1,0:T(8,128)S(1)} %pad_maximum_fusion.3), channel_id=1, source_target_pairs={{0,4},{1,3},{2,6},{3,1},{4,0},{5,7},{6,2},{7,5},{8,12},{9,11},{10,... | collective-permute-start | bytes 393224 | tf_op jit(solution)/shard_map/ppermute | solution.py:294
  105.5 10.8 %collective-permute-start.45 = (f32[4,72,128]{2,1,0:T(8,128)S(1)}, f32[4,72,128]{2,1,0:T(8,128)S(1)}, u32[]{:S(2)}, u32[]{:S(2)}) collective-permute-start(f32[4,72,128]{2,1,0:T(8,128)S(1)} %pad_maximum_fusion), channel_id=1, source_target_pairs={{0,4},{1,3},{2,6},{3,1},{4,0},{5,7},{6,2},{7,5},{8,12},{9,11},{10,... | collective-permute-start | bytes 442376 | tf_op jit(solution)/shard_map/ppermute | solution.py:294
  107.5 11.0 %collective-permute-start.10 = (f32[8,64,128]{2,1,0:T(8,128)S(1)}, f32[8,64,128]{2,1,0:T(8,128)S(1)}, u32[]{:S(2)}, u32[]{:S(2)}) collective-permute-start(f32[8,64,128]{2,1,0:T(8,128)S(1)} %get-tuple-element.110), channel_id=1, source_target_pairs={{0,2},{1,5},{2,0},{3,7},{4,6},{5,1},{6,4},{7,3},{8,10},{9,13},{10,... | collective-permute-start | bytes 786440 | tf_op jit(solution)/shard_map/ppermute | solution.py:294
  110.3 8.3 %collective-permute-start.22 = (f32[8,64,128]{2,1,0:T(8,128)S(1)}, f32[8,64,128]{2,1,0:T(8,128)S(1)}, u32[]{:S(2)}, u32[]{:S(2)}) collective-permute-start(f32[8,64,128]{2,1,0:T(8,128)S(1)} %get-tuple-element.108), channel_id=1, source_target_pairs={{0,2},{1,5},{2,0},{3,7},{4,6},{5,1},{6,4},{7,3},{8,10},{9,13},{10,... | collective-permute-start | bytes 786440 | tf_op jit(solution)/shard_map/ppermute | solution.py:294
  116.3 6.8 %collective-permute-start.46 = (f32[8,72,128]{2,1,0:T(8,128)S(1)}, f32[8,72,128]{2,1,0:T(8,128)S(1)}, u32[]{:S(2)}, u32[]{:S(2)}) collective-permute-start(f32[8,72,128]{2,1,0:T(8,128)S(1)} %get-tuple-element.104), channel_id=1, source_target_pairs={{0,2},{1,5},{2,0},{3,7},{4,6},{5,1},{6,4},{7,3},{8,10},{9,13},{10,... | collective-permute-start | bytes 884744 | tf_op jit(solution)/shard_map/ppermute | solution.py:294
  116.4 9.5 %collective-permute-start.34 = (f32[8,64,128]{2,1,0:T(8,128)S(1)}, f32[8,64,128]{2,1,0:T(8,128)S(1)}, u32[]{:S(2)}, u32[]{:S(2)}) collective-permute-start(f32[8,64,128]{2,1,0:T(8,128)S(1)} %get-tuple-element.106), channel_id=1, source_target_pairs={{0,2},{1,5},{2,0},{3,7},{4,6},{5,1},{6,4},{7,3},{8,10},{9,13},{10,... | collective-permute-start | bytes 786440 | tf_op jit(solution)/shard_map/ppermute | solution.py:294
  118.5 7.5 %collective-permute-start.11 = (f32[16,64,128]{2,1,0:T(8,128)S(1)}, f32[16,64,128]{2,1,0:T(8,128)S(1)}, u32[]{:S(2)}, u32[]{:S(2)}) collective-permute-start(f32[16,64,128]{2,1,0:T(8,128)S(1)} %constant_dynamic-update-slice_fusion.5.refs_0_), channel_id=1, source_target_pairs={{0,1},{1,0},{2,3},{3,2},{4,5},{5,4},{6,7},{7,6},{8,9},{9,8},{10,11... | collective-permute-start | bytes 1572872 | tf_op jit(solution)/shard_map/ppermute | solution.py:297
  118.6 8.9 %collective-permute-start.23 = (f32[16,64,128]{2,1,0:T(8,128)S(1)}, f32[16,64,128]{2,1,0:T(8,128)S(1)}, u32[]{:S(2)}, u32[]{:S(2)}) collective-permute-start(f32[16,64,128]{2,1,0:T(8,128)S(1)} %constant_dynamic-update-slice_fusion.16.refs_1_), channel_id=1, source_target_pairs={{0,1},{1,0},{2,3},{3,2},{4,5},{5,4},{6,7},{7,6},{8,9},{9,8},{10,11... | collective-permute-start | bytes 1572872 | tf_op jit(solution)/shard_map/ppermute | solution.py:297
  123.1 7.5 %collective-permute-start.47 = (f32[16,72,128]{2,1,0:T(8,128)S(1)}, f32[16,72,128]{2,1,0:T(8,128)S(1)}, u32[]{:S(2)}, u32[]{:S(2)}) collective-permute-start(f32[16,72,128]{2,1,0:T(8,128)S(1)} %constant_dynamic-update-slice_fusion.38.refs_1_), channel_id=1, source_target_pairs={{0,1},{1,0},{2,3},{3,2},{4,5},{5,4},{6,7},{7,6},{8,9},{9,8},{10,11... | collective-permute-start | bytes 1769480 | tf_op jit(solution)/shard_map/ppermute | solution.py:297
  125.9 3.2 %collective-permute-start.35 = (f32[16,64,128]{2,1,0:T(8,128)S(1)}, f32[16,64,128]{2,1,0:T(8,128)S(1)}, u32[]{:S(2)}, u32[]{:S(2)}) collective-permute-start(f32[16,64,128]{2,1,0:T(8,128)S(1)} %constant_dynamic-update-slice_fusion.27.refs_1_), channel_id=1, source_target_pairs={{0,1},{1,0},{2,3},{3,2},{4,5},{5,4},{6,7},{7,6},{8,9},{9,8},{10,11... | collective-permute-start | bytes 1572872 | tf_op jit(solution)/shard_map/ppermute | solution.py:297

commit v2 on v0

v2 whole, which is shorter than its diff:
```python
import functools

import jax
import jax.numpy as jnp
from jax import lax
from jax.experimental import pallas as pl
from jax.experimental.pallas import tpu as pltpu
from jax.sharding import PartitionSpec as P

B = 64
K = 32
NODES = 2
RIDGE = 1.0
LANES = 128
EXTRA = 8
VMEM_LIMIT = 48 * 2**20
SIZES = [2, 2, 2, 2]
BUNDLES = [[0], [1], [2], [3]]
BATCHES = [[0, 1], [2], [3]]


class Plan:
    def __init__(self, devices):
        bits = devices.bit_length() - 1
        assert devices == 1 << bits and bits >= 4
        self.top = devices // 2
        self.unit = self.items = devices // 4
        self.units = B // self.unit
        assert self.units >= 1
        self.stages = [(2, 4), (4, 2)] + [(1 << b, 1 << b) for b in range(3, bits - 1)]

    def partner(self, stage, device):
        return device ^ self.stages[stage][device & 1]

    def mask(self, item, core):
        total = 0
        for i, (even, odd) in enumerate(reversed(self.stages)):
            total = total ^ (((item >> i) & 1) * (even + core * (odd - even)))
        return total

    def low_bin(self, device, item):
        return ((device ^ self.mask(item, device & 1)) >> 1) & (self.unit - 1)

    def mirrored(self, item):
        at = len(self.stages) - 2
        differ = ((item >> at) ^ (item >> (at + 1))) & 1
        return item ^ (differ * (3 << at))

    def sizes(self):
        if self.units == 8:
            return SIZES, BUNDLES, BATCHES
        return [self.units], [[0]], [[0]]


def hist_body(plan, first_unit, count, has_totals, bins, spread, keep, send):
    me = lax.axis_index("dp")
    rows = bins.shape[0]
    step = min(rows, 256)

    @pl.loop(0, plan.items)
    def _(item):
        low_bin = plan.low_bin(me, item)
        for u in range(count):
            level = (first_unit + u) * plan.unit + low_bin
            level = level.astype(jnp.float32).astype(jnp.bfloat16)
            total = jnp.zeros((spread.shape[0], bins.shape[1]), jnp.float32)
            for start in range(0, rows, step):
                below = jnp.where(
                    bins[start : start + step, :] <= level, jnp.bfloat16(1), jnp.bfloat16(0)
                )
                total += jnp.dot(
                    spread[:, start : start + step], below, preferred_element_type=jnp.float32
                )
            at = pl.ds(u * 2 * K, 2 * K)
            keep[item, at, :] = total[: 2 * K, :]
            send[plan.mirrored(item), at, :] = total[2 * K :, :]

    if has_totals:
        sums = jnp.sum(spread[...].astype(jnp.float32), axis=1, keepdims=True)
        lane = lax.broadcasted_iota(jnp.int32, (EXTRA, bins.shape[1]), 1)
        for target, base in ((keep, 0), (send, 2 * K)):
            packed = jnp.zeros((EXTRA, bins.shape[1]), jnp.float32)
            for i in range(2 * K // EXTRA):
                part = sums[base + i * EXTRA : base + (i + 1) * EXTRA, :]
                packed = jnp.where(lane == i, part, packed)
            for item in range(plan.items):
                target[item, pl.ds(count * 2 * K, EXTRA), :] = packed


def first_kernel(plan, count, blocks, *refs):
    bins_in, node_in, grad_in, hess_in, keep, send, bins, spread = refs[:8]
    raw, node, paired, sems = refs[8:]
    me = lax.axis_index("dp")
    core = me & 1
    step = bins.shape[0] // blocks
    width = grad_in.shape[0]
    small = [
        pltpu.make_async_copy(node_in, node, sems.at[0]),
        pltpu.make_async_copy(grad_in, paired.at[pl.ds(0, width), :], sems.at[1]),
        pltpu.make_async_copy(hess_in, paired.at[pl.ds(width, width), :], sems.at[2]),
    ]
    large = [
        pltpu.make_async_copy(
            bins_in.at[pl.ds(i * step, step), :], raw.at[pl.ds(i * step, step), :], sems.at[3 + i]
        )
        for i in range(blocks)
    ]
    for copy in small + large:
        copy.start()
    for copy in small:
        copy.wait()
    for slot in range(NODES):
        here = (node[...] == (core ^ slot)).astype(jnp.float32)
        spread[slot * 2 * K : (slot + 1) * 2 * K, :] = (
            paired[...].astype(jnp.float32) * here
        ).astype(jnp.bfloat16)
    for i, copy in enumerate(large):
        copy.wait()
        at = slice(i * step, (i + 1) * step)
        bins[at, :] = raw[at, :].astype(jnp.float32).astype(jnp.bfloat16)
    hist_body(plan, 0, count, True, bins, spread, keep, send)


def next_kernel(plan, first_unit, count, bins, spread, keep, send):
    hist_body(plan, first_unit, count, False, bins, spread, keep, send)


class Chain:
    def __init__(self):
        self.last = None

    def __call__(
        self, body, out_shape, operands, flops=0, moved=0, in_place=None, out_place=None, **more
    ):
        n = len(operands)
        spec = {
            True: pl.BlockSpec(memory_space=pltpu.VMEM),
            False: pl.BlockSpec(memory_space=pl.ANY),
            None: pl.BlockSpec(memory_space=pltpu.HBM),
        }
        in_specs = [spec[x] for x in in_place or [True] * n]
        out_specs = [spec[x] for x in out_place or [True] * len(out_shape)]
        operands = list(operands)
        if self.last is not None:
            in_specs.append(spec[False])
            operands.append(self.last)

            def run(*refs):
                body(*refs[:n], *refs[n + 1 :])
        else:
            run = body
        outs = pl.pallas_call(
            run,
            out_shape=out_shape,
            in_specs=in_specs,
            out_specs=out_specs,
            compiler_params=pltpu.CompilerParams(vmem_limit_bytes=VMEM_LIMIT),
            cost_estimate=pl.CostEstimate(flops=10**10, bytes_accessed=1024, transcendentals=0),
            **more,
        )(*operands)
        self.last = outs[-1]
        return outs


def f32(*shape):
    return jax.ShapeDtypeStruct(shape, jnp.float32)


def add_body(n_outs, *refs):
    parts, outs = refs[:-n_outs], refs[-n_outs:]
    each = outs[0].shape[0]
    row = 0
    for mine, theirs in zip(parts[::2], parts[1::2], strict=True):
        rows = mine.shape[1]
        for i, out in enumerate(outs):
            at = slice(i * each, (i + 1) * each)
            out[:, row : row + rows, :] = mine[at] + theirs[at]
        row += rows


def join_body(*refs):
    parts, out = refs[:-1], refs[-1]
    each = out.shape[0] // len(parts)
    for i, part in enumerate(parts):
        out[i * each : (i + 1) * each] = part[...]


def score(g, h):
    return g * g / (h + RIDGE)


def curves_body(sizes, n_parts, first_unit, has_totals, last, *refs):
    n = sum(n for n, _ in n_parts)
    parts, refs = refs[:n], refs[n:]
    if has_totals:
        weights, *refs = refs
        if not last:
            totals, gains = refs
    elif last:
        packed, old_gains, weights = refs
    else:
        packed, old_gains, weights, gains = refs
    width = weights.shape[2]
    row = lax.broadcasted_iota(jnp.int32, (EXTRA, width), 0)

    def summed(mine, start):
        total = mine[0][0, start : start + EXTRA, :]
        for part in mine[1:]:
            total += part[0, start : start + EXTRA, :]
        return total

    if has_totals:
        block = summed(parts[: n_parts[0][0]], sizes[0] * 2 * K)
        gain_rows = jnp.zeros((EXTRA, width), jnp.float32)
        if not last:
            totals[...] = block
    else:
        block = packed[...]
        gain_rows = old_gains[...]
    columns = [
        jnp.broadcast_to(block[:, i : i + 1], (EXTRA, width)) for i in range(2 * K // EXTRA)
    ]
    unit = 0
    taken = 0
    for n, chunks in n_parts:
        mine = parts[taken : taken + n]
        taken += n
        at = 0
        for chunk in chunks:
            for u in range(sizes[chunk]):
                gain = jnp.zeros((EXTRA, width), jnp.float32)
                for i in range(K // EXTRA):
                    gl = summed(mine, at + i * EXTRA)
                    hl = summed(mine, at + K + i * EXTRA)
                    g, h = columns[i], columns[K // EXTRA + i]
                    gain += score(gl, hl) + score(g - gl, h - hl) - score(g, h)
                    to = unit * K + i * EXTRA
                    weights[0, to : to + EXTRA, :] = -gl / (hl + RIDGE)
                mean = jnp.sum(gain, axis=0, keepdims=True) / K
                gain_rows = jnp.where(row == first_unit + unit, mean, gain_rows)
                at += 2 * K
                unit += 1
            if has_totals and chunk == 0:
                at += EXTRA
    if last:
        weights[0, unit * K : unit * K + EXTRA, :] = gain_rows
    else:
        gains[...] = gain_rows


def place_body(plan, first_unit, count, last, first, *refs):
    if not first:
        refs = refs[1:]
    mine, theirs, weights = refs[:3]
    if last:
        gains, held, lines, sems, held_sems = refs[3:]
    else:
        token, sems = refs[3:]
        token[...] = jnp.zeros_like(token)
    me = lax.axis_index("dp")
    copies = []
    fetched = []
    for side, source in enumerate((mine, theirs)):
        who = me ^ side
        if last:
            fetch = pltpu.make_async_copy(
                source.at[:, pl.ds(count * K, EXTRA), :], held.at[side], held_sems.at[side]
            )
            fetch.start()
            fetched.append(fetch)
        for item in range(plan.items):
            low_bin = plan.low_bin(who, item)
            for u in range(count):
                copy = pltpu.make_async_copy(
                    source.at[item, pl.ds(u * K, K), :],
                    weights.at[who & 1, (first_unit + u) * plan.unit + low_bin],
                    sems.at[(side * plan.items + item) * count + u],
                )
                copy.start()
                copies.append(copy)
    if last:
        for side in range(2):
            fetched[side].wait()
        for side in range(2):
            who = me ^ side
            for item in range(plan.items):
                low_bin = plan.low_bin(who, item)
                for u in range(plan.units):
                    line = pl.ds(u * plan.unit + low_bin, 1)
                    for h in range(lines.shape[0]):
                        lines[h, who & 1, line, :] = held[
                            side, item, u : u + 1, h * LANES : (h + 1) * LANES
                        ]
        for h in range(lines.shape[0]):
            gains[:, :, h * LANES : (h + 1) * LANES] = lines[h]
    for copy in copies:
        copy.wait()


def on_device(bin_index, node_ids, gradients, hessians):
    devices = lax.axis_size("dp")
    plan = Plan(devices)
    rows, features = bin_index.shape
    width = gradients.shape[1]
    chain = Chain()

    def swap(x, partner):
        return lax.ppermute(x, "dp", [(d, partner(d)) for d in range(devices)])

    def swap_stage(x, stage):
        return swap(x, functools.partial(plan.partner, stage))

    def swap_cores(x):
        return swap(x, lambda d: d ^ 1)

    def swap_top(x):
        return swap(x, lambda d: d ^ plan.top)

    sizes, bundles, batches = plan.sizes()
    starts = [sum(sizes[:i]) for i in range(len(sizes))]
    n_stages = len(plan.stages)
    got = {}
    shared = {}

    def depth(chunk):
        return sizes[chunk] * 2 * K + (EXTRA if chunk == 0 else 0)

    def add(parts, groups):
        height = sum(p.shape[1] for p, _ in parts)
        items = parts[0][0].shape[0] // groups
        return chain(
            functools.partial(add_body, groups), [f32(items, height, features)] * groups, sum(parts, [])
        )

    def histogram(c):
        halves = [f32(plan.items, depth(c), features)] * 2
        if c == 0:
            blocks = 8
            keep, send, bins, spread = chain(
                functools.partial(first_kernel, plan, sizes[c], blocks),
                [
                    *halves,
                    jax.ShapeDtypeStruct((rows, features), jnp.bfloat16),
                    jax.ShapeDtypeStruct((NODES * 2 * K, rows), jnp.bfloat16),
                ],
                [
                    pltpu.with_memory_space_constraint(x, pltpu.HBM)
                    for x in (bin_index, node_ids.reshape(1, rows), gradients.T, hessians.T)
                ],
                in_place=[None] * 4,
                scratch_shapes=[
                    pltpu.VMEM((rows, features), jnp.int32),
                    pltpu.VMEM((1, rows), jnp.int32),
                    pltpu.VMEM((2 * width, rows), jnp.bfloat16),
                    pltpu.SemaphoreType.DMA((3 + blocks,)),
                ],
            )
            shared["data"] = (bins, spread)
        else:
            keep, send = chain(
                functools.partial(next_kernel, plan, starts[c], sizes[c]), halves, shared["data"]
            )
        got["C", c] = [keep, swap_cores(send)]

    def over_cores(c):
        mine, other = add([got["C", c]], 2)
        got["S", c] = [mine, swap_stage(other, 0)]

    def over_first(c):
        mine, other = add([got["S", c]], 2)
        got["T", c] = [mine, swap_stage(other, 1)]

    def over_next(b, stage):
        parts = [got["T", c] for c in bundles[b]] if stage == 2 else [got["Z", b]]
        if stage < n_stages:
            mine, other = add(parts, 2)
            got["Z", b] = [mine, swap_stage(other, stage)]
        else:
            (mine,) = add(parts, 1)
            got["Z", b] = [mine, swap_top(mine)]

    def curves(g):
        batch = batches[g]
        chunks = [c for b in batch for c in bundles[b]]
        count = sum(sizes[c] for c in chunks)
        last = g == len(batches) - 1
        parts = sum((got["Z", b] for b in batch), [])
        n_parts = [(len(got["Z", b]), bundles[b]) for b in batch]
        outs = [f32(1, count * K + (EXTRA if last else 0), features)]
        if not last:
            outs += [f32(EXTRA, features)] * (2 if g == 0 else 1)
        extra = [] if g == 0 else [shared["totals"], shared["gains"]]
        outs = chain(
            functools.partial(curves_body, sizes, n_parts, starts[chunks[0]], g == 0, last),
            outs,
            parts + extra,
        )
        if not last:
            shared["gains"] = outs[-1]
            if g == 0:
                shared["totals"] = outs[1]
        got["G", g] = [outs[0], swap_stage(outs[0], n_stages - 1)]

    def gather(g, stage):
        parts = got["G", g]
        items, height, _ = parts[0].shape
        (joined,) = chain(join_body, [f32(2 * items, height, features)], parts)
        got["G", g] = [joined, swap_stage(joined, stage - 1) if stage else swap_cores(joined)]

    def place(g):
        chunks = [c for b in batches[g] for c in bundles[b]]
        count = sum(sizes[c] for c in chunks)
        last = g == len(batches) - 1
        out_shape = [f32(NODES, B, K, features), f32(EXTRA, LANES)]
        scratch = [pltpu.SemaphoreType.DMA((2 * plan.items * count,))]
        if last:
            out_shape[1] = f32(NODES, B, features)
            scratch = [
                pltpu.VMEM((2, plan.items, EXTRA, features), jnp.float32),
                pltpu.VMEM((features // LANES, NODES, B, LANES), jnp.float32),
                *scratch,
                pltpu.SemaphoreType.DMA((2,)),
            ]
        buffer = [] if g == 0 else [shared["weights"]]
        operands = [*buffer, *got["G", g]]
        shared["weights"], shared["gains_out"] = chain(
            functools.partial(place_body, plan, starts[chunks[0]], count, last, g == 0),
            out_shape,
            operands,
            in_place=[None] * len(buffer) + [False] * 2,
            out_place=[None, True],
            scratch_shapes=scratch,
            input_output_aliases={0: 0} if buffer else {},
        )

    tasks = []
    for c in range(len(sizes)):
        tasks += [(c - 0.2, histogram, c), (c + 0.9, over_cores, c), (c + 2, over_first, c)]
    for b, bundle in enumerate(bundles):
        for stage in range(2, n_stages + 1):
            tasks.append((bundle[-1] + 1 + stage + 0.02 * stage, over_next, b, stage))
    for g, batch in enumerate(batches):
        at = bundles[batch[-1]][-1] + n_stages + 2.1 - (0.5 if g < len(batches) - 1 else 0)
        tasks.append((at, curves, g))
        for i, stage in enumerate(reversed(range(n_stages))):
            tasks.append((at + 1 + i, gather, g, stage))
        tasks.append((at + 1 + n_stages, place, g))
    for _, task, *arguments in sorted(tasks, key=lambda t: t[0]):
        task(*arguments)
    return shared["gains_out"].transpose(2, 0, 1), shared["weights"].transpose(3, 0, 1, 2)


def solution(mesh):
    return jax.shard_map(
        on_device,
        mesh=mesh,
        in_specs=(P("dp", None), P("dp"), P("dp", None), P("dp", None)),
        out_specs=(P(), P()),
        check_vma=False,
    )
```

time: 402 us -> 102 us (0.25)
  waiting for transfers between devices: 228 us -> 43.2 us
  matrix products: 68.9 us -> 0 us
  local copies, waits for them, and re-layouts: 49.9 us -> 0 us
  other arithmetic: 39.9 us -> 0 us
  starting transfers between devices: 0.08 us -> 34.5 us
  Pallas kernels: 0 us -> 23 us
  between operations: 14.1 us -> 0.98 us
    reduce_scatter x1 -> x0, waiting for transfers between devices: 152 us -> none  [on_device(): lax.psum_scatter(lax.fori_loop(0, rows_here // row_step, add_block, empty...]
    all_gather x1 -> x0, waiting for transfers between devices: 76.2 us -> none  [on_device(): whole = lax.all_gather(owned, 'dp', axis=0, tiled=True)]
    dot_general x8 -> x0, matrix products: 68.9 us -> none  [add_block(): lax.dot_general(onehot, block_spread, (((0,), (0,)), ((), ())), preferred...]
    ppermute x0 -> x32, waiting for transfers between devices: none -> 43.2 us  [swap(): return lax.ppermute(x, 'dp', [(d, partner(d)) for d in range(devices)])]
    ppermute x0 -> x32, starting transfers between devices: none -> 34.5 us  [swap(): return lax.ppermute(x, 'dp', [(d, partner(d)) for d in range(devices)])]
    pallas_call x0 -> x35, Pallas kernels: none -> 23 us  [__call__(): pl.pallas_call(run, out_shape=out_shape, in_specs=in_specs, out_specs=out...]
    eq x8 -> x0, other arithmetic: 22.7 us -> none  [add_block(): block_bins[:, :, None] == levels[None, None, :]]
    transpose x1 -> x0, local copies, waits for them, and re-layouts: 13.6 us -> none  [arrange(): return jnp.transpose(hist.reshape(-1, B, NODES, 2 * K), (0, 2, 1, 3))]
  transfers between devices with their start and end apart: 2 -> 32, of which waited for: 2 -> 16; matrix products, arithmetic and copies ran while one was open for 0% -> 0% of each run, Pallas kernels for 0% -> 15%
where the time goes in v2:
time: 102 us
  waiting for transfers between devices  43.2 us (42%)
  starting transfers between devices  34.5 us (34%)
  Pallas kernels  23 us (23%)
    ppermute x32, waiting for transfers between devices, swap(): return lax.ppermute(x, 'dp', [(d, partner(d)) for d in range(devices)])  43.2 us
    ppermute x32, starting transfers between devices, swap(): return lax.ppermute(x, 'dp', [(d, partner(d)) for d in range(devices)])  34.5 us
    pallas_call x35, Pallas kernels, __call__(): pl.pallas_call(run, out_shape=out_shape, in_specs=in_specs, out_specs=out...  23 us
  transfers between devices with their start and end apart: 32, of which 16 were waited for; matrix products, arithmetic and copies ran while one was open for 0% of the time, Pallas kernels for 15%

profile of v2, /device:TPU:0, one launch (start us, length us, event | category | flops | bytes accessed | tf_op | source)
XLA Modules:
  0.0 101.7 jit_solution(15347105436605835385)
XLA Ops:
  0.6 5.5 %shard_map.59 = (f32[8,136,256]{2,1,0:T(8,128)S(1)}, f32[8,136,256]{2,1,0:T(8,128)S(1)}, bf16[2048,256]{1,0:T(8,128)(2,1)S(1)}, bf16[128,2048]{1,0:T(8,128)(2,1)S(1)}) custom-call(s32[2048,256]{1,0:T(8,128)} %refs_0_.1, s32[1,2048]{1,0:T(1,128)} %bitcast.7, bf16[32,2048]{1,0:T(8,128)(2,1)} %bitcast.5, bf16[32,2048]{1,0:T(8,128)(2,1)} %bitcast.6), custom_call_target="tpu_custom_call" | custom-call | flops 10000000000 | bytes 1024 | tf_op jit(solution)/shard_map/pallas_call | solution.py:152
  6.2 0.6 collective-permute-start
  6.7 3.6 %shard_map.60 = (f32[8,128,256]{2,1,0:T(8,128)S(1)}, f32[8,128,256]{2,1,0:T(8,128)S(1)}) custom-call(bf16[2048,256]{1,0:T(8,128)(2,1)S(1)} %get-tuple-element.49.refs_0_, bf16[128,2048]{1,0:T(8,128)(2,1)S(1)} %get-tuple-element.50.refs_1_.refs_2_, bf16[128,2048]{1,0:T(8,128)(2,1)S(1)} %get-tuple-element.50.refs_1_.refs_2_), custom_call_target="tpu_custom_call" | custom-call | flops 10000000000 | bytes 1024 | tf_op jit(solution)/shard_map/pallas_call | solution.py:152
  10.4 0.1 collective-permute-start.2
  10.5 0.1 shard_map.61
  10.6 3.0 %collective-permute-start.1 = (f32[4,136,256]{2,1,0:T(8,128)S(1)}, f32[4,136,256]{2,1,0:T(8,128)S(1)}, u32[]{:S(2)}, u32[]{:S(2)}) collective-permute-start(f32[4,136,256]{2,1,0:T(8,128)S(1)} %get-tuple-element.53.refs_2_), channel_id=1, source_target_pairs={{0,2},{1,5},{2,0},{3,7},{4,6},{5,1},{6,4},{7,3},{8,10},{9,13},{10,... | collective-permute-start | bytes 1671176 | tf_op jit(solution)/shard_map/ppermute | solution.py:308
  13.6 3.7 %shard_map.62 = (f32[8,128,256]{2,1,0:T(8,128)S(1)}, f32[8,128,256]{2,1,0:T(8,128)S(1)}) custom-call(bf16[2048,256]{1,0:T(8,128)(2,1)S(1)} %get-tuple-element.49.refs_0_, bf16[128,2048]{1,0:T(8,128)(2,1)S(1)} %get-tuple-element.50.refs_1_.refs_2_, f32[4,136,256]{2,1,0:T(8,128)S(1)} %get-tuple-element.53.refs_2_), custom_call_target="tpu_custom_call" | custom-call | flops 10000000000 | bytes 1024 | tf_op jit(solution)/shard_map/pallas_call | solution.py:152
  17.3 0.1 collective-permute-start.5
  17.4 0.1 shard_map.63
  17.5 1.4 %collective-permute-start.4 = (f32[4,128,256]{2,1,0:T(8,128)S(1)}, f32[4,128,256]{2,1,0:T(8,128)S(1)}, u32[]{:S(2)}, u32[]{:S(2)}) collective-permute-start(f32[4,128,256]{2,1,0:T(8,128)S(1)} %get-tuple-element.56.refs_2_), channel_id=1, source_target_pairs={{0,2},{1,5},{2,0},{3,7},{4,6},{5,1},{6,4},{7,3},{8,10},{9,13},{10,... | collective-permute-start | bytes 1572872 | tf_op jit(solution)/shard_map/ppermute | solution.py:308
  18.9 2.3 %collective-permute-done.1.refs_1_ = f32[4,136,256]{2,1,0:T(8,128)S(1)} collective-permute-done((f32[4,136,256]{2,1,0:T(8,128)S(1)}, f32[4,136,256]{2,1,0:T(8,128)S(1)}, u32[]{:S(2)}, u32[]{:S(2)}) %collective-permute-start.1) | collective-permute-done | bytes 557088 | tf_op jit(solution)/shard_map/ppermute | solution.py:308
  21.2 2.1 %collective-permute-start.3 = (f32[2,136,256]{2,1,0:T(8,128)S(1)}, f32[2,136,256]{2,1,0:T(8,128)S(1)}, u32[]{:S(2)}, u32[]{:S(2)}) collective-permute-start(f32[2,136,256]{2,1,0:T(8,128)S(1)} %get-tuple-element.58.refs_2_), channel_id=1, source_target_pairs={{0,4},{1,3},{2,6},{3,1},{4,0},{5,7},{6,2},{7,5},{8,12},{9,11},{10,... | collective-permute-start | bytes 835592 | tf_op jit(solution)/shard_map/ppermute | solution.py:308
  23.3 3.7 %shard_map.65 = (f32[8,128,256]{2,1,0:T(8,128)S(1)}, f32[8,128,256]{2,1,0:T(8,128)S(1)}) custom-call(bf16[2048,256]{1,0:T(8,128)(2,1)S(1)} %get-tuple-element.49.refs_0_, bf16[128,2048]{1,0:T(8,128)(2,1)S(1)} %get-tuple-element.50.refs_1_.refs_2_, f32[2,136,256]{2,1,0:T(8,128)S(1)} %get-tuple-element.58.refs_2_), custom_call_target="tpu_custom_call" | custom-call | flops 10000000000 | bytes 1024 | tf_op jit(solution)/shard_map/pallas_call | solution.py:152
  27.0 0.1 collective-permute-start.9
  27.1 0.1 shard_map.66
  27.2 1.6 %collective-permute-start.8 = (f32[4,128,256]{2,1,0:T(8,128)S(1)}, f32[4,128,256]{2,1,0:T(8,128)S(1)}, u32[]{:S(2)}, u32[]{:S(2)}) collective-permute-start(f32[4,128,256]{2,1,0:T(8,128)S(1)} %get-tuple-element.62.refs_2_), channel_id=1, source_target_pairs={{0,2},{1,5},{2,0},{3,7},{4,6},{5,1},{6,4},{7,3},{8,10},{9,13},{10,... | collective-permute-start | bytes 1572872 | tf_op jit(solution)/shard_map/ppermute | solution.py:308
  28.8 0.9 collective-permute-done.4.refs_1_
  29.8 2.1 %collective-permute-start.7 = (f32[2,128,256]{2,1,0:T(8,128)S(1)}, f32[2,128,256]{2,1,0:T(8,128)S(1)}, u32[]{:S(2)}, u32[]{:S(2)}) collective-permute-start(f32[2,128,256]{2,1,0:T(8,128)S(1)} %get-tuple-element.63.refs_2_), channel_id=1, source_target_pairs={{0,4},{1,3},{2,6},{3,1},{4,0},{5,7},{6,2},{7,5},{8,12},{9,11},{10,... | collective-permute-start | bytes 786440 | tf_op jit(solution)/shard_map/ppermute | solution.py:308
  32.0 1.6 %collective-permute-start.6 = (f32[1,136,256]{2,1,0:T(8,128)S(1)}, f32[1,136,256]{2,1,0:T(8,128)S(1)}, u32[]{:S(2)}, u32[]{:S(2)}) collective-permute-start(f32[1,136,256]{2,1,0:T(8,128)S(1)} %get-tuple-element.65.refs_2_), channel_id=1, source_target_pairs={{0,8},{1,9},{2,10},{3,11},{4,12},{5,13},{6,14},{7,15},{8,0},{9,1},... | collective-permute-start | bytes 417800 | tf_op jit(solution)/shard_map/ppermute | solution.py:308
  33.6 0.1 shard_map.69
  33.7 1.5 %collective-permute-start.13 = (f32[4,128,256]{2,1,0:T(8,128)S(1)}, f32[4,128,256]{2,1,0:T(8,128)S(1)}, u32[]{:S(2)}, u32[]{:S(2)}) collective-permute-start(f32[4,128,256]{2,1,0:T(8,128)S(1)} %get-tuple-element.69.refs_2_), channel_id=1, source_target_pairs={{0,2},{1,5},{2,0},{3,7},{4,6},{5,1},{6,4},{7,3},{8,10},{9,13},{10,... | collective-permute-start | bytes 1572872 | tf_op jit(solution)/shard_map/ppermute | solution.py:308
  35.3 3.7 %collective-permute-done.8.refs_1_ = f32[4,128,256]{2,1,0:T(8,128)S(1)} collective-permute-done((f32[4,128,256]{2,1,0:T(8,128)S(1)}, f32[4,128,256]{2,1,0:T(8,128)S(1)}, u32[]{:S(2)}, u32[]{:S(2)}) %collective-permute-start.8) | collective-permute-done | bytes 524320 | tf_op jit(solution)/shard_map/ppermute | solution.py:308
  39.0 0.1 shard_map.70
  39.0 1.3 %collective-permute-start.12 = (f32[2,128,256]{2,1,0:T(8,128)S(1)}, f32[2,128,256]{2,1,0:T(8,128)S(1)}, u32[]{:S(2)}, u32[]{:S(2)}) collective-permute-start(f32[2,128,256]{2,1,0:T(8,128)S(1)} %get-tuple-element.70.refs_2_), channel_id=1, source_target_pairs={{0,4},{1,3},{2,6},{3,1},{4,0},{5,7},{6,2},{7,5},{8,12},{9,11},{10,... | collective-permute-start | bytes 786440 | tf_op jit(solution)/shard_map/ppermute | solution.py:308
  40.4 1.6 %collective-permute-start.11 = (f32[1,128,256]{2,1,0:T(8,128)S(1)}, f32[1,128,256]{2,1,0:T(8,128)S(1)}, u32[]{:S(2)}, u32[]{:S(2)}) collective-permute-start(f32[1,128,256]{2,1,0:T(8,128)S(1)} %get-tuple-element.71.refs_2_), channel_id=1, source_target_pairs={{0,8},{1,9},{2,10},{3,11},{4,12},{5,13},{6,14},{7,15},{8,0},{9,1},... | collective-permute-start | bytes 393224 | tf_op jit(solution)/shard_map/ppermute | solution.py:308
  42.1 2.7 %collective-permute-start.10 = (f32[1,136,256]{2,1,0:T(8,128)S(1)}, f32[1,136,256]{2,1,0:T(8,128)S(1)}, u32[]{:S(2)}, u32[]{:S(2)}) collective-permute-start(f32[1,136,256]{2,1,0:T(8,128)S(1)} %shard_map.72.refs_2_.refs_0_), channel_id=1, source_target_pairs={{0,16},{1,17},{2,18},{3,19},{4,20},{5,21},{6,22},{7,23},{8,24},{9,... | collective-permute-start | bytes 417800 | tf_op jit(solution)/shard_map/ppermute | solution.py:308
  44.7 2.7 %collective-permute-done.13.refs_1_ = f32[4,128,256]{2,1,0:T(8,128)S(1)} collective-permute-done((f32[4,128,256]{2,1,0:T(8,128)S(1)}, f32[4,128,256]{2,1,0:T(8,128)S(1)}, u32[]{:S(2)}, u32[]{:S(2)}) %collective-permute-start.13) | collective-permute-done | bytes 524320 | tf_op jit(solution)/shard_map/ppermute | solution.py:308
  47.4 0.1 shard_map.73
  47.5 2.8 %collective-permute-start.14 = (f32[1,128,256]{2,1,0:T(8,128)S(1)}, f32[1,128,256]{2,1,0:T(8,128)S(1)}, u32[]{:S(2)}, u32[]{:S(2)}) collective-permute-start(f32[1,128,256]{2,1,0:T(8,128)S(1)} %shard_map.75.refs_2_.refs_4_), channel_id=1, source_target_pairs={{0,16},{1,17},{2,18},{3,19},{4,20},{5,21},{6,22},{7,23},{8,24},{9,... | collective-permute-start | bytes 393224 | tf_op jit(solution)/shard_map/ppermute | solution.py:308
  50.3 1.1 %collective-permute-start.17 = (f32[2,128,256]{2,1,0:T(8,128)S(1)}, f32[2,128,256]{2,1,0:T(8,128)S(1)}, u32[]{:S(2)}, u32[]{:S(2)}) collective-permute-start(f32[2,128,256]{2,1,0:T(8,128)S(1)} %get-tuple-element.75.refs_2_), channel_id=1, source_target_pairs={{0,4},{1,3},{2,6},{3,1},{4,0},{5,7},{6,2},{7,5},{8,12},{9,11},{10,... | collective-permute-start | bytes 786440 | tf_op jit(solution)/shard_map/ppermute | solution.py:308
  51.4 1.6 %collective-permute-start.16 = (f32[1,128,256]{2,1,0:T(8,128)S(1)}, f32[1,128,256]{2,1,0:T(8,128)S(1)}, u32[]{:S(2)}, u32[]{:S(2)}) collective-permute-start(f32[1,128,256]{2,1,0:T(8,128)S(1)} %get-tuple-element.76.refs_2_), channel_id=1, source_target_pairs={{0,8},{1,9},{2,10},{3,11},{4,12},{5,13},{6,14},{7,15},{8,0},{9,1},... | collective-permute-start | bytes 393224 | tf_op jit(solution)/shard_map/ppermute | solution.py:308
  53.1 3.4 %collective-permute-done.14.refs_3_ = f32[1,128,256]{2,1,0:T(8,128)S(1)} collective-permute-done((f32[1,128,256]{2,1,0:T(8,128)S(1)}, f32[1,128,256]{2,1,0:T(8,128)S(1)}, u32[]{:S(2)}, u32[]{:S(2)}) %collective-permute-start.14) | collective-permute-done | bytes 131104 | tf_op jit(solution)/shard_map/ppermute | solution.py:308
  56.4 0.1 shard_map.76
  56.6 0.1 collective-permute-start.15
  56.6 0.1 collective-permute-done.17.refs_1_
  56.7 2.0 %collective-permute-start.19 = (f32[1,128,256]{2,1,0:T(8,128)S(1)}, f32[1,128,256]{2,1,0:T(8,128)S(1)}, u32[]{:S(2)}, u32[]{:S(2)}) collective-permute-start(f32[1,128,256]{2,1,0:T(8,128)S(1)} %get-tuple-element.81.refs_2_), channel_id=1, source_target_pairs={{0,8},{1,9},{2,10},{3,11},{4,12},{5,13},{6,14},{7,15},{8,0},{9,1},... | collective-permute-start | bytes 393224 | tf_op jit(solution)/shard_map/ppermute | solution.py:308
  58.8 1.4 %collective-permute-start.20 = (f32[1,128,256]{2,1,0:T(8,128)S(1)}, f32[1,128,256]{2,1,0:T(8,128)S(1)}, u32[]{:S(2)}, u32[]{:S(2)}) collective-permute-start(f32[1,128,256]{2,1,0:T(8,128)S(1)} %shard_map.78.refs_2_.refs_0_), channel_id=1, source_target_pairs={{0,16},{1,17},{2,18},{3,19},{4,20},{5,21},{6,22},{7,23},{8,24},{9,... | collective-permute-start | bytes 393224 | tf_op jit(solution)/shard_map/ppermute | solution.py:308
  60.2 5.0 %collective-permute-done.15.refs_1_ = f32[1,128,256]{2,1,0:T(8,128)S(1)} collective-permute-done((f32[1,128,256]{2,1,0:T(8,128)S(1)}, f32[1,128,256]{2,1,0:T(8,128)S(1)}, u32[]{:S(2)}, u32[]{:S(2)}) %collective-permute-start.15) | collective-permute-done | bytes 131104 | tf_op jit(solution)/shard_map/ppermute | solution.py:308
  65.2 0.1 collective-permute-start.18
  65.3 0.6 collective-permute-done.20.refs_1_
  65.9 0.1 shard_map.80
  66.0 2.6 %collective-permute-start.23 = (f32[1,64,256]{2,1,0:T(8,128)S(1)}, f32[1,64,256]{2,1,0:T(8,128)S(1)}, u32[]{:S(2)}, u32[]{:S(2)}) collective-permute-start(f32[1,64,256]{2,1,0:T(8,128)S(1)} %get-tuple-element.85.refs_0_), channel_id=1, source_target_pairs={{0,8},{1,9},{2,10},{3,11},{4,12},{5,13},{6,14},{7,15},{8,0},{9,1},... | collective-permute-start | bytes 196616 | tf_op jit(solution)/shard_map/ppermute | solution.py:308
  68.6 2.0 %collective-permute-start.22 = (f32[1,128,256]{2,1,0:T(8,128)S(1)}, f32[1,128,256]{2,1,0:T(8,128)S(1)}, u32[]{:S(2)}, u32[]{:S(2)}) collective-permute-start(f32[1,128,256]{2,1,0:T(8,128)S(1)} %shard_map.81.refs_2_.refs_0_), channel_id=1, source_target_pairs={{0,16},{1,17},{2,18},{3,19},{4,20},{5,21},{6,22},{7,23},{8,24},{9,... | collective-permute-start | bytes 393224 | tf_op jit(solution)/shard_map/ppermute | solution.py:308
  70.6 3.0 %collective-permute-done.18.refs_1_ = f32[2,128,256]{2,1,0:T(8,128)S(1)} collective-permute-done((f32[2,128,256]{2,1,0:T(8,128)S(1)}, f32[2,128,256]{2,1,0:T(8,128)S(1)}, u32[]{:S(2)}, u32[]{:S(2)}) %collective-permute-start.18) | collective-permute-done | bytes 262176 | tf_op jit(solution)/shard_map/ppermute | solution.py:308
  73.6 0.1 collective-permute-start.21
  73.7 0.1 collective-permute-start.26
  73.9 1.7 %collective-permute-done.22.refs_1_ = f32[1,128,256]{2,1,0:T(8,128)S(1)} collective-permute-done((f32[1,128,256]{2,1,0:T(8,128)S(1)}, f32[1,128,256]{2,1,0:T(8,128)S(1)}, u32[]{:S(2)}, u32[]{:S(2)}) %collective-permute-start.22) | collective-permute-done | bytes 131104 | tf_op jit(solution)/shard_map/ppermute | solution.py:308
  75.6 0.1 shard_map.84.refs_2_.refs_0_
  75.7 0.1 collective-permute-start.25
  75.8 7.1 %collective-permute-done.21.refs_1_ = f32[4,128,256]{2,1,0:T(8,128)S(1)} collective-permute-done((f32[4,128,256]{2,1,0:T(8,128)S(1)}, f32[4,128,256]{2,1,0:T(8,128)S(1)}, u32[]{:S(2)}, u32[]{:S(2)}) %collective-permute-start.21) | collective-permute-done | bytes 524320 | tf_op jit(solution)/shard_map/ppermute | solution.py:308
  83.0 0.1 collective-permute-start.24
  83.1 0.1 collective-permute-start.27
  83.2 0.1 collective-permute-start.29
  83.3 2.4 %collective-permute-done.24.refs_1_ = f32[8,128,256]{2,1,0:T(8,128)S(1)} collective-permute-done((f32[8,128,256]{2,1,0:T(8,128)S(1)}, f32[8,128,256]{2,1,0:T(8,128)S(1)}, u32[]{:S(2)}, u32[]{:S(2)}) %collective-permute-start.24) | collective-permute-done | bytes 1048608 | tf_op jit(solution)/shard_map/ppermute | solution.py:308
  85.7 1.9 %shard_map.88 = (f32[2,64,32,256]{3,2,1,0:T(8,128)}, f32[8,128]{1,0:T(8,128)S(1)}) custom-call(f32[8,128,256]{2,1,0:T(8,128)S(1)} %shard_map.85.refs_2_.refs_0_, f32[8,128,256]{2,1,0:T(8,128)S(1)} %collective-permute-done.24.refs_1_, f32[2,72,256]{2,1,0:T(8,128)S(1)} %shard_map.87.refs_2_.refs_0_), custom_call_target="tpu_custom_call" | custom-call | flops 10000000000 | bytes 1024 | tf_op jit(solution)/shard_map/pallas_call | solution.py:152
  87.5 3.2 %collective-permute-done.27.refs_1_ = f32[4,64,256]{2,1,0:T(8,128)S(1)} collective-permute-done((f32[4,64,256]{2,1,0:T(8,128)S(1)}, f32[4,64,256]{2,1,0:T(8,128)S(1)}, u32[]{:S(2)}, u32[]{:S(2)}) %collective-permute-start.27) | collective-permute-done | bytes 262176 | tf_op jit(solution)/shard_map/ppermute | solution.py:308
  90.8 0.1 collective-permute-start.28
  90.9 0.4 collective-permute-start.30
  91.2 1.5 %collective-permute-done.28.refs_2_ = f32[8,64,256]{2,1,0:T(8,128)S(1)} collective-permute-done((f32[8,64,256]{2,1,0:T(8,128)S(1)}, f32[8,64,256]{2,1,0:T(8,128)S(1)}, u32[]{:S(2)}, u32[]{:S(2)}) %collective-permute-start.28) | collective-permute-done | bytes 524320 | tf_op jit(solution)/shard_map/ppermute | solution.py:308
  92.7 1.2 %shard_map.91 = (f32[2,64,32,256]{3,2,1,0:T(8,128)}, f32[8,128]{1,0:T(8,128)S(1)}) custom-call(f32[2,64,32,256]{3,2,1,0:T(8,128)} %get-tuple-element.86.refs_0_, f32[8,64,256]{2,1,0:T(8,128)S(1)} %shard_map.89.refs_2_.refs_1_, f32[8,64,256]{2,1,0:T(8,128)S(1)} %collective-permute-done.28.refs_2_, ...), custom_call_target="tpu_custom_call", output_to_operand_aliasing={{0}: (0, {})} | custom-call | flops 10000000000 | bytes 1024 | tf_op jit(solution)/shard_map/pallas_call | solution.py:152
  94.0 3.7 %collective-permute-done.30.refs_1_ = f32[4,72,256]{2,1,0:T(8,128)S(1)} collective-permute-done((f32[4,72,256]{2,1,0:T(8,128)S(1)}, f32[4,72,256]{2,1,0:T(8,128)S(1)}, u32[]{:S(2)}, u32[]{:S(2)}) %collective-permute-start.30) | collective-permute-done | bytes 294944 | tf_op jit(solution)/shard_map/ppermute | solution.py:308
  97.7 0.1 collective-permute-start.31
  97.8 2.0 %collective-permute-done.31.refs_2_ = f32[8,72,256]{2,1,0:T(8,128)S(1)} collective-permute-done((f32[8,72,256]{2,1,0:T(8,128)S(1)}, f32[8,72,256]{2,1,0:T(8,128)S(1)}, u32[]{:S(2)}, u32[]{:S(2)}) %collective-permute-start.31) | collective-permute-done | bytes 589856 | tf_op jit(solution)/shard_map/ppermute | solution.py:308
  99.8 1.9 %shard_map.93 = (f32[2,64,32,256]{3,2,1,0:T(8,128)}, f32[2,64,256]{2,1,0:T(8,128)}) custom-call(f32[2,64,32,256]{3,2,1,0:T(8,128)} %get-tuple-element.88.refs_0_, f32[8,72,256]{2,1,0:T(8,128)S(1)} %shard_map.92.refs_1_.refs_3_, f32[8,72,256]{2,1,0:T(8,128)S(1)} %collective-permute-done.31.refs_2_, ...), custom_call_target="tpu_custom_call", output_to_operand_aliasing={{0}: (0, {})} | custom-call | flops 10000000000 | bytes 1024 | tf_op jit(solution)/shard_map/pallas_call | solution.py:152
  (35 shorter events, 0.6 us)
Async XLA Ops:
  6.2 4.3 %collective-permute-start = (f32[8,136,256]{2,1,0:T(8,128)S(1)}, f32[8,136,256]{2,1,0:T(8,128)S(1)}, u32[]{:S(2)}, u32[]{:S(2)}) collective-permute-start(f32[8,136,256]{2,1,0:T(8,128)S(1)} %get-tuple-element.48), channel_id=1, source_target_pairs={{0,1},{1,0},{2,3},{3,2},{4,5},{5,4},{6,7},{7,6},{8,9},{9,8},{10,11... | collective-permute-start | bytes 3342344 | tf_op jit(solution)/shard_map/ppermute | solution.py:308
  10.4 7.0 %collective-permute-start.2 = (f32[8,128,256]{2,1,0:T(8,128)S(1)}, f32[8,128,256]{2,1,0:T(8,128)S(1)}, u32[]{:S(2)}, u32[]{:S(2)}) collective-permute-start(f32[8,128,256]{2,1,0:T(8,128)S(1)} %get-tuple-element.51.refs_2_), channel_id=1, source_target_pairs={{0,1},{1,0},{2,3},{3,2},{4,5},{5,4},{6,7},{7,6},{8,9},{9,8},{10,11... | collective-permute-start | bytes 3145736 | tf_op jit(solution)/shard_map/ppermute | solution.py:308
  10.6 10.5 %collective-permute-start.1 = (f32[4,136,256]{2,1,0:T(8,128)S(1)}, f32[4,136,256]{2,1,0:T(8,128)S(1)}, u32[]{:S(2)}, u32[]{:S(2)}) collective-permute-start(f32[4,136,256]{2,1,0:T(8,128)S(1)} %get-tuple-element.53.refs_2_), channel_id=1, source_target_pairs={{0,2},{1,5},{2,0},{3,7},{4,6},{5,1},{6,4},{7,3},{8,10},{9,13},{10,... | collective-permute-start | bytes 1671176 | tf_op jit(solution)/shard_map/ppermute | solution.py:308
  17.3 9.8 %collective-permute-start.5 = (f32[8,128,256]{2,1,0:T(8,128)S(1)}, f32[8,128,256]{2,1,0:T(8,128)S(1)}, u32[]{:S(2)}, u32[]{:S(2)}) collective-permute-start(f32[8,128,256]{2,1,0:T(8,128)S(1)} %get-tuple-element.55.refs_2_), channel_id=1, source_target_pairs={{0,1},{1,0},{2,3},{3,2},{4,5},{5,4},{6,7},{7,6},{8,9},{9,8},{10,11... | collective-permute-start | bytes 3145736 | tf_op jit(solution)/shard_map/ppermute | solution.py:308
  17.5 12.2 %collective-permute-start.4 = (f32[4,128,256]{2,1,0:T(8,128)S(1)}, f32[4,128,256]{2,1,0:T(8,128)S(1)}, u32[]{:S(2)}, u32[]{:S(2)}) collective-permute-start(f32[4,128,256]{2,1,0:T(8,128)S(1)} %get-tuple-element.56.refs_2_), channel_id=1, source_target_pairs={{0,2},{1,5},{2,0},{3,7},{4,6},{5,1},{6,4},{7,3},{8,10},{9,13},{10,... | collective-permute-start | bytes 1572872 | tf_op jit(solution)/shard_map/ppermute | solution.py:308
  21.2 10.7 %collective-permute-start.3 = (f32[2,136,256]{2,1,0:T(8,128)S(1)}, f32[2,136,256]{2,1,0:T(8,128)S(1)}, u32[]{:S(2)}, u32[]{:S(2)}) collective-permute-start(f32[2,136,256]{2,1,0:T(8,128)S(1)} %get-tuple-element.58.refs_2_), channel_id=1, source_target_pairs={{0,4},{1,3},{2,6},{3,1},{4,0},{5,7},{6,2},{7,5},{8,12},{9,11},{10,... | collective-permute-start | bytes 835592 | tf_op jit(solution)/shard_map/ppermute | solution.py:308
  27.0 6.6 %collective-permute-start.9 = (f32[8,128,256]{2,1,0:T(8,128)S(1)}, f32[8,128,256]{2,1,0:T(8,128)S(1)}, u32[]{:S(2)}, u32[]{:S(2)}) collective-permute-start(f32[8,128,256]{2,1,0:T(8,128)S(1)} %get-tuple-element.61.refs_2_), channel_id=1, source_target_pairs={{0,1},{1,0},{2,3},{3,2},{4,5},{5,4},{6,7},{7,6},{8,9},{9,8},{10,11... | collective-permute-start | bytes 3145736 | tf_op jit(solution)/shard_map/ppermute | solution.py:308
  27.2 11.7 %collective-permute-start.8 = (f32[4,128,256]{2,1,0:T(8,128)S(1)}, f32[4,128,256]{2,1,0:T(8,128)S(1)}, u32[]{:S(2)}, u32[]{:S(2)}) collective-permute-start(f32[4,128,256]{2,1,0:T(8,128)S(1)} %get-tuple-element.62.refs_2_), channel_id=1, source_target_pairs={{0,2},{1,5},{2,0},{3,7},{4,6},{5,1},{6,4},{7,3},{8,10},{9,13},{10,... | collective-permute-start | bytes 1572872 | tf_op jit(solution)/shard_map/ppermute | solution.py:308
  29.8 10.6 %collective-permute-start.7 = (f32[2,128,256]{2,1,0:T(8,128)S(1)}, f32[2,128,256]{2,1,0:T(8,128)S(1)}, u32[]{:S(2)}, u32[]{:S(2)}) collective-permute-start(f32[2,128,256]{2,1,0:T(8,128)S(1)} %get-tuple-element.63.refs_2_), channel_id=1, source_target_pairs={{0,4},{1,3},{2,6},{3,1},{4,0},{5,7},{6,2},{7,5},{8,12},{9,11},{10,... | collective-permute-start | bytes 786440 | tf_op jit(solution)/shard_map/ppermute | solution.py:308
  32.0 10.1 %collective-permute-start.6 = (f32[1,136,256]{2,1,0:T(8,128)S(1)}, f32[1,136,256]{2,1,0:T(8,128)S(1)}, u32[]{:S(2)}, u32[]{:S(2)}) collective-permute-start(f32[1,136,256]{2,1,0:T(8,128)S(1)} %get-tuple-element.65.refs_2_), channel_id=1, source_target_pairs={{0,8},{1,9},{2,10},{3,11},{4,12},{5,13},{6,14},{7,15},{8,0},{9,1},... | collective-permute-start | bytes 417800 | tf_op jit(solution)/shard_map/ppermute | solution.py:308
  33.7 13.7 %collective-permute-start.13 = (f32[4,128,256]{2,1,0:T(8,128)S(1)}, f32[4,128,256]{2,1,0:T(8,128)S(1)}, u32[]{:S(2)}, u32[]{:S(2)}) collective-permute-start(f32[4,128,256]{2,1,0:T(8,128)S(1)} %get-tuple-element.69.refs_2_), channel_id=1, source_target_pairs={{0,2},{1,5},{2,0},{3,7},{4,6},{5,1},{6,4},{7,3},{8,10},{9,13},{10,... | collective-permute-start | bytes 1572872 | tf_op jit(solution)/shard_map/ppermute | solution.py:308
  39.0 8.4 %collective-permute-start.12 = (f32[2,128,256]{2,1,0:T(8,128)S(1)}, f32[2,128,256]{2,1,0:T(8,128)S(1)}, u32[]{:S(2)}, u32[]{:S(2)}) collective-permute-start(f32[2,128,256]{2,1,0:T(8,128)S(1)} %get-tuple-element.70.refs_2_), channel_id=1, source_target_pairs={{0,4},{1,3},{2,6},{3,1},{4,0},{5,7},{6,2},{7,5},{8,12},{9,11},{10,... | collective-permute-start | bytes 786440 | tf_op jit(solution)/shard_map/ppermute | solution.py:308
  40.4 7.1 %collective-permute-start.11 = (f32[1,128,256]{2,1,0:T(8,128)S(1)}, f32[1,128,256]{2,1,0:T(8,128)S(1)}, u32[]{:S(2)}, u32[]{:S(2)}) collective-permute-start(f32[1,128,256]{2,1,0:T(8,128)S(1)} %get-tuple-element.71.refs_2_), channel_id=1, source_target_pairs={{0,8},{1,9},{2,10},{3,11},{4,12},{5,13},{6,14},{7,15},{8,0},{9,1},... | collective-permute-start | bytes 393224 | tf_op jit(solution)/shard_map/ppermute | solution.py:308
  42.1 11.0 %collective-permute-start.10 = (f32[1,136,256]{2,1,0:T(8,128)S(1)}, f32[1,136,256]{2,1,0:T(8,128)S(1)}, u32[]{:S(2)}, u32[]{:S(2)}) collective-permute-start(f32[1,136,256]{2,1,0:T(8,128)S(1)} %shard_map.72.refs_2_.refs_0_), channel_id=1, source_target_pairs={{0,16},{1,17},{2,18},{3,19},{4,20},{5,21},{6,22},{7,23},{8,24},{9,... | collective-permute-start | bytes 417800 | tf_op jit(solution)/shard_map/ppermute | solution.py:308
  47.5 8.9 %collective-permute-start.14 = (f32[1,128,256]{2,1,0:T(8,128)S(1)}, f32[1,128,256]{2,1,0:T(8,128)S(1)}, u32[]{:S(2)}, u32[]{:S(2)}) collective-permute-start(f32[1,128,256]{2,1,0:T(8,128)S(1)} %shard_map.75.refs_2_.refs_4_), channel_id=1, source_target_pairs={{0,16},{1,17},{2,18},{3,19},{4,20},{5,21},{6,22},{7,23},{8,24},{9,... | collective-permute-start | bytes 393224 | tf_op jit(solution)/shard_map/ppermute | solution.py:308
  50.3 6.4 %collective-permute-start.17 = (f32[2,128,256]{2,1,0:T(8,128)S(1)}, f32[2,128,256]{2,1,0:T(8,128)S(1)}, u32[]{:S(2)}, u32[]{:S(2)}) collective-permute-start(f32[2,128,256]{2,1,0:T(8,128)S(1)} %get-tuple-element.75.refs_2_), channel_id=1, source_target_pairs={{0,4},{1,3},{2,6},{3,1},{4,0},{5,7},{6,2},{7,5},{8,12},{9,11},{10,... | collective-permute-start | bytes 786440 | tf_op jit(solution)/shard_map/ppermute | solution.py:308
  51.4 7.4 %collective-permute-start.16 = (f32[1,128,256]{2,1,0:T(8,128)S(1)}, f32[1,128,256]{2,1,0:T(8,128)S(1)}, u32[]{:S(2)}, u32[]{:S(2)}) collective-permute-start(f32[1,128,256]{2,1,0:T(8,128)S(1)} %get-tuple-element.76.refs_2_), channel_id=1, source_target_pairs={{0,8},{1,9},{2,10},{3,11},{4,12},{5,13},{6,14},{7,15},{8,0},{9,1},... | collective-permute-start | bytes 393224 | tf_op jit(solution)/shard_map/ppermute | solution.py:308
  56.6 8.6 %collective-permute-start.15 = (f32[1,128,256]{2,1,0:T(8,128)S(1)}, f32[1,128,256]{2,1,0:T(8,128)S(1)}, u32[]{:S(2)}, u32[]{:S(2)}) collective-permute-start(f32[1,128,256]{2,1,0:T(8,128)S(1)} %get-tuple-element.77.refs_0_), channel_id=1, source_target_pairs={{0,8},{1,9},{2,10},{3,11},{4,12},{5,13},{6,14},{7,15},{8,0},{9,1},... | collective-permute-start | bytes 393224 | tf_op jit(solution)/shard_map/ppermute | solution.py:308
  56.7 11.8 %collective-permute-start.19 = (f32[1,128,256]{2,1,0:T(8,128)S(1)}, f32[1,128,256]{2,1,0:T(8,128)S(1)}, u32[]{:S(2)}, u32[]{:S(2)}) collective-permute-start(f32[1,128,256]{2,1,0:T(8,128)S(1)} %get-tuple-element.81.refs_2_), channel_id=1, source_target_pairs={{0,8},{1,9},{2,10},{3,11},{4,12},{5,13},{6,14},{7,15},{8,0},{9,1},... | collective-permute-start | bytes 393224 | tf_op jit(solution)/shard_map/ppermute | solution.py:308
  58.8 7.1 %collective-permute-start.20 = (f32[1,128,256]{2,1,0:T(8,128)S(1)}, f32[1,128,256]{2,1,0:T(8,128)S(1)}, u32[]{:S(2)}, u32[]{:S(2)}) collective-permute-start(f32[1,128,256]{2,1,0:T(8,128)S(1)} %shard_map.78.refs_2_.refs_0_), channel_id=1, source_target_pairs={{0,16},{1,17},{2,18},{3,19},{4,20},{5,21},{6,22},{7,23},{8,24},{9,... | collective-permute-start | bytes 393224 | tf_op jit(solution)/shard_map/ppermute | solution.py:308
  65.2 8.4 %collective-permute-start.18 = (f32[2,128,256]{2,1,0:T(8,128)S(1)}, f32[2,128,256]{2,1,0:T(8,128)S(1)}, u32[]{:S(2)}, u32[]{:S(2)}) collective-permute-start(f32[2,128,256]{2,1,0:T(8,128)S(1)} %shard_map.79.refs_4_.refs_0_), channel_id=1, source_target_pairs={{0,4},{1,3},{2,6},{3,1},{4,0},{5,7},{6,2},{7,5},{8,12},{9,11},{10,... | collective-permute-start | bytes 786440 | tf_op jit(solution)/shard_map/ppermute | solution.py:308
  66.0 7.7 %collective-permute-start.23 = (f32[1,64,256]{2,1,0:T(8,128)S(1)}, f32[1,64,256]{2,1,0:T(8,128)S(1)}, u32[]{:S(2)}, u32[]{:S(2)}) collective-permute-start(f32[1,64,256]{2,1,0:T(8,128)S(1)} %get-tuple-element.85.refs_0_), channel_id=1, source_target_pairs={{0,8},{1,9},{2,10},{3,11},{4,12},{5,13},{6,14},{7,15},{8,0},{9,1},... | collective-permute-start | bytes 196616 | tf_op jit(solution)/shard_map/ppermute | solution.py:308
  68.6 7.0 %collective-permute-start.22 = (f32[1,128,256]{2,1,0:T(8,128)S(1)}, f32[1,128,256]{2,1,0:T(8,128)S(1)}, u32[]{:S(2)}, u32[]{:S(2)}) collective-permute-start(f32[1,128,256]{2,1,0:T(8,128)S(1)} %shard_map.81.refs_2_.refs_0_), channel_id=1, source_target_pairs={{0,16},{1,17},{2,18},{3,19},{4,20},{5,21},{6,22},{7,23},{8,24},{9,... | collective-permute-start | bytes 393224 | tf_op jit(solution)/shard_map/ppermute | solution.py:308
  73.6 9.2 %collective-permute-start.21 = (f32[4,128,256]{2,1,0:T(8,128)S(1)}, f32[4,128,256]{2,1,0:T(8,128)S(1)}, u32[]{:S(2)}, u32[]{:S(2)}) collective-permute-start(f32[4,128,256]{2,1,0:T(8,128)S(1)} %shard_map.82.refs_2_.refs_0_), channel_id=1, source_target_pairs={{0,2},{1,5},{2,0},{3,7},{4,6},{5,1},{6,4},{7,3},{8,10},{9,13},{10,... | collective-permute-start | bytes 1572872 | tf_op jit(solution)/shard_map/ppermute | solution.py:308
  73.7 9.3 %collective-permute-start.26 = (f32[2,64,256]{2,1,0:T(8,128)S(1)}, f32[2,64,256]{2,1,0:T(8,128)S(1)}, u32[]{:S(2)}, u32[]{:S(2)}) collective-permute-start(f32[2,64,256]{2,1,0:T(8,128)S(1)} %shard_map.83.refs_4_.refs_0_), channel_id=1, source_target_pairs={{0,4},{1,3},{2,6},{3,1},{4,0},{5,7},{6,2},{7,5},{8,12},{9,11},{10,... | collective-permute-start | bytes 393224 | tf_op jit(solution)/shard_map/ppermute | solution.py:308
  75.7 7.5 %collective-permute-start.25 = (f32[1,72,256]{2,1,0:T(8,128)S(1)}, f32[1,72,256]{2,1,0:T(8,128)S(1)}, u32[]{:S(2)}, u32[]{:S(2)}) collective-permute-start(f32[1,72,256]{2,1,0:T(8,128)S(1)} %shard_map.84.refs_2_.refs_0_), channel_id=1, source_target_pairs={{0,8},{1,9},{2,10},{3,11},{4,12},{5,13},{6,14},{7,15},{8,0},{9,1},... | collective-permute-start | bytes 221192 | tf_op jit(solution)/shard_map/ppermute | solution.py:308
  83.0 2.7 %collective-permute-start.24 = (f32[8,128,256]{2,1,0:T(8,128)S(1)}, f32[8,128,256]{2,1,0:T(8,128)S(1)}, u32[]{:S(2)}, u32[]{:S(2)}) collective-permute-start(f32[8,128,256]{2,1,0:T(8,128)S(1)} %shard_map.85.refs_2_.refs_0_), channel_id=1, source_target_pairs={{0,1},{1,0},{2,3},{3,2},{4,5},{5,4},{6,7},{7,6},{8,9},{9,8},{10,11... | collective-permute-start | bytes 3145736 | tf_op jit(solution)/shard_map/ppermute | solution.py:308
  83.1 7.6 %collective-permute-start.27 = (f32[4,64,256]{2,1,0:T(8,128)S(1)}, f32[4,64,256]{2,1,0:T(8,128)S(1)}, u32[]{:S(2)}, u32[]{:S(2)}) collective-permute-start(f32[4,64,256]{2,1,0:T(8,128)S(1)} %shard_map.86.refs_2_.refs_0_), channel_id=1, source_target_pairs={{0,2},{1,5},{2,0},{3,7},{4,6},{5,1},{6,4},{7,3},{8,10},{9,13},{10,... | collective-permute-start | bytes 786440 | tf_op jit(solution)/shard_map/ppermute | solution.py:308
  83.2 7.7 %collective-permute-start.29 = (f32[2,72,256]{2,1,0:T(8,128)S(1)}, f32[2,72,256]{2,1,0:T(8,128)S(1)}, u32[]{:S(2)}, u32[]{:S(2)}) collective-permute-start(f32[2,72,256]{2,1,0:T(8,128)S(1)} %shard_map.87.refs_2_.refs_0_), channel_id=1, source_target_pairs={{0,4},{1,3},{2,6},{3,1},{4,0},{5,7},{6,2},{7,5},{8,12},{9,11},{10,... | collective-permute-start | bytes 442376 | tf_op jit(solution)/shard_map/ppermute | solution.py:308
  90.8 2.0 %collective-permute-start.28 = (f32[8,64,256]{2,1,0:T(8,128)S(1)}, f32[8,64,256]{2,1,0:T(8,128)S(1)}, u32[]{:S(2)}, u32[]{:S(2)}) collective-permute-start(f32[8,64,256]{2,1,0:T(8,128)S(1)} %shard_map.89.refs_2_.refs_1_), channel_id=1, source_target_pairs={{0,1},{1,0},{2,3},{3,2},{4,5},{5,4},{6,7},{7,6},{8,9},{9,8},{10,11... | collective-permute-start | bytes 1572872 | tf_op jit(solution)/shard_map/ppermute | solution.py:308
  90.9 6.8 %collective-permute-start.30 = (f32[4,72,256]{2,1,0:T(8,128)S(1)}, f32[4,72,256]{2,1,0:T(8,128)S(1)}, u32[]{:S(2)}, u32[]{:S(2)}) collective-permute-start(f32[4,72,256]{2,1,0:T(8,128)S(1)} %shard_map.90.refs_3_.refs_0_), channel_id=1, source_target_pairs={{0,2},{1,5},{2,0},{3,7},{4,6},{5,1},{6,4},{7,3},{8,10},{9,13},{10,... | collective-permute-start | bytes 884744 | tf_op jit(solution)/shard_map/ppermute | solution.py:308
  97.7 2.1 %collective-permute-start.31 = (f32[8,72,256]{2,1,0:T(8,128)S(1)}, f32[8,72,256]{2,1,0:T(8,128)S(1)}, u32[]{:S(2)}, u32[]{:S(2)}) collective-permute-start(f32[8,72,256]{2,1,0:T(8,128)S(1)} %shard_map.92.refs_1_.refs_3_), channel_id=1, source_target_pairs={{0,1},{1,0},{2,3},{3,2},{4,5},{5,4},{6,7},{7,6},{8,9},{9,8},{10,11... | collective-permute-start | bytes 1769480 | tf_op jit(solution)/shard_map/ppermute | solution.py:308

commit v3 on v2

--- a/solution.py
+++ b/solution.py
@@ -15,8 +15,11 @@
 EXTRA = 8
 VMEM_LIMIT = 48 * 2**20
 SIZES = [2, 2, 2, 2]
-BUNDLES = [[0], [1], [2], [3]]
-BATCHES = [[0, 1], [2], [3]]
+BATCHES = [[0], [1], [2], [3]]
+HALVE = [('xyz', 'yxz'), ('zxy', 'xyz'), ('zxy', 'yzx'), ('xzy', 'yxz')]
+GATHER = [('xyz', 'zxy'), ('xzy', 'yzx'), ('xzy', 'zyx'), ('xzy', 'zyx')]
+ORDER = [('K', 0), ('K', 1), ('S', 0, 0), ('S', 1, 0), ('K', 2), ('S', 0, 1), ('S', 2, 0), ('K', 3), ('S', 1, 1), ('S', 0, 2), ('S', 3, 0), ('S', 2, 1), ('S', 1, 2), ('S', 0, 3), ('S', 3, 1), ('S', 1, 3), ('S', 2, 2), ('S', 3, 2), ('S', 2, 3), ('R', 0), ('S', 3, 3), ('R', 1), ('G', 0, 2), ('G', 1, 2), ('R', 2), ('G', 0, 1), ('G', 2, 2), ('R', 3), ('G', 1, 1), ('G', 3, 2), ('G', 2, 1), ('G', 1, 0), ('G', 3, 1), ('G', 0, 0), ('G', 2, 0), ('P', 0), ('P', 1), ('G', 3, 0), ('P', 2), ('P', 3)]
+FLIP = {"x": 2, "y": 4, "z": 8}
 
 
 class Plan:
@@ -27,41 +30,51 @@
         self.unit = self.items = devices // 4
         self.units = B // self.unit
         assert self.units >= 1
-        self.stages = [(2, 4), (4, 2)] + [(1 << b, 1 << b) for b in range(3, bits - 1)]
-
-    def partner(self, stage, device):
-        return device ^ self.stages[stage][device & 1]
-
-    def mask(self, item, core):
-        total = 0
-        for i, (even, odd) in enumerate(reversed(self.stages)):
-            total = total ^ (((item >> i) & 1) * (even + core * (odd - even)))
-        return total
-
-    def low_bin(self, device, item):
-        return ((device ^ self.mask(item, device & 1)) >> 1) & (self.unit - 1)
-
-    def mirrored(self, item):
-        at = len(self.stages) - 2
-        differ = ((item >> at) ^ (item >> (at + 1))) & 1
-        return item ^ (differ * (3 << at))
-
-    def sizes(self):
-        if self.units == 8:
-            return SIZES, BUNDLES, BATCHES
-        return [self.units], [[0]], [[0]]
-
-
-def hist_body(plan, first_unit, count, has_totals, bins, spread, keep, send):
+        self.n_stages = bits - 2
+        if devices == 32 and self.units == sum(SIZES):
+            self.sizes, self.batches, self.order = SIZES, BATCHES, ORDER
+            self.halve = [self.paths(*pair) for pair in HALVE]
+            self.gather = [self.paths(*pair) for pair in GATHER]
+        else:
+            self.sizes, self.batches, self.order = [self.units], [[0]], []
+            later = [(1 << b, 1 << b) for b in range(3, bits - 1)]
+            self.halve = self.gather = [[(2, 4), (4, 2), *later]]
+
+    def paths(self, even, odd):
+        return [(FLIP[e], FLIP[o]) for e, o in zip(even, odd, strict=True)]
+
+
+def mask(path, item, core):
+    total = 0
+    for i, (even, odd) in enumerate(reversed(path)):
+        total = total ^ (((item >> i) & 1) * (even + core * (odd - even)))
+    return total
+
+
+def low_bin(path, device, item):
+    return ((device ^ mask(path, item, device & 1)) >> 1) & ((1 << len(path)) - 1)
+
+
+def mirrored(path, item, core):
+    even, odd = ([stage[c] for stage in reversed(path)] for c in (0, 1))
+    total = 0
+    for i in range(len(path)):
+        on_even, on_odd = 1 << odd.index(even[i]), 1 << even.index(odd[i])
+        total = total ^ (((item >> i) & 1) * (on_even + core * (on_odd - on_even)))
+    return total
+
+
+def hist_body(plan, path, first_unit, count, has_totals, bins, spread, keep, send):
     me = lax.axis_index("dp")
     rows = bins.shape[0]
     step = min(rows, 256)
 
     @pl.loop(0, plan.items)
     def _(item):
-        low_bin = plan.low_bin(me, item)
+        own = low_bin(path, me, item)
+        theirs = mirrored(path, item, me & 1)
         for u in range(count):
-            level = (first_unit + u) * plan.unit + low_bin
+            level = (first_unit + u) * plan.unit + own
             level = level.astype(jnp.float32).astype(jnp.bfloat16)
             total = jnp.zeros((spread.shape[0], bins.shape[1]), jnp.float32)
             for start in range(0, rows, step):
@@ -73,7 +86,7 @@
                 )
             at = pl.ds(u * 2 * K, 2 * K)
             keep[item, at, :] = total[: 2 * K, :]
-            send[plan.mirrored(item), at, :] = total[2 * K :, :]
+            send[theirs, at, :] = total[2 * K :, :]
 
     if has_totals:
         sums = jnp.sum(spread[...].astype(jnp.float32), axis=1, keepdims=True)
@@ -87,7 +100,7 @@
                 target[item, pl.ds(count * 2 * K, EXTRA), :] = packed
 
 
-def first_kernel(plan, count, blocks, *refs):
+def first_kernel(plan, path, count, blocks, *refs):
     bins_in, node_in, grad_in, hess_in, keep, send, bins, spread = refs[:8]
     raw, node, paired, sems = refs[8:]
     me = lax.axis_index("dp")
@@ -118,11 +131,11 @@
         copy.wait()
         at = slice(i * step, (i + 1) * step)
         bins[at, :] = raw[at, :].astype(jnp.float32).astype(jnp.bfloat16)
-    hist_body(plan, 0, count, True, bins, spread, keep, send)
-
-
-def next_kernel(plan, first_unit, count, bins, spread, keep, send):
-    hist_body(plan, first_unit, count, False, bins, spread, keep, send)
+    hist_body(plan, path, 0, count, True, bins, spread, keep, send)
+
+
+def next_kernel(plan, path, first_unit, count, bins, spread, keep, send):
+    hist_body(plan, path, first_unit, count, False, bins, spread, keep, send)
 
 
 class Chain:
@@ -130,7 +143,7 @@
         self.last = None
 
     def __call__(
-        self, body, out_shape, operands, flops=0, moved=0, in_place=None, out_place=None, **more
+        self, body, out_shape, operands, flops=10**10, in_place=None, out_place=None, **more
     ):
         n = len(operands)
         spec = {
@@ -155,7 +168,7 @@
             in_specs=in_specs,
             out_specs=out_specs,
             compiler_params=pltpu.CompilerParams(vmem_limit_bytes=VMEM_LIMIT),
-            cost_estimate=pl.CostEstimate(flops=10**10, bytes_accessed=1024, transcendentals=0),
+            cost_estimate=pl.CostEstimate(flops=flops, bytes_accessed=1024, transcendentals=0),
             **more,
         )(*operands)
         self.last = outs[-1]
@@ -248,7 +261,7 @@
         gains[...] = gain_rows
 
 
-def place_body(plan, first_unit, count, last, first, *refs):
+def place_body(plan, path, first_unit, count, last, first, *refs):
     if not first:
         refs = refs[1:]
     mine, theirs, weights = refs[:3]
@@ -269,11 +282,11 @@
             fetch.start()
             fetched.append(fetch)
         for item in range(plan.items):
-            low_bin = plan.low_bin(who, item)
+            own = low_bin(path, who, item)
             for u in range(count):
                 copy = pltpu.make_async_copy(
                     source.at[item, pl.ds(u * K, K), :],
-                    weights.at[who & 1, (first_unit + u) * plan.unit + low_bin],
+                    weights.at[who & 1, (first_unit + u) * plan.unit + own],
                     sems.at[(side * plan.items + item) * count + u],
                 )
                 copy.start()
@@ -284,9 +297,9 @@
         for side in range(2):
             who = me ^ side
             for item in range(plan.items):
-                low_bin = plan.low_bin(who, item)
+                own = low_bin(path, who, item)
                 for u in range(plan.units):
-                    line = pl.ds(u * plan.unit + low_bin, 1)
+                    line = pl.ds(u * plan.unit + own, 1)
                     for h in range(lines.shape[0]):
                         lines[h, who & 1, line, :] = held[
                             side, item, u : u + 1, h * LANES : (h + 1) * LANES
@@ -308,7 +321,7 @@
         return lax.ppermute(x, "dp", [(d, partner(d)) for d in range(devices)])
 
     def swap_stage(x, stage):
-        return swap(x, functools.partial(plan.partner, stage))
+        return swap(x, lambda d: d ^ stage[d & 1])
 
     def swap_cores(x):
         return swap(x, lambda d: d ^ 1)
@@ -316,20 +329,19 @@
     def swap_top(x):
         return swap(x, lambda d: d ^ plan.top)
 
-    sizes, bundles, batches = plan.sizes()
+    sizes, batches = plan.sizes, plan.batches
     starts = [sum(sizes[:i]) for i in range(len(sizes))]
-    n_stages = len(plan.stages)
+    n_stages = plan.n_stages
     got = {}
     shared = {}
 
     def depth(chunk):
         return sizes[chunk] * 2 * K + (EXTRA if chunk == 0 else 0)
 
-    def add(parts, groups):
-        height = sum(p.shape[1] for p, _ in parts)
-        items = parts[0][0].shape[0] // groups
+    def add(pair, n_outs):
+        items, height, _ = pair[0].shape
         return chain(
-            functools.partial(add_body, groups), [f32(items, height, features)] * groups, sum(parts, [])
+            functools.partial(add_body, n_outs), [f32(items // n_outs, height, features)] * n_outs, pair
         )
 
     def histogram(c):
@@ -337,7 +349,7 @@
         if c == 0:
             blocks = 8
             keep, send, bins, spread = chain(
-                functools.partial(first_kernel, plan, sizes[c], blocks),
+                functools.partial(first_kernel, plan, plan.halve[c], sizes[c], blocks),
                 [
                     *halves,
                     jax.ShapeDtypeStruct((rows, features), jnp.bfloat16),
@@ -358,34 +370,27 @@
             shared["data"] = (bins, spread)
         else:
             keep, send = chain(
-                functools.partial(next_kernel, plan, starts[c], sizes[c]), halves, shared["data"]
+                functools.partial(next_kernel, plan, plan.halve[c], starts[c], sizes[c]),
+                halves,
+                shared["data"],
+                flops=10**10,
             )
-        got["C", c] = [keep, swap_cores(send)]
-
-    def over_cores(c):
-        mine, other = add([got["C", c]], 2)
-        got["S", c] = [mine, swap_stage(other, 0)]
-
-    def over_first(c):
-        mine, other = add([got["S", c]], 2)
-        got["T", c] = [mine, swap_stage(other, 1)]
-
-    def over_next(b, stage):
-        parts = [got["T", c] for c in bundles[b]] if stage == 2 else [got["Z", b]]
+        got[c] = [keep, swap_cores(send)]
+
+    def reduce(c, stage):
         if stage < n_stages:
-            mine, other = add(parts, 2)
-            got["Z", b] = [mine, swap_stage(other, stage)]
+            mine, other = add(got[c], 2)
+            got[c] = [mine, swap_stage(other, plan.halve[c][stage])]
         else:
-            (mine,) = add(parts, 1)
-            got["Z", b] = [mine, swap_top(mine)]
+            (mine,) = add(got[c], 1)
+            got[c] = [mine, swap_top(mine)]
 
     def curves(g):
-        batch = batches[g]
-        chunks = [c for b in batch for c in bundles[b]]
+        chunks = batches[g]
         count = sum(sizes[c] for c in chunks)
         last = g == len(batches) - 1
-        parts = sum((got["Z", b] for b in batch), [])
-        n_parts = [(len(got["Z", b]), bundles[b]) for b in batch]
+        parts = sum((got[c] for c in chunks), [])
+        n_parts = [(2, [c]) for c in chunks]
         outs = [f32(1, count * K + (EXTRA if last else 0), features)]
         if not last:
             outs += [f32(EXTRA, features)] * (2 if g == 0 else 1)
@@ -399,16 +404,19 @@
             shared["gains"] = outs[-1]
             if g == 0:
                 shared["totals"] = outs[1]
-        got["G", g] = [outs[0], swap_stage(outs[0], n_stages - 1)]
+        got["G", g] = [outs[0], swap_stage(outs[0], plan.gather[g][-1])]
 
     def gather(g, stage):
         parts = got["G", g]
         items, height, _ = parts[0].shape
         (joined,) = chain(join_body, [f32(2 * items, height, features)], parts)
-        got["G", g] = [joined, swap_stage(joined, stage - 1) if stage else swap_cores(joined)]
+        if stage:
+            got["G", g] = [joined, swap_stage(joined, plan.gather[g][stage - 1])]
+        else:
+            got["G", g] = [joined, swap_cores(joined)]
 
     def place(g):
-        chunks = [c for b in batches[g] for c in bundles[b]]
+        chunks = batches[g]
         count = sum(sizes[c] for c in chunks)
         last = g == len(batches) - 1
         out_shape = [f32(NODES, B, K, features), f32(EXTRA, LANES)]
@@ -424,7 +432,7 @@
         buffer = [] if g == 0 else [shared["weights"]]
         operands = [*buffer, *got["G", g]]
         shared["weights"], shared["gains_out"] = chain(
-            functools.partial(place_body, plan, starts[chunks[0]], count, last, g == 0),
+            functools.partial(place_body, plan, plan.gather[g], starts[chunks[0]], count, last, g == 0),
             out_shape,
             operands,
             in_place=[None] * len(buffer) + [False] * 2,
@@ -435,18 +443,18 @@
 
     tasks = []
     for c in range(len(sizes)):
-        tasks += [(c - 0.2, histogram, c), (c + 0.9, over_cores, c), (c + 2, over_first, c)]
-    for b, bundle in enumerate(bundles):
-        for stage in range(2, n_stages + 1):
-            tasks.append((bundle[-1] + 1 + stage + 0.02 * stage, over_next, b, stage))
-    for g, batch in enumerate(batches):
-        at = bundles[batch[-1]][-1] + n_stages + 2.1 - (0.5 if g < len(batches) - 1 else 0)
-        tasks.append((at, curves, g))
+        tasks.append((c - 0.2, ("K", c)))
+        for stage in range(n_stages + 1):
+            tasks.append((c + 1 + 1.02 * stage, ("S", c, stage)))
+    for g, chunks in enumerate(batches):
+        at = chunks[-1] + n_stages + 2.1 - (0.5 if g < len(batches) - 1 else 0)
+        tasks.append((at, ("R", g)))
         for i, stage in enumerate(reversed(range(n_stages))):
-            tasks.append((at + 1 + i, gather, g, stage))
-        tasks.append((at + 1 + n_stages, place, g))
-    for _, task, *arguments in sorted(tasks, key=lambda t: t[0]):
-        task(*arguments)
+            tasks.append((at + 1 + i, ("G", g, stage)))
+        tasks.append((at + 1 + n_stages, ("P", g)))
+    kinds = {"K": histogram, "S": reduce, "R": curves, "G": gather, "P": place}
+    for name, *arguments in plan.order or [task for _, task in sorted(tasks, key=lambda t: t[0])]:
+        kinds[name](*arguments)
     return shared["gains_out"].transpose(2, 0, 1), shared["weights"].transpose(3, 0, 1, 2)
 
 

time: 102 us -> 92.4 us (0.906)
  waiting for transfers between devices: 43.2 us -> 26 us
  starting transfers between devices: 34.5 us -> 41.5 us
    ppermute x32 -> x36, waiting for transfers between devices: 43.2 us -> 26 us  [swap(): return lax.ppermute(x, 'dp', [(d, partner(d)) for d in range(devices)])]
    ppermute x32 -> x36, starting transfers between devices: 34.5 us -> 41.5 us  [swap(): return lax.ppermute(x, 'dp', [(d, partner(d)) for d in range(devices)])]
    pallas_call x35 -> x40, Pallas kernels: 23 us -> 23.7 us  [__call__(): pl.pallas_call(run, out_shape=out_shape, in_specs=in_specs, out_specs=out...]
  transfers between devices with their start and end apart: 32 -> 36, of which waited for: 16 -> 15; matrix products, arithmetic and copies ran while one was open for 0% -> 0% of each run, Pallas kernels for 15% -> 18%
where the time goes in v3:
time: 92.4 us; the launch traced here: 92.2 us
  starting transfers between devices  41.5 us (45%)
  waiting for transfers between devices  26 us (28%)
  Pallas kernels  23.7 us (26%)
  between operations  0.95 us (1%)
    ppermute x36, starting transfers between devices, swap(): return lax.ppermute(x, 'dp', [(d, partner(d)) for d in range(devices)])  41.5 us
    ppermute x36, waiting for transfers between devices, swap(): return lax.ppermute(x, 'dp', [(d, partner(d)) for d in range(devices)])  26 us
    pallas_call x40, Pallas kernels, __call__(): pl.pallas_call(run, out_shape=out_shape, in_specs=in_specs, out_specs=out...  23.7 us
  transfers between devices with their start and end apart: 36, of which 15 were waited for; matrix products, arithmetic and copies ran while one was open for 0% of the time, Pallas kernels for 18%

profile of v3, /device:TPU:0, one launch (start us, length us, event | category | flops | bytes accessed | tf_op | source)
XLA Modules:
  0.0 92.2 jit_solution(3565852387977209461)
XLA Ops:
  0.6 5.5 %shard_map.59 = (f32[8,136,256]{2,1,0:T(8,128)S(1)}, f32[8,136,256]{2,1,0:T(8,128)S(1)}, bf16[2048,256]{1,0:T(8,128)(2,1)S(1)}, bf16[128,2048]{1,0:T(8,128)(2,1)S(1)}) custom-call(s32[2048,256]{1,0:T(8,128)} %refs_0_.1, s32[1,2048]{1,0:T(1,128)} %bitcast.7, bf16[32,2048]{1,0:T(8,128)(2,1)} %bitcast.5, bf16[32,2048]{1,0:T(8,128)(2,1)} %bitcast.6), custom_call_target="tpu_custom_call" | custom-call | flops 10000000000 | bytes 1024 | tf_op jit(solution)/shard_map/pallas_call | solution.py:165
  6.2 0.6 collective-permute-start
  6.7 3.7 %shard_map.60 = (f32[8,128,256]{2,1,0:T(8,128)S(1)}, f32[8,128,256]{2,1,0:T(8,128)S(1)}) custom-call(bf16[2048,256]{1,0:T(8,128)(2,1)S(1)} %get-tuple-element.53.refs_0_, bf16[128,2048]{1,0:T(8,128)(2,1)S(1)} %get-tuple-element.54.refs_1_.refs_2_, bf16[128,2048]{1,0:T(8,128)(2,1)S(1)} %get-tuple-element.54.refs_1_.refs_2_), custom_call_target="tpu_custom_call" | custom-call | flops 10000000000 | bytes 1024 | tf_op jit(solution)/shard_map/pallas_call | solution.py:165
  10.4 0.1 collective-permute-start.2
  10.5 0.1 shard_map.61
  10.6 3.0 %collective-permute-start.1 = (f32[4,136,256]{2,1,0:T(8,128)S(1)}, f32[4,136,256]{2,1,0:T(8,128)S(1)}, u32[]{:S(2)}, u32[]{:S(2)}) collective-permute-start(f32[4,136,256]{2,1,0:T(8,128)S(1)} %get-tuple-element.57.refs_2_), channel_id=1, source_target_pairs={{0,2},{1,5},{2,0},{3,7},{4,6},{5,1},{6,4},{7,3},{8,10},{9,13},{10,... | collective-permute-start | bytes 1671176 | tf_op jit(solution)/shard_map/ppermute | solution.py:321
  13.6 0.1 shard_map.62
  13.8 3.7 %shard_map.63 = (f32[8,128,256]{2,1,0:T(8,128)S(1)}, f32[8,128,256]{2,1,0:T(8,128)S(1)}) custom-call(bf16[2048,256]{1,0:T(8,128)(2,1)S(1)} %get-tuple-element.53.refs_0_, bf16[128,2048]{1,0:T(8,128)(2,1)S(1)} %get-tuple-element.54.refs_1_.refs_2_, f32[4,128,256]{2,1,0:T(8,128)S(1)} %get-tuple-element.59.refs_2_), custom_call_target="tpu_custom_call" | custom-call | flops 10000000000 | bytes 1024 | tf_op jit(solution)/shard_map/pallas_call | solution.py:165
  17.4 0.1 collective-permute-start.5
  17.5 2.5 %collective-permute-start.4 = (f32[4,128,256]{2,1,0:T(8,128)S(1)}, f32[4,128,256]{2,1,0:T(8,128)S(1)}, u32[]{:S(2)}, u32[]{:S(2)}) collective-permute-start(f32[4,128,256]{2,1,0:T(8,128)S(1)} %get-tuple-element.59.refs_2_), channel_id=1, source_target_pairs={{0,8},{1,3},{2,10},{3,1},{4,12},{5,7},{6,14},{7,5},{8,0},{9,11},{1... | collective-permute-start | bytes 1572872 | tf_op jit(solution)/shard_map/ppermute | solution.py:321
  20.0 1.2 %collective-permute-done.1.refs_1_ = f32[4,136,256]{2,1,0:T(8,128)S(1)} collective-permute-done((f32[4,136,256]{2,1,0:T(8,128)S(1)}, f32[4,136,256]{2,1,0:T(8,128)S(1)}, u32[]{:S(2)}, u32[]{:S(2)}) %collective-permute-start.1) | collective-permute-done | bytes 557088 | tf_op jit(solution)/shard_map/ppermute | solution.py:321
  21.3 2.4 %collective-permute-start.3 = (f32[2,136,256]{2,1,0:T(8,128)S(1)}, f32[2,136,256]{2,1,0:T(8,128)S(1)}, u32[]{:S(2)}, u32[]{:S(2)}) collective-permute-start(f32[2,136,256]{2,1,0:T(8,128)S(1)} %get-tuple-element.62.refs_2_), channel_id=1, source_target_pairs={{0,4},{1,3},{2,6},{3,1},{4,0},{5,7},{6,2},{7,5},{8,12},{9,11},{10,... | collective-permute-start | bytes 835592 | tf_op jit(solution)/shard_map/ppermute | solution.py:321
  23.7 0.1 shard_map.65
  23.9 1.6 %collective-permute-start.8 = (f32[4,128,256]{2,1,0:T(8,128)S(1)}, f32[4,128,256]{2,1,0:T(8,128)S(1)}, u32[]{:S(2)}, u32[]{:S(2)}) collective-permute-start(f32[4,128,256]{2,1,0:T(8,128)S(1)} %get-tuple-element.65.refs_2_), channel_id=1, source_target_pairs={{0,8},{1,5},{2,10},{3,7},{4,12},{5,1},{6,14},{7,3},{8,0},{9,13},{1... | collective-permute-start | bytes 1572872 | tf_op jit(solution)/shard_map/ppermute | solution.py:321
  25.5 3.7 %shard_map.66 = (f32[8,128,256]{2,1,0:T(8,128)S(1)}, f32[8,128,256]{2,1,0:T(8,128)S(1)}) custom-call(bf16[2048,256]{1,0:T(8,128)(2,1)S(1)} %get-tuple-element.53.refs_0_, bf16[128,2048]{1,0:T(8,128)(2,1)S(1)} %get-tuple-element.54.refs_1_.refs_2_, f32[4,128,256]{2,1,0:T(8,128)S(1)} %get-tuple-element.65.refs_2_), custom_call_target="tpu_custom_call" | custom-call | flops 10000000000 | bytes 1024 | tf_op jit(solution)/shard_map/pallas_call | solution.py:165
  29.3 0.1 shard_map.67
  29.3 1.6 %collective-permute-start.7 = (f32[2,128,256]{2,1,0:T(8,128)S(1)}, f32[2,128,256]{2,1,0:T(8,128)S(1)}, u32[]{:S(2)}, u32[]{:S(2)}) collective-permute-start(f32[2,128,256]{2,1,0:T(8,128)S(1)} %get-tuple-element.67.refs_2_), channel_id=1, source_target_pairs={{0,2},{1,5},{2,0},{3,7},{4,6},{5,1},{6,4},{7,3},{8,10},{9,13},{10,... | collective-permute-start | bytes 786440 | tf_op jit(solution)/shard_map/ppermute | solution.py:321
  30.9 0.3 collective-permute-done.3.refs_1_
  31.3 2.1 %collective-permute-start.6 = (f32[1,136,256]{2,1,0:T(8,128)S(1)}, f32[1,136,256]{2,1,0:T(8,128)S(1)}, u32[]{:S(2)}, u32[]{:S(2)}) collective-permute-start(f32[1,136,256]{2,1,0:T(8,128)S(1)} %get-tuple-element.69.refs_2_), channel_id=1, source_target_pairs={{0,8},{1,9},{2,10},{3,11},{4,12},{5,13},{6,14},{7,15},{8,0},{9,1},... | collective-permute-start | bytes 417800 | tf_op jit(solution)/shard_map/ppermute | solution.py:321
  33.4 0.1 shard_map.69
  33.5 1.7 %collective-permute-start.13 = (f32[4,128,256]{2,1,0:T(8,128)S(1)}, f32[4,128,256]{2,1,0:T(8,128)S(1)}, u32[]{:S(2)}, u32[]{:S(2)}) collective-permute-start(f32[4,128,256]{2,1,0:T(8,128)S(1)} %get-tuple-element.73.refs_2_), channel_id=1, source_target_pairs={{0,2},{1,5},{2,0},{3,7},{4,6},{5,1},{6,4},{7,3},{8,10},{9,13},{10,... | collective-permute-start | bytes 1572872 | tf_op jit(solution)/shard_map/ppermute | solution.py:321
  35.2 0.5 collective-permute-start.11
  35.7 0.1 collective-permute-done.7.refs_1_
  35.8 1.5 %collective-permute-start.12 = (f32[1,128,256]{2,1,0:T(8,128)S(1)}, f32[1,128,256]{2,1,0:T(8,128)S(1)}, u32[]{:S(2)}, u32[]{:S(2)}) collective-permute-start(f32[1,128,256]{2,1,0:T(8,128)S(1)} %get-tuple-element.75.refs_2_), channel_id=1, source_target_pairs={{0,4},{1,9},{2,6},{3,11},{4,0},{5,13},{6,2},{7,15},{8,12},{9,1},{1... | collective-permute-start | bytes 393224 | tf_op jit(solution)/shard_map/ppermute | solution.py:321
  37.4 2.7 %collective-permute-start.10 = (f32[1,136,256]{2,1,0:T(8,128)S(1)}, f32[1,136,256]{2,1,0:T(8,128)S(1)}, u32[]{:S(2)}, u32[]{:S(2)}) collective-permute-start(f32[1,136,256]{2,1,0:T(8,128)S(1)} %shard_map.72.refs_2_.refs_0_), channel_id=1, source_target_pairs={{0,16},{1,17},{2,18},{3,19},{4,20},{5,21},{6,22},{7,23},{8,24},{9,... | collective-permute-start | bytes 417800 | tf_op jit(solution)/shard_map/ppermute | solution.py:321
  40.0 2.7 %collective-permute-done.13.refs_1_ = f32[4,128,256]{2,1,0:T(8,128)S(1)} collective-permute-done((f32[4,128,256]{2,1,0:T(8,128)S(1)}, f32[4,128,256]{2,1,0:T(8,128)S(1)}, u32[]{:S(2)}, u32[]{:S(2)}) %collective-permute-start.13) | collective-permute-done | bytes 524320 | tf_op jit(solution)/shard_map/ppermute | solution.py:321
  42.8 0.1 collective-permute-start.15
  42.9 3.1 %collective-permute-start.17 = (f32[1,128,256]{2,1,0:T(8,128)S(1)}, f32[1,128,256]{2,1,0:T(8,128)S(1)}, u32[]{:S(2)}, u32[]{:S(2)}) collective-permute-start(f32[1,128,256]{2,1,0:T(8,128)S(1)} %shard_map.74.refs_2_.refs_0_), channel_id=1, source_target_pairs={{0,16},{1,17},{2,18},{3,19},{4,20},{5,21},{6,22},{7,23},{8,24},{9,... | collective-permute-start | bytes 393224 | tf_op jit(solution)/shard_map/ppermute | solution.py:321
  46.1 1.5 %collective-permute-start.14 = (f32[1,128,256]{2,1,0:T(8,128)S(1)}, f32[1,128,256]{2,1,0:T(8,128)S(1)}, u32[]{:S(2)}, u32[]{:S(2)}) collective-permute-start(f32[1,128,256]{2,1,0:T(8,128)S(1)} %get-tuple-element.81.refs_2_), channel_id=1, source_target_pairs={{0,4},{1,3},{2,6},{3,1},{4,0},{5,7},{6,2},{7,5},{8,12},{9,11},{10,... | collective-permute-start | bytes 393224 | tf_op jit(solution)/shard_map/ppermute | solution.py:321
  47.6 6.7 %collective-permute-done.15.refs_1_ = f32[2,128,256]{2,1,0:T(8,128)S(1)} collective-permute-done((f32[2,128,256]{2,1,0:T(8,128)S(1)}, f32[2,128,256]{2,1,0:T(8,128)S(1)}, u32[]{:S(2)}, u32[]{:S(2)}) %collective-permute-start.15) | collective-permute-done | bytes 262176 | tf_op jit(solution)/shard_map/ppermute | solution.py:321
  54.3 1.6 %collective-permute-start.18 = (f32[1,128,256]{2,1,0:T(8,128)S(1)}, f32[1,128,256]{2,1,0:T(8,128)S(1)}, u32[]{:S(2)}, u32[]{:S(2)}) collective-permute-start(f32[1,128,256]{2,1,0:T(8,128)S(1)} %get-tuple-element.83.refs_2_), channel_id=1, source_target_pairs={{0,4},{1,9},{2,6},{3,11},{4,0},{5,13},{6,2},{7,15},{8,12},{9,1},{1... | collective-permute-start | bytes 393224 | tf_op jit(solution)/shard_map/ppermute | solution.py:321
  55.9 0.1 collective-permute-start.20
  56.0 0.1 shard_map.78
  56.1 3.2 %collective-permute-done.18.refs_1_ = f32[1,128,256]{2,1,0:T(8,128)S(1)} collective-permute-done((f32[1,128,256]{2,1,0:T(8,128)S(1)}, f32[1,128,256]{2,1,0:T(8,128)S(1)}, u32[]{:S(2)}, u32[]{:S(2)}) %collective-permute-start.18) | collective-permute-done | bytes 131104 | tf_op jit(solution)/shard_map/ppermute | solution.py:321
  59.3 0.1 collective-permute-start.23
  59.4 0.1 shard_map.80
  59.5 1.6 %collective-permute-start.21 = (f32[1,64,256]{2,1,0:T(8,128)S(1)}, f32[1,64,256]{2,1,0:T(8,128)S(1)}, u32[]{:S(2)}, u32[]{:S(2)}) collective-permute-start(f32[1,64,256]{2,1,0:T(8,128)S(1)} %get-tuple-element.89.refs_0_), channel_id=1, source_target_pairs={{0,4},{1,3},{2,6},{3,1},{4,0},{5,7},{6,2},{7,5},{8,12},{9,11},{10,... | collective-permute-start | bytes 196616 | tf_op jit(solution)/shard_map/ppermute | solution.py:321
  61.1 0.6 collective-permute-start.19
  61.7 2.2 %collective-permute-done.21.refs_1_ = f32[1,64,256]{2,1,0:T(8,128)S(1)} collective-permute-done((f32[1,64,256]{2,1,0:T(8,128)S(1)}, f32[1,64,256]{2,1,0:T(8,128)S(1)}, u32[]{:S(2)}, u32[]{:S(2)}) %collective-permute-start.21) | collective-permute-done | bytes 65568 | tf_op jit(solution)/shard_map/ppermute | solution.py:321
  63.9 1.8 %collective-permute-start.26 = (f32[2,64,256]{2,1,0:T(8,128)S(1)}, f32[2,64,256]{2,1,0:T(8,128)S(1)}, u32[]{:S(2)}, u32[]{:S(2)}) collective-permute-start(f32[2,64,256]{2,1,0:T(8,128)S(1)} %shard_map.82.refs_4_.refs_0_), channel_id=1, source_target_pairs={{0,8},{1,9},{2,10},{3,11},{4,12},{5,13},{6,14},{7,15},{8,0},{9,1},... | collective-permute-start | bytes 393224 | tf_op jit(solution)/shard_map/ppermute | solution.py:321
  65.7 0.5 collective-permute-done.20.refs_1_
  66.2 0.1 shard_map.83
  66.3 0.5 collective-permute-start.24
  66.8 1.3 %collective-permute-start.22 = (f32[4,64,256]{2,1,0:T(8,128)S(1)}, f32[4,64,256]{2,1,0:T(8,128)S(1)}, u32[]{:S(2)}, u32[]{:S(2)}) collective-permute-start(f32[4,64,256]{2,1,0:T(8,128)S(1)} %shard_map.84.refs_2_.refs_0_), channel_id=1, source_target_pairs={{0,2},{1,9},{2,0},{3,11},{4,6},{5,13},{6,4},{7,15},{8,10},{9,1},{1... | collective-permute-start | bytes 786440 | tf_op jit(solution)/shard_map/ppermute | solution.py:321
  68.1 2.5 %collective-permute-done.24.refs_1_ = f32[1,64,256]{2,1,0:T(8,128)S(1)} collective-permute-done((f32[1,64,256]{2,1,0:T(8,128)S(1)}, f32[1,64,256]{2,1,0:T(8,128)S(1)}, u32[]{:S(2)}, u32[]{:S(2)}) %collective-permute-start.24) | collective-permute-done | bytes 65568 | tf_op jit(solution)/shard_map/ppermute | solution.py:321
  70.7 0.1 collective-permute-start.29
  70.7 0.1 shard_map.86.refs_2_.refs_0_
  70.9 2.0 %collective-permute-start.25 = (f32[1,72,256]{2,1,0:T(8,128)S(1)}, f32[1,72,256]{2,1,0:T(8,128)S(1)}, u32[]{:S(2)}, u32[]{:S(2)}) collective-permute-start(f32[1,72,256]{2,1,0:T(8,128)S(1)} %shard_map.86.refs_2_.refs_0_), channel_id=1, source_target_pairs={{0,4},{1,3},{2,6},{3,1},{4,0},{5,7},{6,2},{7,5},{8,12},{9,11},{10,... | collective-permute-start | bytes 221192 | tf_op jit(solution)/shard_map/ppermute | solution.py:321
  72.8 2.0 %collective-permute-start.28 = (f32[4,64,256]{2,1,0:T(8,128)S(1)}, f32[4,64,256]{2,1,0:T(8,128)S(1)}, u32[]{:S(2)}, u32[]{:S(2)}) collective-permute-start(f32[4,64,256]{2,1,0:T(8,128)S(1)} %shard_map.87.refs_2_.refs_0_), channel_id=1, source_target_pairs={{0,2},{1,5},{2,0},{3,7},{4,6},{5,1},{6,4},{7,3},{8,10},{9,13},{10,... | collective-permute-start | bytes 786440 | tf_op jit(solution)/shard_map/ppermute | solution.py:321
  74.9 1.2 %collective-permute-done.25.refs_1_ = f32[1,72,256]{2,1,0:T(8,128)S(1)} collective-permute-done((f32[1,72,256]{2,1,0:T(8,128)S(1)}, f32[1,72,256]{2,1,0:T(8,128)S(1)}, u32[]{:S(2)}, u32[]{:S(2)}) %collective-permute-start.25) | collective-permute-done | bytes 73760 | tf_op jit(solution)/shard_map/ppermute | solution.py:321
  76.1 1.2 %collective-permute-start.27 = (f32[2,72,256]{2,1,0:T(8,128)S(1)}, f32[2,72,256]{2,1,0:T(8,128)S(1)}, u32[]{:S(2)}, u32[]{:S(2)}) collective-permute-start(f32[2,72,256]{2,1,0:T(8,128)S(1)} %shard_map.88.refs_2_.refs_0_), channel_id=1, source_target_pairs={{0,8},{1,5},{2,10},{3,7},{4,12},{5,1},{6,14},{7,3},{8,0},{9,13},{1... | collective-permute-start | bytes 442376 | tf_op jit(solution)/shard_map/ppermute | solution.py:321
  77.4 1.9 %collective-permute-start.31 = (f32[4,64,256]{2,1,0:T(8,128)S(1)}, f32[4,64,256]{2,1,0:T(8,128)S(1)}, u32[]{:S(2)}, u32[]{:S(2)}) collective-permute-start(f32[4,64,256]{2,1,0:T(8,128)S(1)} %shard_map.89.refs_2_.refs_0_), channel_id=1, source_target_pairs={{0,2},{1,9},{2,0},{3,11},{4,6},{5,13},{6,4},{7,15},{8,10},{9,1},{1... | collective-permute-start | bytes 786440 | tf_op jit(solution)/shard_map/ppermute | solution.py:321
  79.4 1.9 %collective-permute-done.27.refs_1_ = f32[2,72,256]{2,1,0:T(8,128)S(1)} collective-permute-done((f32[2,72,256]{2,1,0:T(8,128)S(1)}, f32[2,72,256]{2,1,0:T(8,128)S(1)}, u32[]{:S(2)}, u32[]{:S(2)}) %collective-permute-start.27) | collective-permute-done | bytes 147488 | tf_op jit(solution)/shard_map/ppermute | solution.py:321
  81.4 1.4 %collective-permute-start.34 = (f32[4,72,256]{2,1,0:T(8,128)S(1)}, f32[4,72,256]{2,1,0:T(8,128)S(1)}, u32[]{:S(2)}, u32[]{:S(2)}) collective-permute-start(f32[4,72,256]{2,1,0:T(8,128)S(1)} %shard_map.91.refs_2_.refs_0_), channel_id=1, source_target_pairs={{0,2},{1,9},{2,0},{3,11},{4,6},{5,13},{6,4},{7,15},{8,10},{9,1},{1... | collective-permute-start | bytes 884744 | tf_op jit(solution)/shard_map/ppermute | solution.py:321
  82.8 0.1 collective-permute-start.30
  82.9 0.9 collective-permute-done.31.refs_1_
  83.9 0.1 collective-permute-start.33
  83.9 0.9 collective-permute-done.30.refs_1_
  84.8 1.2 %shard_map.94 = (f32[2,64,32,256]{3,2,1,0:T(8,128)}, f32[8,128]{1,0:T(8,128)S(1)}) custom-call(f32[8,64,256]{2,1,0:T(8,128)S(1)} %shard_map.92.refs_2_.refs_0_, f32[8,64,256]{2,1,0:T(8,128)S(1)} %collective-permute-done.30.refs_1_, f32[8,64,256]{2,1,0:T(8,128)S(1)} %shard_map.93.refs_2_.refs_1_), custom_call_target="tpu_custom_call" | custom-call | flops 10000000000 | bytes 1024 | tf_op jit(solution)/shard_map/pallas_call | solution.py:165
  86.1 1.2 %shard_map.95 = (f32[2,64,32,256]{3,2,1,0:T(8,128)}, f32[8,128]{1,0:T(8,128)S(1)}) custom-call(f32[2,64,32,256]{3,2,1,0:T(8,128)} %get-tuple-element.92.refs_0_, f32[8,64,256]{2,1,0:T(8,128)S(1)} %shard_map.90.refs_2_.refs_1_, f32[8,64,256]{2,1,0:T(8,128)S(1)} %collective-permute-done.32.refs_2_, ...), custom_call_target="tpu_custom_call", output_to_operand_aliasing={{0}: (0, {})} | custom-call | flops 10000000000 | bytes 1024 | tf_op jit(solution)/shard_map/pallas_call | solution.py:165
  87.3 0.8 collective-permute-done.34.refs_1_
  88.3 1.2 %shard_map.97 = (f32[2,64,32,256]{3,2,1,0:T(8,128)}, f32[8,128]{1,0:T(8,128)S(1)}) custom-call(f32[2,64,32,256]{3,2,1,0:T(8,128)} %get-tuple-element.94.refs_0_, f32[8,64,256]{2,1,0:T(8,128)S(1)} %shard_map.93.refs_2_.refs_1_, f32[8,64,256]{2,1,0:T(8,128)S(1)} %collective-permute-done.33.refs_2_, ...), custom_call_target="tpu_custom_call", output_to_operand_aliasing={{0}: (0, {})} | custom-call | flops 10000000000 | bytes 1024 | tf_op jit(solution)/shard_map/pallas_call | solution.py:165
  89.5 0.7 collective-permute-done.35.refs_2_
  90.3 1.9 %shard_map.98 = (f32[2,64,32,256]{3,2,1,0:T(8,128)}, f32[2,64,256]{2,1,0:T(8,128)}) custom-call(f32[2,64,32,256]{3,2,1,0:T(8,128)} %get-tuple-element.96.refs_0_, f32[8,72,256]{2,1,0:T(8,128)S(1)} %shard_map.96.refs_3_.refs_1_, f32[8,72,256]{2,1,0:T(8,128)S(1)} %collective-permute-done.35.refs_2_, ...), custom_call_target="tpu_custom_call", output_to_operand_aliasing={{0}: (0, {})} | custom-call | flops 10000000000 | bytes 1024 | tf_op jit(solution)/shard_map/pallas_call | solution.py:165
  (48 shorter events, 1.0 us)
Async XLA Ops:
  6.2 4.3 %collective-permute-start = (f32[8,136,256]{2,1,0:T(8,128)S(1)}, f32[8,136,256]{2,1,0:T(8,128)S(1)}, u32[]{:S(2)}, u32[]{:S(2)}) collective-permute-start(f32[8,136,256]{2,1,0:T(8,128)S(1)} %get-tuple-element.52), channel_id=1, source_target_pairs={{0,1},{1,0},{2,3},{3,2},{4,5},{5,4},{6,7},{7,6},{8,9},{9,8},{10,11... | collective-permute-start | bytes 3342344 | tf_op jit(solution)/shard_map/ppermute | solution.py:321
  10.4 3.2 %collective-permute-start.2 = (f32[8,128,256]{2,1,0:T(8,128)S(1)}, f32[8,128,256]{2,1,0:T(8,128)S(1)}, u32[]{:S(2)}, u32[]{:S(2)}) collective-permute-start(f32[8,128,256]{2,1,0:T(8,128)S(1)} %get-tuple-element.55.refs_2_), channel_id=1, source_target_pairs={{0,1},{1,0},{2,3},{3,2},{4,5},{5,4},{6,7},{7,6},{8,9},{9,8},{10,11... | collective-permute-start | bytes 3145736 | tf_op jit(solution)/shard_map/ppermute | solution.py:321
  10.6 10.7 %collective-permute-start.1 = (f32[4,136,256]{2,1,0:T(8,128)S(1)}, f32[4,136,256]{2,1,0:T(8,128)S(1)}, u32[]{:S(2)}, u32[]{:S(2)}) collective-permute-start(f32[4,136,256]{2,1,0:T(8,128)S(1)} %get-tuple-element.57.refs_2_), channel_id=1, source_target_pairs={{0,2},{1,5},{2,0},{3,7},{4,6},{5,1},{6,4},{7,3},{8,10},{9,13},{10,... | collective-permute-start | bytes 1671176 | tf_op jit(solution)/shard_map/ppermute | solution.py:321
  17.4 6.3 %collective-permute-start.5 = (f32[8,128,256]{2,1,0:T(8,128)S(1)}, f32[8,128,256]{2,1,0:T(8,128)S(1)}, u32[]{:S(2)}, u32[]{:S(2)}) collective-permute-start(f32[8,128,256]{2,1,0:T(8,128)S(1)} %get-tuple-element.60.refs_2_), channel_id=1, source_target_pairs={{0,1},{1,0},{2,3},{3,2},{4,5},{5,4},{6,7},{7,6},{8,9},{9,8},{10,11... | collective-permute-start | bytes 3145736 | tf_op jit(solution)/shard_map/ppermute | solution.py:321
  17.5 11.7 %collective-permute-start.4 = (f32[4,128,256]{2,1,0:T(8,128)S(1)}, f32[4,128,256]{2,1,0:T(8,128)S(1)}, u32[]{:S(2)}, u32[]{:S(2)}) collective-permute-start(f32[4,128,256]{2,1,0:T(8,128)S(1)} %get-tuple-element.59.refs_2_), channel_id=1, source_target_pairs={{0,8},{1,3},{2,10},{3,1},{4,12},{5,7},{6,14},{7,5},{8,0},{9,11},{1... | collective-permute-start | bytes 1572872 | tf_op jit(solution)/shard_map/ppermute | solution.py:321
  21.3 9.9 %collective-permute-start.3 = (f32[2,136,256]{2,1,0:T(8,128)S(1)}, f32[2,136,256]{2,1,0:T(8,128)S(1)}, u32[]{:S(2)}, u32[]{:S(2)}) collective-permute-start(f32[2,136,256]{2,1,0:T(8,128)S(1)} %get-tuple-element.62.refs_2_), channel_id=1, source_target_pairs={{0,4},{1,3},{2,6},{3,1},{4,0},{5,7},{6,2},{7,5},{8,12},{9,11},{10,... | collective-permute-start | bytes 835592 | tf_op jit(solution)/shard_map/ppermute | solution.py:321
  23.9 11.3 %collective-permute-start.8 = (f32[4,128,256]{2,1,0:T(8,128)S(1)}, f32[4,128,256]{2,1,0:T(8,128)S(1)}, u32[]{:S(2)}, u32[]{:S(2)}) collective-permute-start(f32[4,128,256]{2,1,0:T(8,128)S(1)} %get-tuple-element.65.refs_2_), channel_id=1, source_target_pairs={{0,8},{1,5},{2,10},{3,7},{4,12},{5,1},{6,14},{7,3},{8,0},{9,13},{1... | collective-permute-start | bytes 1572872 | tf_op jit(solution)/shard_map/ppermute | solution.py:321
  29.2 4.2 %collective-permute-start.9 = (f32[8,128,256]{2,1,0:T(8,128)S(1)}, f32[8,128,256]{2,1,0:T(8,128)S(1)}, u32[]{:S(2)}, u32[]{:S(2)}) collective-permute-start(f32[8,128,256]{2,1,0:T(8,128)S(1)} %get-tuple-element.66.refs_2_), channel_id=1, source_target_pairs={{0,1},{1,0},{2,3},{3,2},{4,5},{5,4},{6,7},{7,6},{8,9},{9,8},{10,11... | collective-permute-start | bytes 3145736 | tf_op jit(solution)/shard_map/ppermute | solution.py:321
  29.3 6.4 %collective-permute-start.7 = (f32[2,128,256]{2,1,0:T(8,128)S(1)}, f32[2,128,256]{2,1,0:T(8,128)S(1)}, u32[]{:S(2)}, u32[]{:S(2)}) collective-permute-start(f32[2,128,256]{2,1,0:T(8,128)S(1)} %get-tuple-element.67.refs_2_), channel_id=1, source_target_pairs={{0,2},{1,5},{2,0},{3,7},{4,6},{5,1},{6,4},{7,3},{8,10},{9,13},{10,... | collective-permute-start | bytes 786440 | tf_op jit(solution)/shard_map/ppermute | solution.py:321
  31.3 6.1 %collective-permute-start.6 = (f32[1,136,256]{2,1,0:T(8,128)S(1)}, f32[1,136,256]{2,1,0:T(8,128)S(1)}, u32[]{:S(2)}, u32[]{:S(2)}) collective-permute-start(f32[1,136,256]{2,1,0:T(8,128)S(1)} %get-tuple-element.69.refs_2_), channel_id=1, source_target_pairs={{0,8},{1,9},{2,10},{3,11},{4,12},{5,13},{6,14},{7,15},{8,0},{9,1},... | collective-permute-start | bytes 417800 | tf_op jit(solution)/shard_map/ppermute | solution.py:321
  33.5 9.2 %collective-permute-start.13 = (f32[4,128,256]{2,1,0:T(8,128)S(1)}, f32[4,128,256]{2,1,0:T(8,128)S(1)}, u32[]{:S(2)}, u32[]{:S(2)}) collective-permute-start(f32[4,128,256]{2,1,0:T(8,128)S(1)} %get-tuple-element.73.refs_2_), channel_id=1, source_target_pairs={{0,2},{1,5},{2,0},{3,7},{4,6},{5,1},{6,4},{7,3},{8,10},{9,13},{10,... | collective-permute-start | bytes 1572872 | tf_op jit(solution)/shard_map/ppermute | solution.py:321
  35.2 10.8 %collective-permute-start.11 = (f32[2,128,256]{2,1,0:T(8,128)S(1)}, f32[2,128,256]{2,1,0:T(8,128)S(1)}, u32[]{:S(2)}, u32[]{:S(2)}) collective-permute-start(f32[2,128,256]{2,1,0:T(8,128)S(1)} %get-tuple-element.74.refs_2_), channel_id=1, source_target_pairs={{0,2},{1,9},{2,0},{3,11},{4,6},{5,13},{6,4},{7,15},{8,10},{9,1},{1... | collective-permute-start | bytes 786440 | tf_op jit(solution)/shard_map/ppermute | solution.py:321
  35.8 7.1 %collective-permute-start.12 = (f32[1,128,256]{2,1,0:T(8,128)S(1)}, f32[1,128,256]{2,1,0:T(8,128)S(1)}, u32[]{:S(2)}, u32[]{:S(2)}) collective-permute-start(f32[1,128,256]{2,1,0:T(8,128)S(1)} %get-tuple-element.75.refs_2_), channel_id=1, source_target_pairs={{0,4},{1,9},{2,6},{3,11},{4,0},{5,13},{6,2},{7,15},{8,12},{9,1},{1... | collective-permute-start | bytes 393224 | tf_op jit(solution)/shard_map/ppermute | solution.py:321
  37.4 18.6 %collective-permute-start.10 = (f32[1,136,256]{2,1,0:T(8,128)S(1)}, f32[1,136,256]{2,1,0:T(8,128)S(1)}, u32[]{:S(2)}, u32[]{:S(2)}) collective-permute-start(f32[1,136,256]{2,1,0:T(8,128)S(1)} %shard_map.72.refs_2_.refs_0_), channel_id=1, source_target_pairs={{0,16},{1,17},{2,18},{3,19},{4,20},{5,21},{6,22},{7,23},{8,24},{9,... | collective-permute-start | bytes 417800 | tf_op jit(solution)/shard_map/ppermute | solution.py:321
  42.8 11.5 %collective-permute-start.15 = (f32[2,128,256]{2,1,0:T(8,128)S(1)}, f32[2,128,256]{2,1,0:T(8,128)S(1)}, u32[]{:S(2)}, u32[]{:S(2)}) collective-permute-start(f32[2,128,256]{2,1,0:T(8,128)S(1)} %get-tuple-element.79.refs_2_), channel_id=1, source_target_pairs={{0,8},{1,3},{2,10},{3,1},{4,12},{5,7},{6,14},{7,5},{8,0},{9,11},{1... | collective-permute-start | bytes 786440 | tf_op jit(solution)/shard_map/ppermute | solution.py:321
  42.9 16.5 %collective-permute-start.17 = (f32[1,128,256]{2,1,0:T(8,128)S(1)}, f32[1,128,256]{2,1,0:T(8,128)S(1)}, u32[]{:S(2)}, u32[]{:S(2)}) collective-permute-start(f32[1,128,256]{2,1,0:T(8,128)S(1)} %shard_map.74.refs_2_.refs_0_), channel_id=1, source_target_pairs={{0,16},{1,17},{2,18},{3,19},{4,20},{5,21},{6,22},{7,23},{8,24},{9,... | collective-permute-start | bytes 393224 | tf_op jit(solution)/shard_map/ppermute | solution.py:321
  46.1 9.8 %collective-permute-start.14 = (f32[1,128,256]{2,1,0:T(8,128)S(1)}, f32[1,128,256]{2,1,0:T(8,128)S(1)}, u32[]{:S(2)}, u32[]{:S(2)}) collective-permute-start(f32[1,128,256]{2,1,0:T(8,128)S(1)} %get-tuple-element.81.refs_2_), channel_id=1, source_target_pairs={{0,4},{1,3},{2,6},{3,1},{4,0},{5,7},{6,2},{7,5},{8,12},{9,11},{10,... | collective-permute-start | bytes 393224 | tf_op jit(solution)/shard_map/ppermute | solution.py:321
  54.3 5.0 %collective-permute-start.18 = (f32[1,128,256]{2,1,0:T(8,128)S(1)}, f32[1,128,256]{2,1,0:T(8,128)S(1)}, u32[]{:S(2)}, u32[]{:S(2)}) collective-permute-start(f32[1,128,256]{2,1,0:T(8,128)S(1)} %get-tuple-element.83.refs_2_), channel_id=1, source_target_pairs={{0,4},{1,9},{2,6},{3,11},{4,0},{5,13},{6,2},{7,15},{8,12},{9,1},{1... | collective-permute-start | bytes 393224 | tf_op jit(solution)/shard_map/ppermute | solution.py:321
  55.9 10.3 %collective-permute-start.20 = (f32[1,128,256]{2,1,0:T(8,128)S(1)}, f32[1,128,256]{2,1,0:T(8,128)S(1)}, u32[]{:S(2)}, u32[]{:S(2)}) collective-permute-start(f32[1,128,256]{2,1,0:T(8,128)S(1)} %shard_map.77.refs_2_.refs_0_), channel_id=1, source_target_pairs={{0,16},{1,17},{2,18},{3,19},{4,20},{5,21},{6,22},{7,23},{8,24},{9,... | collective-permute-start | bytes 393224 | tf_op jit(solution)/shard_map/ppermute | solution.py:321
  56.1 5.0 %collective-permute-start.16 = (f32[1,64,256]{2,1,0:T(8,128)S(1)}, f32[1,64,256]{2,1,0:T(8,128)S(1)}, u32[]{:S(2)}, u32[]{:S(2)}) collective-permute-start(f32[1,64,256]{2,1,0:T(8,128)S(1)} %get-tuple-element.84.refs_0_), channel_id=1, source_target_pairs={{0,8},{1,5},{2,10},{3,7},{4,12},{5,1},{6,14},{7,3},{8,0},{9,13},{1... | collective-permute-start | bytes 196616 | tf_op jit(solution)/shard_map/ppermute | solution.py:321
  59.3 11.4 %collective-permute-start.23 = (f32[1,128,256]{2,1,0:T(8,128)S(1)}, f32[1,128,256]{2,1,0:T(8,128)S(1)}, u32[]{:S(2)}, u32[]{:S(2)}) collective-permute-start(f32[1,128,256]{2,1,0:T(8,128)S(1)} %shard_map.79.refs_4_.refs_0_), channel_id=1, source_target_pairs={{0,16},{1,17},{2,18},{3,19},{4,20},{5,21},{6,22},{7,23},{8,24},{9,... | collective-permute-start | bytes 393224 | tf_op jit(solution)/shard_map/ppermute | solution.py:321
  59.5 4.3 %collective-permute-start.21 = (f32[1,64,256]{2,1,0:T(8,128)S(1)}, f32[1,64,256]{2,1,0:T(8,128)S(1)}, u32[]{:S(2)}, u32[]{:S(2)}) collective-permute-start(f32[1,64,256]{2,1,0:T(8,128)S(1)} %get-tuple-element.89.refs_0_), channel_id=1, source_target_pairs={{0,4},{1,3},{2,6},{3,1},{4,0},{5,7},{6,2},{7,5},{8,12},{9,11},{10,... | collective-permute-start | bytes 196616 | tf_op jit(solution)/shard_map/ppermute | solution.py:321
  61.1 5.7 %collective-permute-start.19 = (f32[2,64,256]{2,1,0:T(8,128)S(1)}, f32[2,64,256]{2,1,0:T(8,128)S(1)}, u32[]{:S(2)}, u32[]{:S(2)}) collective-permute-start(f32[2,64,256]{2,1,0:T(8,128)S(1)} %shard_map.81.refs_2_.refs_0_), channel_id=1, source_target_pairs={{0,4},{1,3},{2,6},{3,1},{4,0},{5,7},{6,2},{7,5},{8,12},{9,11},{10,... | collective-permute-start | bytes 393224 | tf_op jit(solution)/shard_map/ppermute | solution.py:321
  63.9 8.9 %collective-permute-start.26 = (f32[2,64,256]{2,1,0:T(8,128)S(1)}, f32[2,64,256]{2,1,0:T(8,128)S(1)}, u32[]{:S(2)}, u32[]{:S(2)}) collective-permute-start(f32[2,64,256]{2,1,0:T(8,128)S(1)} %shard_map.82.refs_4_.refs_0_), channel_id=1, source_target_pairs={{0,8},{1,9},{2,10},{3,11},{4,12},{5,13},{6,14},{7,15},{8,0},{9,1},... | collective-permute-start | bytes 393224 | tf_op jit(solution)/shard_map/ppermute | solution.py:321
  66.3 4.3 %collective-permute-start.24 = (f32[1,64,256]{2,1,0:T(8,128)S(1)}, f32[1,64,256]{2,1,0:T(8,128)S(1)}, u32[]{:S(2)}, u32[]{:S(2)}) collective-permute-start(f32[1,64,256]{2,1,0:T(8,128)S(1)} %get-tuple-element.91.refs_0_), channel_id=1, source_target_pairs={{0,4},{1,3},{2,6},{3,1},{4,0},{5,7},{6,2},{7,5},{8,12},{9,11},{10,... | collective-permute-start | bytes 196616 | tf_op jit(solution)/shard_map/ppermute | solution.py:321
  66.8 16.0 %collective-permute-start.22 = (f32[4,64,256]{2,1,0:T(8,128)S(1)}, f32[4,64,256]{2,1,0:T(8,128)S(1)}, u32[]{:S(2)}, u32[]{:S(2)}) collective-permute-start(f32[4,64,256]{2,1,0:T(8,128)S(1)} %shard_map.84.refs_2_.refs_0_), channel_id=1, source_target_pairs={{0,2},{1,9},{2,0},{3,11},{4,6},{5,13},{6,4},{7,15},{8,10},{9,1},{1... | collective-permute-start | bytes 786440 | tf_op jit(solution)/shard_map/ppermute | solution.py:321
  70.7 6.7 %collective-permute-start.29 = (f32[2,64,256]{2,1,0:T(8,128)S(1)}, f32[2,64,256]{2,1,0:T(8,128)S(1)}, u32[]{:S(2)}, u32[]{:S(2)}) collective-permute-start(f32[2,64,256]{2,1,0:T(8,128)S(1)} %shard_map.85.refs_4_.refs_0_), channel_id=1, source_target_pairs={{0,8},{1,5},{2,10},{3,7},{4,12},{5,1},{6,14},{7,3},{8,0},{9,13},{1... | collective-permute-start | bytes 393224 | tf_op jit(solution)/shard_map/ppermute | solution.py:321
  70.9 5.3 %collective-permute-start.25 = (f32[1,72,256]{2,1,0:T(8,128)S(1)}, f32[1,72,256]{2,1,0:T(8,128)S(1)}, u32[]{:S(2)}, u32[]{:S(2)}) collective-permute-start(f32[1,72,256]{2,1,0:T(8,128)S(1)} %shard_map.86.refs_2_.refs_0_), channel_id=1, source_target_pairs={{0,4},{1,3},{2,6},{3,1},{4,0},{5,7},{6,2},{7,5},{8,12},{9,11},{10,... | collective-permute-start | bytes 221192 | tf_op jit(solution)/shard_map/ppermute | solution.py:321
  72.8 6.4 %collective-permute-start.28 = (f32[4,64,256]{2,1,0:T(8,128)S(1)}, f32[4,64,256]{2,1,0:T(8,128)S(1)}, u32[]{:S(2)}, u32[]{:S(2)}) collective-permute-start(f32[4,64,256]{2,1,0:T(8,128)S(1)} %shard_map.87.refs_2_.refs_0_), channel_id=1, source_target_pairs={{0,2},{1,5},{2,0},{3,7},{4,6},{5,1},{6,4},{7,3},{8,10},{9,13},{10,... | collective-permute-start | bytes 786440 | tf_op jit(solution)/shard_map/ppermute | solution.py:321
  76.1 5.2 %collective-permute-start.27 = (f32[2,72,256]{2,1,0:T(8,128)S(1)}, f32[2,72,256]{2,1,0:T(8,128)S(1)}, u32[]{:S(2)}, u32[]{:S(2)}) collective-permute-start(f32[2,72,256]{2,1,0:T(8,128)S(1)} %shard_map.88.refs_2_.refs_0_), channel_id=1, source_target_pairs={{0,8},{1,5},{2,10},{3,7},{4,12},{5,1},{6,14},{7,3},{8,0},{9,13},{1... | collective-permute-start | bytes 442376 | tf_op jit(solution)/shard_map/ppermute | solution.py:321
  77.4 6.4 %collective-permute-start.31 = (f32[4,64,256]{2,1,0:T(8,128)S(1)}, f32[4,64,256]{2,1,0:T(8,128)S(1)}, u32[]{:S(2)}, u32[]{:S(2)}) collective-permute-start(f32[4,64,256]{2,1,0:T(8,128)S(1)} %shard_map.89.refs_2_.refs_0_), channel_id=1, source_target_pairs={{0,2},{1,9},{2,0},{3,11},{4,6},{5,13},{6,4},{7,15},{8,10},{9,1},{1... | collective-permute-start | bytes 786440 | tf_op jit(solution)/shard_map/ppermute | solution.py:321
  79.3 6.7 %collective-permute-start.32 = (f32[8,64,256]{2,1,0:T(8,128)S(1)}, f32[8,64,256]{2,1,0:T(8,128)S(1)}, u32[]{:S(2)}, u32[]{:S(2)}) collective-permute-start(f32[8,64,256]{2,1,0:T(8,128)S(1)} %shard_map.90.refs_2_.refs_1_), channel_id=1, source_target_pairs={{0,1},{1,0},{2,3},{3,2},{4,5},{5,4},{6,7},{7,6},{8,9},{9,8},{10,11... | collective-permute-start | bytes 1572872 | tf_op jit(solution)/shard_map/ppermute | solution.py:321
  81.4 6.8 %collective-permute-start.34 = (f32[4,72,256]{2,1,0:T(8,128)S(1)}, f32[4,72,256]{2,1,0:T(8,128)S(1)}, u32[]{:S(2)}, u32[]{:S(2)}) collective-permute-start(f32[4,72,256]{2,1,0:T(8,128)S(1)} %shard_map.91.refs_2_.refs_0_), channel_id=1, source_target_pairs={{0,2},{1,9},{2,0},{3,11},{4,6},{5,13},{6,4},{7,15},{8,10},{9,1},{1... | collective-permute-start | bytes 884744 | tf_op jit(solution)/shard_map/ppermute | solution.py:321
  82.8 2.0 %collective-permute-start.30 = (f32[8,64,256]{2,1,0:T(8,128)S(1)}, f32[8,64,256]{2,1,0:T(8,128)S(1)}, u32[]{:S(2)}, u32[]{:S(2)}) collective-permute-start(f32[8,64,256]{2,1,0:T(8,128)S(1)} %shard_map.92.refs_2_.refs_0_), channel_id=1, source_target_pairs={{0,1},{1,0},{2,3},{3,2},{4,5},{5,4},{6,7},{7,6},{8,9},{9,8},{10,11... | collective-permute-start | bytes 1572872 | tf_op jit(solution)/shard_map/ppermute | solution.py:321
  83.9 4.4 %collective-permute-start.33 = (f32[8,64,256]{2,1,0:T(8,128)S(1)}, f32[8,64,256]{2,1,0:T(8,128)S(1)}, u32[]{:S(2)}, u32[]{:S(2)}) collective-permute-start(f32[8,64,256]{2,1,0:T(8,128)S(1)} %shard_map.93.refs_2_.refs_1_), channel_id=1, source_target_pairs={{0,1},{1,0},{2,3},{3,2},{4,5},{5,4},{6,7},{7,6},{8,9},{9,8},{10,11... | collective-permute-start | bytes 1572872 | tf_op jit(solution)/shard_map/ppermute | solution.py:321
  88.2 2.1 %collective-permute-start.35 = (f32[8,72,256]{2,1,0:T(8,128)S(1)}, f32[8,72,256]{2,1,0:T(8,128)S(1)}, u32[]{:S(2)}, u32[]{:S(2)}) collective-permute-start(f32[8,72,256]{2,1,0:T(8,128)S(1)} %shard_map.96.refs_3_.refs_1_), channel_id=1, source_target_pairs={{0,1},{1,0},{2,3},{3,2},{4,5},{5,4},{6,7},{7,6},{8,9},{9,8},{10,11... | collective-permute-start | bytes 1769480 | tf_op jit(solution)/shard_map/ppermute | solution.py:321

commit v4 on v3

--- a/solution.py
+++ b/solution.py
@@ -14,11 +14,12 @@
 LANES = 128
 EXTRA = 8
 VMEM_LIMIT = 48 * 2**20
-SIZES = [2, 2, 2, 2]
-BATCHES = [[0], [1], [2], [3]]
-HALVE = [('xyz', 'yxz'), ('zxy', 'xyz'), ('zxy', 'yzx'), ('xzy', 'yxz')]
-GATHER = [('xyz', 'zxy'), ('xzy', 'yzx'), ('xzy', 'zyx'), ('xzy', 'zyx')]
-ORDER = [('K', 0), ('K', 1), ('S', 0, 0), ('S', 1, 0), ('K', 2), ('S', 0, 1), ('S', 2, 0), ('K', 3), ('S', 1, 1), ('S', 0, 2), ('S', 3, 0), ('S', 2, 1), ('S', 1, 2), ('S', 0, 3), ('S', 3, 1), ('S', 1, 3), ('S', 2, 2), ('S', 3, 2), ('S', 2, 3), ('R', 0), ('S', 3, 3), ('R', 1), ('G', 0, 2), ('G', 1, 2), ('R', 2), ('G', 0, 1), ('G', 2, 2), ('R', 3), ('G', 1, 1), ('G', 3, 2), ('G', 2, 1), ('G', 1, 0), ('G', 3, 1), ('G', 0, 0), ('G', 2, 0), ('P', 0), ('P', 1), ('G', 3, 0), ('P', 2), ('P', 3)]
+SIZES = [1, 1, 2, 2, 2]
+BATCHES = [[0, 1], [2], [3], [4]]
+HALVE = [('zxy', 'zyx'), ('zxy', 'zyx'), ('xzy', 'yzx'), ('xzy', 'yzx'), ('xyz', 'yxz')]
+GATHER = [('xzy', 'yzx'), ('xzy', 'yzx'), ('zxy', 'zyx'), ('xyz', 'yxz')]
+ORDER = [('K', 0), ('K', 2), ('S', 0, 0), ('K', 1), ('S', 2, 0), ('K', 3), ('S', 1, 0), ('S', 0, 1), ('S', 3, 0), ('K', 4), ('S', 2, 1), ('S', 1, 1), ('S', 0, 2), ('S', 4, 0), ('S', 0, 3), ('S', 1, 2), ('S', 3, 1), ('S', 2, 2), ('S', 4, 1), ('S', 1, 3), ('S', 2, 3), ('S', 3, 2), ('S', 4, 2), ('R', 0), ('S', 3, 3), ('G', 0, 2), ('R', 1), ('S', 4, 3), ('R', 2), ('G', 1, 2), ('G', 2, 2), ('R', 3), ('G', 0, 1), ('G', 2, 1), ('G', 3, 2), ('G', 1, 1), ('G', 0, 0), ('G', 3, 1), ('G', 1, 0), ('G', 2, 0), ('P', 0), ('P', 1), ('G', 3, 0), ('P', 2), ('P', 3)]
+DOTS = 8
 FLIP = {"x": 2, "y": 4, "z": 8}
 
 
@@ -29,7 +30,7 @@
         self.top = devices // 2
         self.unit = self.items = devices // 4
         self.units = B // self.unit
-        assert self.units >= 1
+        assert 1 <= self.units <= EXTRA
         self.n_stages = bits - 2
         if devices == 32 and self.units == sum(SIZES):
             self.sizes, self.batches, self.order = SIZES, BATCHES, ORDER
@@ -69,8 +70,7 @@
     rows = bins.shape[0]
     step = min(rows, 256)
 
-    @pl.loop(0, plan.items)
-    def _(item):
+    def one(item):
         own = low_bin(path, me, item)
         theirs = mirrored(path, item, me & 1)
         for u in range(count):
@@ -87,6 +87,13 @@
             at = pl.ds(u * 2 * K, 2 * K)
             keep[item, at, :] = total[: 2 * K, :]
             send[theirs, at, :] = total[2 * K :, :]
+
+    together = max(1, DOTS // count)
+
+    @pl.loop(0, plan.items // together)
+    def _(turn):
+        for i in range(together):
+            one(turn * together + i)
 
     if has_totals:
         sums = jnp.sum(spread[...].astype(jnp.float32), axis=1, keepdims=True)
@@ -283,14 +290,13 @@
             fetched.append(fetch)
         for item in range(plan.items):
             own = low_bin(path, who, item)
-            for u in range(count):
-                copy = pltpu.make_async_copy(
-                    source.at[item, pl.ds(u * K, K), :],
-                    weights.at[who & 1, (first_unit + u) * plan.unit + own],
-                    sems.at[(side * plan.items + item) * count + u],
-                )
-                copy.start()
-                copies.append(copy)
+            copy = pltpu.make_async_copy(
+                source.at[item, pl.ds(0, count * K), :].reshape(count, K, source.shape[2]),
+                weights.at[who & 1, pl.ds(first_unit, count), own],
+                sems.at[side * plan.items + item],
+            )
+            copy.start()
+            copies.append(copy)
     if last:
         for side in range(2):
             fetched[side].wait()
@@ -298,14 +304,14 @@
             who = me ^ side
             for item in range(plan.items):
                 own = low_bin(path, who, item)
+                for h in range(lines.shape[0]):
+                    lines[h, who & 1, own] = held[side, item, :, h * LANES : (h + 1) * LANES]
+        for h in range(lines.shape[0]):
+            for node in range(NODES):
                 for u in range(plan.units):
-                    line = pl.ds(u * plan.unit + own, 1)
-                    for h in range(lines.shape[0]):
-                        lines[h, who & 1, line, :] = held[
-                            side, item, u : u + 1, h * LANES : (h + 1) * LANES
-                        ]
-        for h in range(lines.shape[0]):
-            gains[:, :, h * LANES : (h + 1) * LANES] = lines[h]
+                    gains[node, u * plan.unit : (u + 1) * plan.unit, h * LANES : (h + 1) * LANES] = lines[
+                        h, node, :, u, :
+                    ]
     for copy in copies:
         copy.wait()
 
@@ -419,13 +425,13 @@
         chunks = batches[g]
         count = sum(sizes[c] for c in chunks)
         last = g == len(batches) - 1
-        out_shape = [f32(NODES, B, K, features), f32(EXTRA, LANES)]
-        scratch = [pltpu.SemaphoreType.DMA((2 * plan.items * count,))]
+        out_shape = [f32(NODES, plan.units, plan.unit, K, features), f32(EXTRA, LANES)]
+        scratch = [pltpu.SemaphoreType.DMA((2 * plan.items,))]
         if last:
             out_shape[1] = f32(NODES, B, features)
             scratch = [
                 pltpu.VMEM((2, plan.items, EXTRA, features), jnp.float32),
-                pltpu.VMEM((features // LANES, NODES, B, LANES), jnp.float32),
+                pltpu.VMEM((features // LANES, NODES, plan.unit, EXTRA, LANES), jnp.float32),
                 *scratch,
                 pltpu.SemaphoreType.DMA((2,)),
             ]
@@ -455,7 +461,8 @@
     kinds = {"K": histogram, "S": reduce, "R": curves, "G": gather, "P": place}
     for name, *arguments in plan.order or [task for _, task in sorted(tasks, key=lambda t: t[0])]:
         kinds[name](*arguments)
-    return shared["gains_out"].transpose(2, 0, 1), shared["weights"].transpose(3, 0, 1, 2)
+    weights = shared["weights"].reshape(NODES, B, K, features)
+    return shared["gains_out"].transpose(2, 0, 1), weights.transpose(3, 0, 1, 2)
 
 
 def solution(mesh):

time: 92.4 us -> 86.5 us (0.936)
  waiting for transfers between devices: 26 us -> 17.2 us
  starting transfers between devices: 41.5 us -> 49.6 us
  Pallas kernels: 23.7 us -> 18.6 us
    ppermute x36 -> x41, waiting for transfers between devices: 26 us -> 17.2 us  [swap(): return lax.ppermute(x, 'dp', [(d, partner(d)) for d in range(devices)])]
    ppermute x36 -> x41, starting transfers between devices: 41.5 us -> 49.6 us  [swap(): return lax.ppermute(x, 'dp', [(d, partner(d)) for d in range(devices)])]
    pallas_call x40 -> x45, Pallas kernels: 23.7 us -> 18.6 us  [__call__(): pl.pallas_call(run, out_shape=out_shape, in_specs=in_specs, out_specs=out...]
  transfers between devices with their start and end apart: 36 -> 41, of which waited for: 15 -> 15; matrix products, arithmetic and copies ran while one was open for 0% -> 0% of each run, Pallas kernels for 18% -> 16%
where the time goes in v4:
time: 86.5 us; the launch traced here: 86.3 us
  starting transfers between devices  49.6 us (57%)
  Pallas kernels  18.6 us (22%)
  waiting for transfers between devices  17.2 us (20%)
  between operations  0.93 us (1%)
    ppermute x41, starting transfers between devices, swap(): return lax.ppermute(x, 'dp', [(d, partner(d)) for d in range(devices)])  49.6 us
    pallas_call x45, Pallas kernels, __call__(): pl.pallas_call(run, out_shape=out_shape, in_specs=in_specs, out_specs=out...  18.6 us
    ppermute x41, waiting for transfers between devices, swap(): return lax.ppermute(x, 'dp', [(d, partner(d)) for d in range(devices)])  17.2 us
  transfers between devices with their start and end apart: 41, of which 15 were waited for; matrix products, arithmetic and copies ran while one was open for 0% of the time, Pallas kernels for 16%

profile of v4, /device:TPU:0, one launch (start us, length us, event | category | flops | bytes accessed | tf_op | source)
XLA Modules:
  0.0 86.3 jit_solution(167044898183420005)
XLA Ops:
  0.6 3.1 %shard_map.59 = (f32[8,72,256]{2,1,0:T(8,128)S(1)}, f32[8,72,256]{2,1,0:T(8,128)S(1)}, bf16[2048,256]{1,0:T(8,128)(2,1)S(1)}, bf16[128,2048]{1,0:T(8,128)(2,1)S(1)}) custom-call(s32[2048,256]{1,0:T(8,128)} %refs_0_.1, s32[1,2048]{1,0:T(1,128)} %bitcast.9, bf16[32,2048]{1,0:T(8,128)(2,1)} %bitcast.7, bf16[32,2048]{1,0:T(8,128)(2,1)} %bitcast.8), custom_call_target="tpu_custom_call" | custom-call | flops 10000000000 | bytes 1024 | tf_op jit(solution)/shard_map/pallas_call | solution.py:172
  3.7 0.5 collective-permute-start
  4.2 2.5 %shard_map.60 = (f32[8,128,256]{2,1,0:T(8,128)S(1)}, f32[8,128,256]{2,1,0:T(8,128)S(1)}) custom-call(bf16[2048,256]{1,0:T(8,128)(2,1)S(1)} %get-tuple-element.61.refs_0_, bf16[128,2048]{1,0:T(8,128)(2,1)S(1)} %get-tuple-element.62.refs_1_.refs_2_, bf16[128,2048]{1,0:T(8,128)(2,1)S(1)} %get-tuple-element.62.refs_1_.refs_2_), custom_call_target="tpu_custom_call" | custom-call | flops 10000000000 | bytes 1024 | tf_op jit(solution)/shard_map/pallas_call | solution.py:172
  6.8 0.1 collective-permute-start.3
  7.0 3.1 %collective-permute-start.1 = (f32[4,72,256]{2,1,0:T(8,128)S(1)}, f32[4,72,256]{2,1,0:T(8,128)S(1)}, u32[]{:S(2)}, u32[]{:S(2)}) collective-permute-start(f32[4,72,256]{2,1,0:T(8,128)S(1)} %get-tuple-element.65.refs_2_), channel_id=1, source_target_pairs={{0,8},{1,9},{2,10},{3,11},{4,12},{5,13},{6,14},{7,15},{8,0},{9,1},... | collective-permute-start | bytes 884744 | tf_op jit(solution)/shard_map/ppermute | solution.py:327
  10.1 1.3 %shard_map.62 = (f32[8,64,256]{2,1,0:T(8,128)S(1)}, f32[8,64,256]{2,1,0:T(8,128)S(1)}) custom-call(bf16[2048,256]{1,0:T(8,128)(2,1)S(1)} %get-tuple-element.61.refs_0_, bf16[128,2048]{1,0:T(8,128)(2,1)S(1)} %get-tuple-element.62.refs_1_.refs_2_, f32[4,72,256]{2,1,0:T(8,128)S(1)} %get-tuple-element.65.refs_2_), custom_call_target="tpu_custom_call" | custom-call | flops 10000000000 | bytes 1024 | tf_op jit(solution)/shard_map/pallas_call | solution.py:172
  11.4 0.1 shard_map.63
  11.6 1.6 %collective-permute-start.6 = (f32[4,128,256]{2,1,0:T(8,128)S(1)}, f32[4,128,256]{2,1,0:T(8,128)S(1)}, u32[]{:S(2)}, u32[]{:S(2)}) collective-permute-start(f32[4,128,256]{2,1,0:T(8,128)S(1)} %get-tuple-element.69.refs_2_), channel_id=1, source_target_pairs={{0,2},{1,5},{2,0},{3,7},{4,6},{5,1},{6,4},{7,3},{8,10},{9,13},{10,... | collective-permute-start | bytes 1572872 | tf_op jit(solution)/shard_map/ppermute | solution.py:327
  13.1 2.5 %shard_map.64 = (f32[8,128,256]{2,1,0:T(8,128)S(1)}, f32[8,128,256]{2,1,0:T(8,128)S(1)}) custom-call(bf16[2048,256]{1,0:T(8,128)(2,1)S(1)} %get-tuple-element.61.refs_0_, bf16[128,2048]{1,0:T(8,128)(2,1)S(1)} %get-tuple-element.62.refs_1_.refs_2_, f32[4,128,256]{2,1,0:T(8,128)S(1)} %get-tuple-element.69.refs_2_), custom_call_target="tpu_custom_call" | custom-call | flops 10000000000 | bytes 1024 | tf_op jit(solution)/shard_map/pallas_call | solution.py:172
  15.7 0.3 collective-permute-start.7
  16.0 0.7 collective-permute-start.5
  16.8 0.5 collective-permute-done.1.refs_1_
  17.3 1.7 %collective-permute-start.4 = (f32[2,72,256]{2,1,0:T(8,128)S(1)}, f32[2,72,256]{2,1,0:T(8,128)S(1)}, u32[]{:S(2)}, u32[]{:S(2)}) collective-permute-start(f32[2,72,256]{2,1,0:T(8,128)S(1)} %get-tuple-element.73.refs_2_), channel_id=1, source_target_pairs={{0,2},{1,5},{2,0},{3,7},{4,6},{5,1},{6,4},{7,3},{8,10},{9,13},{10,... | collective-permute-start | bytes 442376 | tf_op jit(solution)/shard_map/ppermute | solution.py:327
  19.0 0.1 shard_map.67
  19.2 0.8 collective-permute-start.15
  19.9 2.5 %shard_map.68 = (f32[8,128,256]{2,1,0:T(8,128)S(1)}, f32[8,128,256]{2,1,0:T(8,128)S(1)}) custom-call(bf16[2048,256]{1,0:T(8,128)(2,1)S(1)} %get-tuple-element.61.refs_0_, bf16[128,2048]{1,0:T(8,128)(2,1)S(1)} %get-tuple-element.62.refs_1_.refs_2_, f32[4,128,256]{2,1,0:T(8,128)S(1)} %get-tuple-element.77.refs_2_), custom_call_target="tpu_custom_call" | custom-call | flops 10000000000 | bytes 1024 | tf_op jit(solution)/shard_map/pallas_call | solution.py:172
  22.6 1.5 %collective-permute-start.14 = (f32[2,128,256]{2,1,0:T(8,128)S(1)}, f32[2,128,256]{2,1,0:T(8,128)S(1)}, u32[]{:S(2)}, u32[]{:S(2)}) collective-permute-start(f32[2,128,256]{2,1,0:T(8,128)S(1)} %get-tuple-element.79.refs_2_), channel_id=1, source_target_pairs={{0,8},{1,9},{2,10},{3,11},{4,12},{5,13},{6,14},{7,15},{8,0},{9,1},... | collective-permute-start | bytes 786440 | tf_op jit(solution)/shard_map/ppermute | solution.py:327
  24.1 0.5 collective-permute-done.5.refs_1_
  24.6 1.3 %collective-permute-start.11 = (f32[2,64,256]{2,1,0:T(8,128)S(1)}, f32[2,64,256]{2,1,0:T(8,128)S(1)}, u32[]{:S(2)}, u32[]{:S(2)}) collective-permute-start(f32[2,64,256]{2,1,0:T(8,128)S(1)} %get-tuple-element.80.refs_2_), channel_id=1, source_target_pairs={{0,2},{1,5},{2,0},{3,7},{4,6},{5,1},{6,4},{7,3},{8,10},{9,13},{10,... | collective-permute-start | bytes 393224 | tf_op jit(solution)/shard_map/ppermute | solution.py:327
  25.9 1.5 %collective-permute-start.8 = (f32[1,72,256]{2,1,0:T(8,128)S(1)}, f32[1,72,256]{2,1,0:T(8,128)S(1)}, u32[]{:S(2)}, u32[]{:S(2)}) collective-permute-start(f32[1,72,256]{2,1,0:T(8,128)S(1)} %get-tuple-element.82.refs_2_), channel_id=1, source_target_pairs={{0,4},{1,3},{2,6},{3,1},{4,0},{5,7},{6,2},{7,5},{8,12},{9,11},{10,... | collective-permute-start | bytes 221192 | tf_op jit(solution)/shard_map/ppermute | solution.py:327
  27.5 0.1 shard_map.72
  27.6 0.9 %collective-permute-start.13 = (f32[4,128,256]{2,1,0:T(8,128)S(1)}, f32[4,128,256]{2,1,0:T(8,128)S(1)}, u32[]{:S(2)}, u32[]{:S(2)}) collective-permute-start(f32[4,128,256]{2,1,0:T(8,128)S(1)} %get-tuple-element.84.refs_2_), channel_id=1, source_target_pairs={{0,2},{1,5},{2,0},{3,7},{4,6},{5,1},{6,4},{7,3},{8,10},{9,13},{10,... | collective-permute-start | bytes 1572872 | tf_op jit(solution)/shard_map/ppermute | solution.py:327
  28.5 2.4 %collective-permute-done.8.refs_1_ = f32[1,72,256]{2,1,0:T(8,128)S(1)} collective-permute-done((f32[1,72,256]{2,1,0:T(8,128)S(1)}, f32[1,72,256]{2,1,0:T(8,128)S(1)}, u32[]{:S(2)}, u32[]{:S(2)}) %collective-permute-start.8) | collective-permute-done | bytes 73760 | tf_op jit(solution)/shard_map/ppermute | solution.py:327
  30.9 2.7 %collective-permute-start.10 = (f32[1,72,256]{2,1,0:T(8,128)S(1)}, f32[1,72,256]{2,1,0:T(8,128)S(1)}, u32[]{:S(2)}, u32[]{:S(2)}) collective-permute-start(f32[1,72,256]{2,1,0:T(8,128)S(1)} %shard_map.73.refs_2_.refs_0_), channel_id=1, source_target_pairs={{0,16},{1,17},{2,18},{3,19},{4,20},{5,21},{6,22},{7,23},{8,24},{9,... | collective-permute-start | bytes 221192 | tf_op jit(solution)/shard_map/ppermute | solution.py:327
  33.5 1.9 %collective-permute-start.12 = (f32[1,64,256]{2,1,0:T(8,128)S(1)}, f32[1,64,256]{2,1,0:T(8,128)S(1)}, u32[]{:S(2)}, u32[]{:S(2)}) collective-permute-start(f32[1,64,256]{2,1,0:T(8,128)S(1)} %get-tuple-element.87.refs_2_), channel_id=1, source_target_pairs={{0,4},{1,3},{2,6},{3,1},{4,0},{5,7},{6,2},{7,5},{8,12},{9,11},{10,... | collective-permute-start | bytes 196616 | tf_op jit(solution)/shard_map/ppermute | solution.py:327
  35.5 0.4 collective-permute-start.18
  35.9 0.9 %collective-permute-start.19 = (f32[1,128,256]{2,1,0:T(8,128)S(1)}, f32[1,128,256]{2,1,0:T(8,128)S(1)}, u32[]{:S(2)}, u32[]{:S(2)}) collective-permute-start(f32[1,128,256]{2,1,0:T(8,128)S(1)} %get-tuple-element.92.refs_2_), channel_id=1, source_target_pairs={{0,4},{1,3},{2,6},{3,1},{4,0},{5,7},{6,2},{7,5},{8,12},{9,11},{10,... | collective-permute-start | bytes 393224 | tf_op jit(solution)/shard_map/ppermute | solution.py:327
  36.8 1.4 %collective-permute-done.13.refs_1_ = f32[4,128,256]{2,1,0:T(8,128)S(1)} collective-permute-done((f32[4,128,256]{2,1,0:T(8,128)S(1)}, f32[4,128,256]{2,1,0:T(8,128)S(1)}, u32[]{:S(2)}, u32[]{:S(2)}) %collective-permute-start.13) | collective-permute-done | bytes 524320 | tf_op jit(solution)/shard_map/ppermute | solution.py:327
  38.3 1.4 %collective-permute-start.17 = (f32[2,128,256]{2,1,0:T(8,128)S(1)}, f32[2,128,256]{2,1,0:T(8,128)S(1)}, u32[]{:S(2)}, u32[]{:S(2)}) collective-permute-start(f32[2,128,256]{2,1,0:T(8,128)S(1)} %get-tuple-element.93.refs_2_), channel_id=1, source_target_pairs={{0,4},{1,3},{2,6},{3,1},{4,0},{5,7},{6,2},{7,5},{8,12},{9,11},{10,... | collective-permute-start | bytes 786440 | tf_op jit(solution)/shard_map/ppermute | solution.py:327
  39.7 2.9 %collective-permute-start.16 = (f32[1,64,256]{2,1,0:T(8,128)S(1)}, f32[1,64,256]{2,1,0:T(8,128)S(1)}, u32[]{:S(2)}, u32[]{:S(2)}) collective-permute-start(f32[1,64,256]{2,1,0:T(8,128)S(1)} %shard_map.78.refs_2_), channel_id=1, source_target_pairs={{0,16},{1,17},{2,18},{3,19},{4,20},{5,21},{6,22},{7,23},{8,24},{9,... | collective-permute-start | bytes 196616 | tf_op jit(solution)/shard_map/ppermute | solution.py:327
  42.7 0.1 collective-permute-start.24
  42.8 0.4 collective-permute-done.18.refs_1_
  43.2 1.0 %collective-permute-start.21 = (f32[1,128,256]{2,1,0:T(8,128)S(1)}, f32[1,128,256]{2,1,0:T(8,128)S(1)}, u32[]{:S(2)}, u32[]{:S(2)}) collective-permute-start(f32[1,128,256]{2,1,0:T(8,128)S(1)} %get-tuple-element.97.refs_2_), channel_id=1, source_target_pairs={{0,4},{1,3},{2,6},{3,1},{4,0},{5,7},{6,2},{7,5},{8,12},{9,11},{10,... | collective-permute-start | bytes 393224 | tf_op jit(solution)/shard_map/ppermute | solution.py:327
  44.2 0.5 collective-permute-done.17.refs_1_
  44.8 1.2 %collective-permute-start.23 = (f32[1,128,256]{2,1,0:T(8,128)S(1)}, f32[1,128,256]{2,1,0:T(8,128)S(1)}, u32[]{:S(2)}, u32[]{:S(2)}) collective-permute-start(f32[1,128,256]{2,1,0:T(8,128)S(1)} %get-tuple-element.98.refs_4_), channel_id=1, source_target_pairs={{0,8},{1,9},{2,10},{3,11},{4,12},{5,13},{6,14},{7,15},{8,0},{9,1},... | collective-permute-start | bytes 393224 | tf_op jit(solution)/shard_map/ppermute | solution.py:327
  46.1 0.1 shard_map.82
  46.2 2.2 %collective-permute-start.20 = (f32[1,64,256]{2,1,0:T(8,128)S(1)}, f32[1,64,256]{2,1,0:T(8,128)S(1)}, u32[]{:S(2)}, u32[]{:S(2)}) collective-permute-start(f32[1,64,256]{2,1,0:T(8,128)S(1)} %get-tuple-element.99.refs_0_), channel_id=1, source_target_pairs={{0,4},{1,3},{2,6},{3,1},{4,0},{5,7},{6,2},{7,5},{8,12},{9,11},{10,... | collective-permute-start | bytes 196616 | tf_op jit(solution)/shard_map/ppermute | solution.py:327
  48.5 3.7 %collective-permute-start.26 = (f32[1,128,256]{2,1,0:T(8,128)S(1)}, f32[1,128,256]{2,1,0:T(8,128)S(1)}, u32[]{:S(2)}, u32[]{:S(2)}) collective-permute-start(f32[1,128,256]{2,1,0:T(8,128)S(1)} %shard_map.83.refs_2_.refs_0_), channel_id=1, source_target_pairs={{0,16},{1,17},{2,18},{3,19},{4,20},{5,21},{6,22},{7,23},{8,24},{9,... | collective-permute-start | bytes 393224 | tf_op jit(solution)/shard_map/ppermute | solution.py:327
  52.2 2.1 %collective-permute-start.22 = (f32[2,64,256]{2,1,0:T(8,128)S(1)}, f32[2,64,256]{2,1,0:T(8,128)S(1)}, u32[]{:S(2)}, u32[]{:S(2)}) collective-permute-start(f32[2,64,256]{2,1,0:T(8,128)S(1)} %shard_map.84.refs_4_.refs_0_), channel_id=1, source_target_pairs={{0,8},{1,9},{2,10},{3,11},{4,12},{5,13},{6,14},{7,15},{8,0},{9,1},... | collective-permute-start | bytes 393224 | tf_op jit(solution)/shard_map/ppermute | solution.py:327
  54.4 1.8 %collective-permute-start.28 = (f32[1,64,256]{2,1,0:T(8,128)S(1)}, f32[1,64,256]{2,1,0:T(8,128)S(1)}, u32[]{:S(2)}, u32[]{:S(2)}) collective-permute-start(f32[1,64,256]{2,1,0:T(8,128)S(1)} %get-tuple-element.107.refs_0_), channel_id=1, source_target_pairs={{0,4},{1,3},{2,6},{3,1},{4,0},{5,7},{6,2},{7,5},{8,12},{9,11},{10,... | collective-permute-start | bytes 196616 | tf_op jit(solution)/shard_map/ppermute | solution.py:327
  56.2 2.2 %collective-permute-start.25 = (f32[1,128,256]{2,1,0:T(8,128)S(1)}, f32[1,128,256]{2,1,0:T(8,128)S(1)}, u32[]{:S(2)}, u32[]{:S(2)}) collective-permute-start(f32[1,128,256]{2,1,0:T(8,128)S(1)} %shard_map.86.refs_4_.refs_0_), channel_id=1, source_target_pairs={{0,16},{1,17},{2,18},{3,19},{4,20},{5,21},{6,22},{7,23},{8,24},{9,... | collective-permute-start | bytes 393224 | tf_op jit(solution)/shard_map/ppermute | solution.py:327
  58.5 0.9 %collective-permute-done.26.refs_1_ = f32[1,128,256]{2,1,0:T(8,128)S(1)} collective-permute-done((f32[1,128,256]{2,1,0:T(8,128)S(1)}, f32[1,128,256]{2,1,0:T(8,128)S(1)}, u32[]{:S(2)}, u32[]{:S(2)}) %collective-permute-start.26) | collective-permute-done | bytes 131104 | tf_op jit(solution)/shard_map/ppermute | solution.py:327
  59.4 0.1 shard_map.87
  59.5 1.2 %collective-permute-start.27 = (f32[1,64,256]{2,1,0:T(8,128)S(1)}, f32[1,64,256]{2,1,0:T(8,128)S(1)}, u32[]{:S(2)}, u32[]{:S(2)}) collective-permute-start(f32[1,64,256]{2,1,0:T(8,128)S(1)} %get-tuple-element.106.refs_0_), channel_id=1, source_target_pairs={{0,4},{1,3},{2,6},{3,1},{4,0},{5,7},{6,2},{7,5},{8,12},{9,11},{10,... | collective-permute-start | bytes 196616 | tf_op jit(solution)/shard_map/ppermute | solution.py:327
  60.7 1.7 %collective-permute-start.30 = (f32[2,64,256]{2,1,0:T(8,128)S(1)}, f32[2,64,256]{2,1,0:T(8,128)S(1)}, u32[]{:S(2)}, u32[]{:S(2)}) collective-permute-start(f32[2,64,256]{2,1,0:T(8,128)S(1)} %shard_map.88.refs_2_.refs_0_), channel_id=1, source_target_pairs={{0,8},{1,9},{2,10},{3,11},{4,12},{5,13},{6,14},{7,15},{8,0},{9,1},... | collective-permute-start | bytes 393224 | tf_op jit(solution)/shard_map/ppermute | solution.py:327
  62.3 2.2 %collective-permute-done.27.refs_1_ = f32[1,64,256]{2,1,0:T(8,128)S(1)} collective-permute-done((f32[1,64,256]{2,1,0:T(8,128)S(1)}, f32[1,64,256]{2,1,0:T(8,128)S(1)}, u32[]{:S(2)}, u32[]{:S(2)}) %collective-permute-start.27) | collective-permute-done | bytes 65568 | tf_op jit(solution)/shard_map/ppermute | solution.py:327
  64.5 1.0 %collective-permute-start.32 = (f32[2,64,256]{2,1,0:T(8,128)S(1)}, f32[2,64,256]{2,1,0:T(8,128)S(1)}, u32[]{:S(2)}, u32[]{:S(2)}) collective-permute-start(f32[2,64,256]{2,1,0:T(8,128)S(1)} %shard_map.89.refs_4_.refs_0_), channel_id=1, source_target_pairs={{0,2},{1,5},{2,0},{3,7},{4,6},{5,1},{6,4},{7,3},{8,10},{9,13},{10,... | collective-permute-start | bytes 393224 | tf_op jit(solution)/shard_map/ppermute | solution.py:327
  65.6 0.7 collective-permute-start.31
  66.3 1.0 %collective-permute-start.29 = (f32[4,64,256]{2,1,0:T(8,128)S(1)}, f32[4,64,256]{2,1,0:T(8,128)S(1)}, u32[]{:S(2)}, u32[]{:S(2)}) collective-permute-start(f32[4,64,256]{2,1,0:T(8,128)S(1)} %shard_map.91.refs_2_.refs_0_), channel_id=1, source_target_pairs={{0,2},{1,5},{2,0},{3,7},{4,6},{5,1},{6,4},{7,3},{8,10},{9,13},{10,... | collective-permute-start | bytes 786440 | tf_op jit(solution)/shard_map/ppermute | solution.py:327
  67.3 2.3 %collective-permute-done.32.refs_1_ = f32[2,64,256]{2,1,0:T(8,128)S(1)} collective-permute-done((f32[2,64,256]{2,1,0:T(8,128)S(1)}, f32[2,64,256]{2,1,0:T(8,128)S(1)}, u32[]{:S(2)}, u32[]{:S(2)}) %collective-permute-start.32) | collective-permute-done | bytes 131104 | tf_op jit(solution)/shard_map/ppermute | solution.py:327
  69.7 0.4 collective-permute-start.34
  70.1 2.3 %collective-permute-start.36 = (f32[2,72,256]{2,1,0:T(8,128)S(1)}, f32[2,72,256]{2,1,0:T(8,128)S(1)}, u32[]{:S(2)}, u32[]{:S(2)}) collective-permute-start(f32[2,72,256]{2,1,0:T(8,128)S(1)} %shard_map.93.refs_2_.refs_0_), channel_id=1, source_target_pairs={{0,4},{1,3},{2,6},{3,1},{4,0},{5,7},{6,2},{7,5},{8,12},{9,11},{10,... | collective-permute-start | bytes 442376 | tf_op jit(solution)/shard_map/ppermute | solution.py:327
  72.5 0.9 %collective-permute-start.35 = (f32[4,64,256]{2,1,0:T(8,128)S(1)}, f32[4,64,256]{2,1,0:T(8,128)S(1)}, u32[]{:S(2)}, u32[]{:S(2)}) collective-permute-start(f32[4,64,256]{2,1,0:T(8,128)S(1)} %shard_map.94.refs_2_.refs_0_), channel_id=1, source_target_pairs={{0,2},{1,5},{2,0},{3,7},{4,6},{5,1},{6,4},{7,3},{8,10},{9,13},{10,... | collective-permute-start | bytes 786440 | tf_op jit(solution)/shard_map/ppermute | solution.py:327
  73.5 2.1 %collective-permute-done.36.refs_1_ = f32[2,72,256]{2,1,0:T(8,128)S(1)} collective-permute-done((f32[2,72,256]{2,1,0:T(8,128)S(1)}, f32[2,72,256]{2,1,0:T(8,128)S(1)}, u32[]{:S(2)}, u32[]{:S(2)}) %collective-permute-start.36) | collective-permute-done | bytes 147488 | tf_op jit(solution)/shard_map/ppermute | solution.py:327
  75.6 0.9 %collective-permute-start.39 = (f32[4,72,256]{2,1,0:T(8,128)S(1)}, f32[4,72,256]{2,1,0:T(8,128)S(1)}, u32[]{:S(2)}, u32[]{:S(2)}) collective-permute-start(f32[4,72,256]{2,1,0:T(8,128)S(1)} %shard_map.96.refs_2_.refs_0_), channel_id=1, source_target_pairs={{0,2},{1,5},{2,0},{3,7},{4,6},{5,1},{6,4},{7,3},{8,10},{9,13},{10,... | collective-permute-start | bytes 884744 | tf_op jit(solution)/shard_map/ppermute | solution.py:327
  76.5 2.4 %collective-permute-done.35.refs_1_ = f32[4,64,256]{2,1,0:T(8,128)S(1)} collective-permute-done((f32[4,64,256]{2,1,0:T(8,128)S(1)}, f32[4,64,256]{2,1,0:T(8,128)S(1)}, u32[]{:S(2)}, u32[]{:S(2)}) %collective-permute-start.35) | collective-permute-done | bytes 262176 | tf_op jit(solution)/shard_map/ppermute | solution.py:327
  79.1 0.5 collective-permute-start.38
  79.6 1.1 %shard_map.99 = (f32[2,8,8,32,256]{4,3,2,1,0:T(8,128)}, f32[8,128]{1,0:T(8,128)S(1)}) custom-call(f32[8,64,256]{2,1,0:T(8,128)S(1)} %shard_map.95.refs_2_.refs_0_, f32[8,64,256]{2,1,0:T(8,128)S(1)} %collective-permute-done.33.refs_1_, f32[8,64,256]{2,1,0:T(8,128)S(1)} %shard_map.98.refs_2_.refs_1_), custom_call_target="tpu_custom_call" | custom-call | flops 10000000000 | bytes 1024 | tf_op jit(solution)/shard_map/pallas_call | solution.py:172
  80.7 0.2 collective-permute-done.37.refs_2_
  80.9 1.1 %shard_map.100 = (f32[2,8,8,32,256]{4,3,2,1,0:T(8,128)}, f32[8,128]{1,0:T(8,128)S(1)}) custom-call(f32[2,8,8,32,256]{4,3,2,1,0:T(8,128)} %get-tuple-element.108.refs_0_, f32[8,64,256]{2,1,0:T(8,128)S(1)} %shard_map.97.refs_2_.refs_1_, f32[8,64,256]{2,1,0:T(8,128)S(1)} %collective-permute-done.37.refs_2_, ...), custom_call_target="tpu_custom_call", output_to_operand_aliasing={{0}: (0, {})} | custom-call | flops 10000000000 | bytes 1024 | tf_op jit(solution)/shard_map/pallas_call | solution.py:172
  82.0 0.4 collective-permute-done.39.refs_1_
  82.5 1.1 %shard_map.102 = (f32[2,8,8,32,256]{4,3,2,1,0:T(8,128)}, f32[8,128]{1,0:T(8,128)S(1)}) custom-call(f32[2,8,8,32,256]{4,3,2,1,0:T(8,128)} %get-tuple-element.110.refs_0_, f32[8,64,256]{2,1,0:T(8,128)S(1)} %shard_map.98.refs_2_.refs_1_, f32[8,64,256]{2,1,0:T(8,128)S(1)} %collective-permute-done.38.refs_2_, ...), custom_call_target="tpu_custom_call", output_to_operand_aliasing={{0}: (0, {})} | custom-call | flops 10000000000 | bytes 1024 | tf_op jit(solution)/shard_map/pallas_call | solution.py:172
  83.6 0.9 %collective-permute-done.40.refs_2_ = f32[8,72,256]{2,1,0:T(8,128)S(1)} collective-permute-done((f32[8,72,256]{2,1,0:T(8,128)S(1)}, f32[8,72,256]{2,1,0:T(8,128)S(1)}, u32[]{:S(2)}, u32[]{:S(2)}) %collective-permute-start.40) | collective-permute-done | bytes 589856 | tf_op jit(solution)/shard_map/ppermute | solution.py:327
  84.5 1.8 %shard_map.103 = (f32[2,8,8,32,256]{4,3,2,1,0:T(8,128)}, f32[2,64,256]{2,1,0:T(8,128)}) custom-call(f32[2,8,8,32,256]{4,3,2,1,0:T(8,128)} %get-tuple-element.112.refs_0_, f32[8,72,256]{2,1,0:T(8,128)S(1)} %shard_map.101.refs_3_.refs_1_, f32[8,72,256]{2,1,0:T(8,128)S(1)} %collective-permute-done.40.refs_2_, ...), custom_call_target="tpu_custom_call", output_to_operand_aliasing={{0}: (0, {})} | custom-call | flops 10000000000 | bytes 1024 | tf_op jit(solution)/shard_map/pallas_call | solution.py:172
  (63 shorter events, 1.5 us)
Async XLA Ops:
  3.7 3.2 %collective-permute-start = (f32[8,72,256]{2,1,0:T(8,128)S(1)}, f32[8,72,256]{2,1,0:T(8,128)S(1)}, u32[]{:S(2)}, u32[]{:S(2)}) collective-permute-start(f32[8,72,256]{2,1,0:T(8,128)S(1)} %get-tuple-element.60), channel_id=1, source_target_pairs={{0,1},{1,0},{2,3},{3,2},{4,5},{5,4},{6,7},{7,6},{8,9},{9,8},{10,11... | collective-permute-start | bytes 1769480 | tf_op jit(solution)/shard_map/ppermute | solution.py:327
  6.8 4.6 %collective-permute-start.3 = (f32[8,128,256]{2,1,0:T(8,128)S(1)}, f32[8,128,256]{2,1,0:T(8,128)S(1)}, u32[]{:S(2)}, u32[]{:S(2)}) collective-permute-start(f32[8,128,256]{2,1,0:T(8,128)S(1)} %get-tuple-element.63.refs_2_), channel_id=1, source_target_pairs={{0,1},{1,0},{2,3},{3,2},{4,5},{5,4},{6,7},{7,6},{8,9},{9,8},{10,11... | collective-permute-start | bytes 3145736 | tf_op jit(solution)/shard_map/ppermute | solution.py:327
  7.0 10.3 %collective-permute-start.1 = (f32[4,72,256]{2,1,0:T(8,128)S(1)}, f32[4,72,256]{2,1,0:T(8,128)S(1)}, u32[]{:S(2)}, u32[]{:S(2)}) collective-permute-start(f32[4,72,256]{2,1,0:T(8,128)S(1)} %get-tuple-element.65.refs_2_), channel_id=1, source_target_pairs={{0,8},{1,9},{2,10},{3,11},{4,12},{5,13},{6,14},{7,15},{8,0},{9,1},... | collective-permute-start | bytes 884744 | tf_op jit(solution)/shard_map/ppermute | solution.py:327
  11.3 4.6 %collective-permute-start.2 = (f32[8,64,256]{2,1,0:T(8,128)S(1)}, f32[8,64,256]{2,1,0:T(8,128)S(1)}, u32[]{:S(2)}, u32[]{:S(2)}) collective-permute-start(f32[8,64,256]{2,1,0:T(8,128)S(1)} %get-tuple-element.67.refs_2_), channel_id=1, source_target_pairs={{0,1},{1,0},{2,3},{3,2},{4,5},{5,4},{6,7},{7,6},{8,9},{9,8},{10,11... | collective-permute-start | bytes 1572872 | tf_op jit(solution)/shard_map/ppermute | solution.py:327
  11.6 11.0 %collective-permute-start.6 = (f32[4,128,256]{2,1,0:T(8,128)S(1)}, f32[4,128,256]{2,1,0:T(8,128)S(1)}, u32[]{:S(2)}, u32[]{:S(2)}) collective-permute-start(f32[4,128,256]{2,1,0:T(8,128)S(1)} %get-tuple-element.69.refs_2_), channel_id=1, source_target_pairs={{0,2},{1,5},{2,0},{3,7},{4,6},{5,1},{6,4},{7,3},{8,10},{9,13},{10,... | collective-permute-start | bytes 1572872 | tf_op jit(solution)/shard_map/ppermute | solution.py:327
  15.7 3.4 %collective-permute-start.7 = (f32[8,128,256]{2,1,0:T(8,128)S(1)}, f32[8,128,256]{2,1,0:T(8,128)S(1)}, u32[]{:S(2)}, u32[]{:S(2)}) collective-permute-start(f32[8,128,256]{2,1,0:T(8,128)S(1)} %get-tuple-element.70.refs_2_), channel_id=1, source_target_pairs={{0,1},{1,0},{2,3},{3,2},{4,5},{5,4},{6,7},{7,6},{8,9},{9,8},{10,11... | collective-permute-start | bytes 3145736 | tf_op jit(solution)/shard_map/ppermute | solution.py:327
  16.0 8.6 %collective-permute-start.5 = (f32[4,64,256]{2,1,0:T(8,128)S(1)}, f32[4,64,256]{2,1,0:T(8,128)S(1)}, u32[]{:S(2)}, u32[]{:S(2)}) collective-permute-start(f32[4,64,256]{2,1,0:T(8,128)S(1)} %get-tuple-element.71.refs_2_), channel_id=1, source_target_pairs={{0,8},{1,9},{2,10},{3,11},{4,12},{5,13},{6,14},{7,15},{8,0},{9,1},... | collective-permute-start | bytes 786440 | tf_op jit(solution)/shard_map/ppermute | solution.py:327
  17.3 8.6 %collective-permute-start.4 = (f32[2,72,256]{2,1,0:T(8,128)S(1)}, f32[2,72,256]{2,1,0:T(8,128)S(1)}, u32[]{:S(2)}, u32[]{:S(2)}) collective-permute-start(f32[2,72,256]{2,1,0:T(8,128)S(1)} %get-tuple-element.73.refs_2_), channel_id=1, source_target_pairs={{0,2},{1,5},{2,0},{3,7},{4,6},{5,1},{6,4},{7,3},{8,10},{9,13},{10,... | collective-permute-start | bytes 442376 | tf_op jit(solution)/shard_map/ppermute | solution.py:327
  19.2 16.3 %collective-permute-start.15 = (f32[4,128,256]{2,1,0:T(8,128)S(1)}, f32[4,128,256]{2,1,0:T(8,128)S(1)}, u32[]{:S(2)}, u32[]{:S(2)}) collective-permute-start(f32[4,128,256]{2,1,0:T(8,128)S(1)} %get-tuple-element.77.refs_2_), channel_id=1, source_target_pairs={{0,2},{1,5},{2,0},{3,7},{4,6},{5,1},{6,4},{7,3},{8,10},{9,13},{10,... | collective-permute-start | bytes 1572872 | tf_op jit(solution)/shard_map/ppermute | solution.py:327
  22.5 5.0 %collective-permute-start.9 = (f32[8,128,256]{2,1,0:T(8,128)S(1)}, f32[8,128,256]{2,1,0:T(8,128)S(1)}, u32[]{:S(2)}, u32[]{:S(2)}) collective-permute-start(f32[8,128,256]{2,1,0:T(8,128)S(1)} %get-tuple-element.78.refs_2_), channel_id=1, source_target_pairs={{0,1},{1,0},{2,3},{3,2},{4,5},{5,4},{6,7},{7,6},{8,9},{9,8},{10,11... | collective-permute-start | bytes 3145736 | tf_op jit(solution)/shard_map/ppermute | solution.py:327
  22.6 13.3 %collective-permute-start.14 = (f32[2,128,256]{2,1,0:T(8,128)S(1)}, f32[2,128,256]{2,1,0:T(8,128)S(1)}, u32[]{:S(2)}, u32[]{:S(2)}) collective-permute-start(f32[2,128,256]{2,1,0:T(8,128)S(1)} %get-tuple-element.79.refs_2_), channel_id=1, source_target_pairs={{0,8},{1,9},{2,10},{3,11},{4,12},{5,13},{6,14},{7,15},{8,0},{9,1},... | collective-permute-start | bytes 786440 | tf_op jit(solution)/shard_map/ppermute | solution.py:327
  24.6 8.9 %collective-permute-start.11 = (f32[2,64,256]{2,1,0:T(8,128)S(1)}, f32[2,64,256]{2,1,0:T(8,128)S(1)}, u32[]{:S(2)}, u32[]{:S(2)}) collective-permute-start(f32[2,64,256]{2,1,0:T(8,128)S(1)} %get-tuple-element.80.refs_2_), channel_id=1, source_target_pairs={{0,2},{1,5},{2,0},{3,7},{4,6},{5,1},{6,4},{7,3},{8,10},{9,13},{10,... | collective-permute-start | bytes 393224 | tf_op jit(solution)/shard_map/ppermute | solution.py:327
  25.9 4.9 %collective-permute-start.8 = (f32[1,72,256]{2,1,0:T(8,128)S(1)}, f32[1,72,256]{2,1,0:T(8,128)S(1)}, u32[]{:S(2)}, u32[]{:S(2)}) collective-permute-start(f32[1,72,256]{2,1,0:T(8,128)S(1)} %get-tuple-element.82.refs_2_), channel_id=1, source_target_pairs={{0,4},{1,3},{2,6},{3,1},{4,0},{5,7},{6,2},{7,5},{8,12},{9,11},{10,... | collective-permute-start | bytes 221192 | tf_op jit(solution)/shard_map/ppermute | solution.py:327
  27.6 10.6 %collective-permute-start.13 = (f32[4,128,256]{2,1,0:T(8,128)S(1)}, f32[4,128,256]{2,1,0:T(8,128)S(1)}, u32[]{:S(2)}, u32[]{:S(2)}) collective-permute-start(f32[4,128,256]{2,1,0:T(8,128)S(1)} %get-tuple-element.84.refs_2_), channel_id=1, source_target_pairs={{0,2},{1,5},{2,0},{3,7},{4,6},{5,1},{6,4},{7,3},{8,10},{9,13},{10,... | collective-permute-start | bytes 1572872 | tf_op jit(solution)/shard_map/ppermute | solution.py:327
  30.9 15.2 %collective-permute-start.10 = (f32[1,72,256]{2,1,0:T(8,128)S(1)}, f32[1,72,256]{2,1,0:T(8,128)S(1)}, u32[]{:S(2)}, u32[]{:S(2)}) collective-permute-start(f32[1,72,256]{2,1,0:T(8,128)S(1)} %shard_map.73.refs_2_.refs_0_), channel_id=1, source_target_pairs={{0,16},{1,17},{2,18},{3,19},{4,20},{5,21},{6,22},{7,23},{8,24},{9,... | collective-permute-start | bytes 221192 | tf_op jit(solution)/shard_map/ppermute | solution.py:327
  33.5 6.2 %collective-permute-start.12 = (f32[1,64,256]{2,1,0:T(8,128)S(1)}, f32[1,64,256]{2,1,0:T(8,128)S(1)}, u32[]{:S(2)}, u32[]{:S(2)}) collective-permute-start(f32[1,64,256]{2,1,0:T(8,128)S(1)} %get-tuple-element.87.refs_2_), channel_id=1, source_target_pairs={{0,4},{1,3},{2,6},{3,1},{4,0},{5,7},{6,2},{7,5},{8,12},{9,11},{10,... | collective-permute-start | bytes 196616 | tf_op jit(solution)/shard_map/ppermute | solution.py:327
  35.5 7.7 %collective-permute-start.18 = (f32[2,128,256]{2,1,0:T(8,128)S(1)}, f32[2,128,256]{2,1,0:T(8,128)S(1)}, u32[]{:S(2)}, u32[]{:S(2)}) collective-permute-start(f32[2,128,256]{2,1,0:T(8,128)S(1)} %get-tuple-element.91.refs_2_), channel_id=1, source_target_pairs={{0,8},{1,9},{2,10},{3,11},{4,12},{5,13},{6,14},{7,15},{8,0},{9,1},... | collective-permute-start | bytes 786440 | tf_op jit(solution)/shard_map/ppermute | solution.py:327
  35.9 6.7 %collective-permute-start.19 = (f32[1,128,256]{2,1,0:T(8,128)S(1)}, f32[1,128,256]{2,1,0:T(8,128)S(1)}, u32[]{:S(2)}, u32[]{:S(2)}) collective-permute-start(f32[1,128,256]{2,1,0:T(8,128)S(1)} %get-tuple-element.92.refs_2_), channel_id=1, source_target_pairs={{0,4},{1,3},{2,6},{3,1},{4,0},{5,7},{6,2},{7,5},{8,12},{9,11},{10,... | collective-permute-start | bytes 393224 | tf_op jit(solution)/shard_map/ppermute | solution.py:327
  38.3 6.4 %collective-permute-start.17 = (f32[2,128,256]{2,1,0:T(8,128)S(1)}, f32[2,128,256]{2,1,0:T(8,128)S(1)}, u32[]{:S(2)}, u32[]{:S(2)}) collective-permute-start(f32[2,128,256]{2,1,0:T(8,128)S(1)} %get-tuple-element.93.refs_2_), channel_id=1, source_target_pairs={{0,4},{1,3},{2,6},{3,1},{4,0},{5,7},{6,2},{7,5},{8,12},{9,11},{10,... | collective-permute-start | bytes 786440 | tf_op jit(solution)/shard_map/ppermute | solution.py:327
  39.7 6.4 %collective-permute-start.16 = (f32[1,64,256]{2,1,0:T(8,128)S(1)}, f32[1,64,256]{2,1,0:T(8,128)S(1)}, u32[]{:S(2)}, u32[]{:S(2)}) collective-permute-start(f32[1,64,256]{2,1,0:T(8,128)S(1)} %shard_map.78.refs_2_), channel_id=1, source_target_pairs={{0,16},{1,17},{2,18},{3,19},{4,20},{5,21},{6,22},{7,23},{8,24},{9,... | collective-permute-start | bytes 196616 | tf_op jit(solution)/shard_map/ppermute | solution.py:327
  42.7 11.6 %collective-permute-start.24 = (f32[1,128,256]{2,1,0:T(8,128)S(1)}, f32[1,128,256]{2,1,0:T(8,128)S(1)}, u32[]{:S(2)}, u32[]{:S(2)}) collective-permute-start(f32[1,128,256]{2,1,0:T(8,128)S(1)} %shard_map.79.refs_2_.refs_0_), channel_id=1, source_target_pairs={{0,16},{1,17},{2,18},{3,19},{4,20},{5,21},{6,22},{7,23},{8,24},{9,... | collective-permute-start | bytes 393224 | tf_op jit(solution)/shard_map/ppermute | solution.py:327
  43.2 5.2 %collective-permute-start.21 = (f32[1,128,256]{2,1,0:T(8,128)S(1)}, f32[1,128,256]{2,1,0:T(8,128)S(1)}, u32[]{:S(2)}, u32[]{:S(2)}) collective-permute-start(f32[1,128,256]{2,1,0:T(8,128)S(1)} %get-tuple-element.97.refs_2_), channel_id=1, source_target_pairs={{0,4},{1,3},{2,6},{3,1},{4,0},{5,7},{6,2},{7,5},{8,12},{9,11},{10,... | collective-permute-start | bytes 393224 | tf_op jit(solution)/shard_map/ppermute | solution.py:327
  44.8 11.4 %collective-permute-start.23 = (f32[1,128,256]{2,1,0:T(8,128)S(1)}, f32[1,128,256]{2,1,0:T(8,128)S(1)}, u32[]{:S(2)}, u32[]{:S(2)}) collective-permute-start(f32[1,128,256]{2,1,0:T(8,128)S(1)} %get-tuple-element.98.refs_4_), channel_id=1, source_target_pairs={{0,8},{1,9},{2,10},{3,11},{4,12},{5,13},{6,14},{7,15},{8,0},{9,1},... | collective-permute-start | bytes 393224 | tf_op jit(solution)/shard_map/ppermute | solution.py:327
  46.2 6.0 %collective-permute-start.20 = (f32[1,64,256]{2,1,0:T(8,128)S(1)}, f32[1,64,256]{2,1,0:T(8,128)S(1)}, u32[]{:S(2)}, u32[]{:S(2)}) collective-permute-start(f32[1,64,256]{2,1,0:T(8,128)S(1)} %get-tuple-element.99.refs_0_), channel_id=1, source_target_pairs={{0,4},{1,3},{2,6},{3,1},{4,0},{5,7},{6,2},{7,5},{8,12},{9,11},{10,... | collective-permute-start | bytes 196616 | tf_op jit(solution)/shard_map/ppermute | solution.py:327
  48.5 10.9 %collective-permute-start.26 = (f32[1,128,256]{2,1,0:T(8,128)S(1)}, f32[1,128,256]{2,1,0:T(8,128)S(1)}, u32[]{:S(2)}, u32[]{:S(2)}) collective-permute-start(f32[1,128,256]{2,1,0:T(8,128)S(1)} %shard_map.83.refs_2_.refs_0_), channel_id=1, source_target_pairs={{0,16},{1,17},{2,18},{3,19},{4,20},{5,21},{6,22},{7,23},{8,24},{9,... | collective-permute-start | bytes 393224 | tf_op jit(solution)/shard_map/ppermute | solution.py:327
  52.2 14.1 %collective-permute-start.22 = (f32[2,64,256]{2,1,0:T(8,128)S(1)}, f32[2,64,256]{2,1,0:T(8,128)S(1)}, u32[]{:S(2)}, u32[]{:S(2)}) collective-permute-start(f32[2,64,256]{2,1,0:T(8,128)S(1)} %shard_map.84.refs_4_.refs_0_), channel_id=1, source_target_pairs={{0,8},{1,9},{2,10},{3,11},{4,12},{5,13},{6,14},{7,15},{8,0},{9,1},... | collective-permute-start | bytes 393224 | tf_op jit(solution)/shard_map/ppermute | solution.py:327
  54.4 6.2 %collective-permute-start.28 = (f32[1,64,256]{2,1,0:T(8,128)S(1)}, f32[1,64,256]{2,1,0:T(8,128)S(1)}, u32[]{:S(2)}, u32[]{:S(2)}) collective-permute-start(f32[1,64,256]{2,1,0:T(8,128)S(1)} %get-tuple-element.107.refs_0_), channel_id=1, source_target_pairs={{0,4},{1,3},{2,6},{3,1},{4,0},{5,7},{6,2},{7,5},{8,12},{9,11},{10,... | collective-permute-start | bytes 196616 | tf_op jit(solution)/shard_map/ppermute | solution.py:327
  56.2 9.2 %collective-permute-start.25 = (f32[1,128,256]{2,1,0:T(8,128)S(1)}, f32[1,128,256]{2,1,0:T(8,128)S(1)}, u32[]{:S(2)}, u32[]{:S(2)}) collective-permute-start(f32[1,128,256]{2,1,0:T(8,128)S(1)} %shard_map.86.refs_4_.refs_0_), channel_id=1, source_target_pairs={{0,16},{1,17},{2,18},{3,19},{4,20},{5,21},{6,22},{7,23},{8,24},{9,... | collective-permute-start | bytes 393224 | tf_op jit(solution)/shard_map/ppermute | solution.py:327
  59.5 5.0 %collective-permute-start.27 = (f32[1,64,256]{2,1,0:T(8,128)S(1)}, f32[1,64,256]{2,1,0:T(8,128)S(1)}, u32[]{:S(2)}, u32[]{:S(2)}) collective-permute-start(f32[1,64,256]{2,1,0:T(8,128)S(1)} %get-tuple-element.106.refs_0_), channel_id=1, source_target_pairs={{0,4},{1,3},{2,6},{3,1},{4,0},{5,7},{6,2},{7,5},{8,12},{9,11},{10,... | collective-permute-start | bytes 196616 | tf_op jit(solution)/shard_map/ppermute | solution.py:327
  60.7 11.8 %collective-permute-start.30 = (f32[2,64,256]{2,1,0:T(8,128)S(1)}, f32[2,64,256]{2,1,0:T(8,128)S(1)}, u32[]{:S(2)}, u32[]{:S(2)}) collective-permute-start(f32[2,64,256]{2,1,0:T(8,128)S(1)} %shard_map.88.refs_2_.refs_0_), channel_id=1, source_target_pairs={{0,8},{1,9},{2,10},{3,11},{4,12},{5,13},{6,14},{7,15},{8,0},{9,1},... | collective-permute-start | bytes 393224 | tf_op jit(solution)/shard_map/ppermute | solution.py:327
  64.5 5.2 %collective-permute-start.32 = (f32[2,64,256]{2,1,0:T(8,128)S(1)}, f32[2,64,256]{2,1,0:T(8,128)S(1)}, u32[]{:S(2)}, u32[]{:S(2)}) collective-permute-start(f32[2,64,256]{2,1,0:T(8,128)S(1)} %shard_map.89.refs_4_.refs_0_), channel_id=1, source_target_pairs={{0,2},{1,5},{2,0},{3,7},{4,6},{5,1},{6,4},{7,3},{8,10},{9,13},{10,... | collective-permute-start | bytes 393224 | tf_op jit(solution)/shard_map/ppermute | solution.py:327
  65.6 4.5 %collective-permute-start.31 = (f32[1,72,256]{2,1,0:T(8,128)S(1)}, f32[1,72,256]{2,1,0:T(8,128)S(1)}, u32[]{:S(2)}, u32[]{:S(2)}) collective-permute-start(f32[1,72,256]{2,1,0:T(8,128)S(1)} %shard_map.90.refs_2_.refs_0_), channel_id=1, source_target_pairs={{0,8},{1,9},{2,10},{3,11},{4,12},{5,13},{6,14},{7,15},{8,0},{9,1},... | collective-permute-start | bytes 221192 | tf_op jit(solution)/shard_map/ppermute | solution.py:327
  66.3 7.1 %collective-permute-start.29 = (f32[4,64,256]{2,1,0:T(8,128)S(1)}, f32[4,64,256]{2,1,0:T(8,128)S(1)}, u32[]{:S(2)}, u32[]{:S(2)}) collective-permute-start(f32[4,64,256]{2,1,0:T(8,128)S(1)} %shard_map.91.refs_2_.refs_0_), channel_id=1, source_target_pairs={{0,2},{1,5},{2,0},{3,7},{4,6},{5,1},{6,4},{7,3},{8,10},{9,13},{10,... | collective-permute-start | bytes 786440 | tf_op jit(solution)/shard_map/ppermute | solution.py:327
  69.7 9.3 %collective-permute-start.34 = (f32[4,64,256]{2,1,0:T(8,128)S(1)}, f32[4,64,256]{2,1,0:T(8,128)S(1)}, u32[]{:S(2)}, u32[]{:S(2)}) collective-permute-start(f32[4,64,256]{2,1,0:T(8,128)S(1)} %shard_map.92.refs_2_.refs_0_), channel_id=1, source_target_pairs={{0,8},{1,9},{2,10},{3,11},{4,12},{5,13},{6,14},{7,15},{8,0},{9,1},... | collective-permute-start | bytes 786440 | tf_op jit(solution)/shard_map/ppermute | solution.py:327
  70.1 5.4 %collective-permute-start.36 = (f32[2,72,256]{2,1,0:T(8,128)S(1)}, f32[2,72,256]{2,1,0:T(8,128)S(1)}, u32[]{:S(2)}, u32[]{:S(2)}) collective-permute-start(f32[2,72,256]{2,1,0:T(8,128)S(1)} %shard_map.93.refs_2_.refs_0_), channel_id=1, source_target_pairs={{0,4},{1,3},{2,6},{3,1},{4,0},{5,7},{6,2},{7,5},{8,12},{9,11},{10,... | collective-permute-start | bytes 442376 | tf_op jit(solution)/shard_map/ppermute | solution.py:327
  72.5 6.4 %collective-permute-start.35 = (f32[4,64,256]{2,1,0:T(8,128)S(1)}, f32[4,64,256]{2,1,0:T(8,128)S(1)}, u32[]{:S(2)}, u32[]{:S(2)}) collective-permute-start(f32[4,64,256]{2,1,0:T(8,128)S(1)} %shard_map.94.refs_2_.refs_0_), channel_id=1, source_target_pairs={{0,2},{1,5},{2,0},{3,7},{4,6},{5,1},{6,4},{7,3},{8,10},{9,13},{10,... | collective-permute-start | bytes 786440 | tf_op jit(solution)/shard_map/ppermute | solution.py:327
  73.4 6.2 %collective-permute-start.33 = (f32[8,64,256]{2,1,0:T(8,128)S(1)}, f32[8,64,256]{2,1,0:T(8,128)S(1)}, u32[]{:S(2)}, u32[]{:S(2)}) collective-permute-start(f32[8,64,256]{2,1,0:T(8,128)S(1)} %shard_map.95.refs_2_.refs_0_), channel_id=1, source_target_pairs={{0,1},{1,0},{2,3},{3,2},{4,5},{5,4},{6,7},{7,6},{8,9},{9,8},{10,11... | collective-permute-start | bytes 1572872 | tf_op jit(solution)/shard_map/ppermute | solution.py:327
  75.6 6.8 %collective-permute-start.39 = (f32[4,72,256]{2,1,0:T(8,128)S(1)}, f32[4,72,256]{2,1,0:T(8,128)S(1)}, u32[]{:S(2)}, u32[]{:S(2)}) collective-permute-start(f32[4,72,256]{2,1,0:T(8,128)S(1)} %shard_map.96.refs_2_.refs_0_), channel_id=1, source_target_pairs={{0,2},{1,5},{2,0},{3,7},{4,6},{5,1},{6,4},{7,3},{8,10},{9,13},{10,... | collective-permute-start | bytes 884744 | tf_op jit(solution)/shard_map/ppermute | solution.py:327
  78.9 2.0 %collective-permute-start.37 = (f32[8,64,256]{2,1,0:T(8,128)S(1)}, f32[8,64,256]{2,1,0:T(8,128)S(1)}, u32[]{:S(2)}, u32[]{:S(2)}) collective-permute-start(f32[8,64,256]{2,1,0:T(8,128)S(1)} %shard_map.97.refs_2_.refs_1_), channel_id=1, source_target_pairs={{0,1},{1,0},{2,3},{3,2},{4,5},{5,4},{6,7},{7,6},{8,9},{9,8},{10,11... | collective-permute-start | bytes 1572872 | tf_op jit(solution)/shard_map/ppermute | solution.py:327
  79.1 3.4 %collective-permute-start.38 = (f32[8,64,256]{2,1,0:T(8,128)S(1)}, f32[8,64,256]{2,1,0:T(8,128)S(1)}, u32[]{:S(2)}, u32[]{:S(2)}) collective-permute-start(f32[8,64,256]{2,1,0:T(8,128)S(1)} %shard_map.98.refs_2_.refs_1_), channel_id=1, source_target_pairs={{0,1},{1,0},{2,3},{3,2},{4,5},{5,4},{6,7},{7,6},{8,9},{9,8},{10,11... | collective-permute-start | bytes 1572872 | tf_op jit(solution)/shard_map/ppermute | solution.py:327
  82.4 2.1 %collective-permute-start.40 = (f32[8,72,256]{2,1,0:T(8,128)S(1)}, f32[8,72,256]{2,1,0:T(8,128)S(1)}, u32[]{:S(2)}, u32[]{:S(2)}) collective-permute-start(f32[8,72,256]{2,1,0:T(8,128)S(1)} %shard_map.101.refs_3_.refs_1_), channel_id=1, source_target_pairs={{0,1},{1,0},{2,3},{3,2},{4,5},{5,4},{6,7},{7,6},{8,9},{9,8},{10,11... | collective-permute-start | bytes 1769480 | tf_op jit(solution)/shard_map/ppermute | solution.py:327

commit v5 on v4

--- a/solution.py
+++ b/solution.py
@@ -18,7 +18,7 @@
 BATCHES = [[0, 1], [2], [3], [4]]
 HALVE = [('zxy', 'zyx'), ('zxy', 'zyx'), ('xzy', 'yzx'), ('xzy', 'yzx'), ('xyz', 'yxz')]
 GATHER = [('xzy', 'yzx'), ('xzy', 'yzx'), ('zxy', 'zyx'), ('xyz', 'yxz')]
-ORDER = [('K', 0), ('K', 2), ('S', 0, 0), ('K', 1), ('S', 2, 0), ('K', 3), ('S', 1, 0), ('S', 0, 1), ('S', 3, 0), ('K', 4), ('S', 2, 1), ('S', 1, 1), ('S', 0, 2), ('S', 4, 0), ('S', 0, 3), ('S', 1, 2), ('S', 3, 1), ('S', 2, 2), ('S', 4, 1), ('S', 1, 3), ('S', 2, 3), ('S', 3, 2), ('S', 4, 2), ('R', 0), ('S', 3, 3), ('G', 0, 2), ('R', 1), ('S', 4, 3), ('R', 2), ('G', 1, 2), ('G', 2, 2), ('R', 3), ('G', 0, 1), ('G', 2, 1), ('G', 3, 2), ('G', 1, 1), ('G', 0, 0), ('G', 3, 1), ('G', 1, 0), ('G', 2, 0), ('P', 0), ('P', 1), ('G', 3, 0), ('P', 2), ('P', 3)]
+ORDER = [('K', 0), ('K', 2), ('S', 0, 0), ('K', 1), ('S', 2, 0), ('K', 3), ('S', 1, 0), ('S', 0, 1), ('S', 3, 0), ('K', 4), ('S', 2, 1), ('S', 1, 1), ('S', 0, 2), ('S', 4, 0), ('S', 3, 1), ('S', 0, 3), ('S', 1, 2), ('S', 2, 2), ('S', 4, 1), ('S', 1, 3), ('S', 2, 3), ('S', 3, 2), ('S', 4, 2), ('R', 0), ('S', 3, 3), ('G', 0, 2), ('R', 1), ('S', 4, 3), ('R', 2), ('G', 1, 2), ('G', 2, 2), ('R', 3), ('G', 0, 1), ('G', 2, 1), ('G', 3, 2), ('G', 1, 1), ('G', 0, 0), ('G', 3, 1), ('G', 1, 0), ('G', 2, 0), ('P', 0), ('P', 1), ('G', 3, 0), ('P', 2), ('P', 3)]
 DOTS = 8
 FLIP = {"x": 2, "y": 4, "z": 8}
 
@@ -88,7 +88,7 @@
             keep[item, at, :] = total[: 2 * K, :]
             send[theirs, at, :] = total[2 * K :, :]
 
-    together = max(1, DOTS // count)
+    together = min(plan.items, max(1, DOTS // count))
 
     @pl.loop(0, plan.items // together)
     def _(turn):

time: 86.5 us -> 86.3 us (level)
  waiting for transfers between devices: 17.2 us -> 15.4 us
  starting transfers between devices: 49.6 us -> 51.2 us
    ppermute x41, waiting for transfers between devices: 17.2 us -> 15.4 us  [swap(): return lax.ppermute(x, 'dp', [(d, partner(d)) for d in range(devices)])]
    ppermute x41, starting transfers between devices: 49.6 us -> 51.2 us  [swap(): return lax.ppermute(x, 'dp', [(d, partner(d)) for d in range(devices)])]
  transfers between devices with their start and end apart: 41 -> 41, of which waited for: 15 -> 13; matrix products, arithmetic and copies ran while one was open for 0% -> 0% of each run, Pallas kernels for 16% -> 16%
where the time goes in v5:
time: 86.3 us; the launch traced here: 86.1 us
  starting transfers between devices  51.2 us (59%)
  Pallas kernels  18.6 us (22%)
  waiting for transfers between devices  15.4 us (18%)
  between operations  0.93 us (1%)
    ppermute x41, starting transfers between devices, swap(): return lax.ppermute(x, 'dp', [(d, partner(d)) for d in range(devices)])  51.2 us
    pallas_call x45, Pallas kernels, __call__(): pl.pallas_call(run, out_shape=out_shape, in_specs=in_specs, out_specs=out...  18.6 us
    ppermute x41, waiting for transfers between devices, swap(): return lax.ppermute(x, 'dp', [(d, partner(d)) for d in range(devices)])  15.4 us
  transfers between devices with their start and end apart: 41, of which 13 were waited for; matrix products, arithmetic and copies ran while one was open for 0% of the time, Pallas kernels for 16%

profile of v5, /device:TPU:0, one launch (start us, length us, event | category | flops | bytes accessed | tf_op | source)
XLA Modules:
  0.0 86.1 jit_solution(6329092263451468637)
XLA Ops:
  0.6 3.1 %shard_map.59 = (f32[8,72,256]{2,1,0:T(8,128)S(1)}, f32[8,72,256]{2,1,0:T(8,128)S(1)}, bf16[2048,256]{1,0:T(8,128)(2,1)S(1)}, bf16[128,2048]{1,0:T(8,128)(2,1)S(1)}) custom-call(s32[2048,256]{1,0:T(8,128)} %refs_0_.1, s32[1,2048]{1,0:T(1,128)} %bitcast.9, bf16[32,2048]{1,0:T(8,128)(2,1)} %bitcast.7, bf16[32,2048]{1,0:T(8,128)(2,1)} %bitcast.8), custom_call_target="tpu_custom_call" | custom-call | flops 10000000000 | bytes 1024 | tf_op jit(solution)/shard_map/pallas_call | solution.py:172
  3.7 0.5 collective-permute-start
  4.2 2.5 %shard_map.60 = (f32[8,128,256]{2,1,0:T(8,128)S(1)}, f32[8,128,256]{2,1,0:T(8,128)S(1)}) custom-call(bf16[2048,256]{1,0:T(8,128)(2,1)S(1)} %get-tuple-element.61.refs_0_, bf16[128,2048]{1,0:T(8,128)(2,1)S(1)} %get-tuple-element.62.refs_1_.refs_2_, bf16[128,2048]{1,0:T(8,128)(2,1)S(1)} %get-tuple-element.62.refs_1_.refs_2_), custom_call_target="tpu_custom_call" | custom-call | flops 10000000000 | bytes 1024 | tf_op jit(solution)/shard_map/pallas_call | solution.py:172
  6.8 0.1 collective-permute-start.3
  7.0 3.1 %collective-permute-start.1 = (f32[4,72,256]{2,1,0:T(8,128)S(1)}, f32[4,72,256]{2,1,0:T(8,128)S(1)}, u32[]{:S(2)}, u32[]{:S(2)}) collective-permute-start(f32[4,72,256]{2,1,0:T(8,128)S(1)} %get-tuple-element.65.refs_2_), channel_id=1, source_target_pairs={{0,8},{1,9},{2,10},{3,11},{4,12},{5,13},{6,14},{7,15},{8,0},{9,1},... | collective-permute-start | bytes 884744 | tf_op jit(solution)/shard_map/ppermute | solution.py:327
  10.1 1.3 %shard_map.62 = (f32[8,64,256]{2,1,0:T(8,128)S(1)}, f32[8,64,256]{2,1,0:T(8,128)S(1)}) custom-call(bf16[2048,256]{1,0:T(8,128)(2,1)S(1)} %get-tuple-element.61.refs_0_, bf16[128,2048]{1,0:T(8,128)(2,1)S(1)} %get-tuple-element.62.refs_1_.refs_2_, f32[4,72,256]{2,1,0:T(8,128)S(1)} %get-tuple-element.65.refs_2_), custom_call_target="tpu_custom_call" | custom-call | flops 10000000000 | bytes 1024 | tf_op jit(solution)/shard_map/pallas_call | solution.py:172
  11.4 0.1 shard_map.63
  11.6 1.6 %collective-permute-start.6 = (f32[4,128,256]{2,1,0:T(8,128)S(1)}, f32[4,128,256]{2,1,0:T(8,128)S(1)}, u32[]{:S(2)}, u32[]{:S(2)}) collective-permute-start(f32[4,128,256]{2,1,0:T(8,128)S(1)} %get-tuple-element.69.refs_2_), channel_id=1, source_target_pairs={{0,2},{1,5},{2,0},{3,7},{4,6},{5,1},{6,4},{7,3},{8,10},{9,13},{10,... | collective-permute-start | bytes 1572872 | tf_op jit(solution)/shard_map/ppermute | solution.py:327
  13.1 2.5 %shard_map.64 = (f32[8,128,256]{2,1,0:T(8,128)S(1)}, f32[8,128,256]{2,1,0:T(8,128)S(1)}) custom-call(bf16[2048,256]{1,0:T(8,128)(2,1)S(1)} %get-tuple-element.61.refs_0_, bf16[128,2048]{1,0:T(8,128)(2,1)S(1)} %get-tuple-element.62.refs_1_.refs_2_, f32[4,128,256]{2,1,0:T(8,128)S(1)} %get-tuple-element.69.refs_2_), custom_call_target="tpu_custom_call" | custom-call | flops 10000000000 | bytes 1024 | tf_op jit(solution)/shard_map/pallas_call | solution.py:172
  15.7 0.3 collective-permute-start.7
  16.0 0.7 collective-permute-start.5
  16.8 0.5 collective-permute-done.1.refs_1_
  17.3 1.7 %collective-permute-start.4 = (f32[2,72,256]{2,1,0:T(8,128)S(1)}, f32[2,72,256]{2,1,0:T(8,128)S(1)}, u32[]{:S(2)}, u32[]{:S(2)}) collective-permute-start(f32[2,72,256]{2,1,0:T(8,128)S(1)} %get-tuple-element.73.refs_2_), channel_id=1, source_target_pairs={{0,2},{1,5},{2,0},{3,7},{4,6},{5,1},{6,4},{7,3},{8,10},{9,13},{10,... | collective-permute-start | bytes 442376 | tf_op jit(solution)/shard_map/ppermute | solution.py:327
  19.0 0.1 shard_map.67
  19.2 0.8 collective-permute-start.9
  19.9 2.5 %shard_map.68 = (f32[8,128,256]{2,1,0:T(8,128)S(1)}, f32[8,128,256]{2,1,0:T(8,128)S(1)}) custom-call(bf16[2048,256]{1,0:T(8,128)(2,1)S(1)} %get-tuple-element.61.refs_0_, bf16[128,2048]{1,0:T(8,128)(2,1)S(1)} %get-tuple-element.62.refs_1_.refs_2_, f32[4,128,256]{2,1,0:T(8,128)S(1)} %get-tuple-element.77.refs_2_), custom_call_target="tpu_custom_call" | custom-call | flops 10000000000 | bytes 1024 | tf_op jit(solution)/shard_map/pallas_call | solution.py:172
  22.6 1.5 %collective-permute-start.15 = (f32[2,128,256]{2,1,0:T(8,128)S(1)}, f32[2,128,256]{2,1,0:T(8,128)S(1)}, u32[]{:S(2)}, u32[]{:S(2)}) collective-permute-start(f32[2,128,256]{2,1,0:T(8,128)S(1)} %get-tuple-element.79.refs_2_), channel_id=1, source_target_pairs={{0,8},{1,9},{2,10},{3,11},{4,12},{5,13},{6,14},{7,15},{8,0},{9,1},... | collective-permute-start | bytes 786440 | tf_op jit(solution)/shard_map/ppermute | solution.py:327
  24.1 0.5 collective-permute-done.5.refs_1_
  24.6 1.3 %collective-permute-start.12 = (f32[2,64,256]{2,1,0:T(8,128)S(1)}, f32[2,64,256]{2,1,0:T(8,128)S(1)}, u32[]{:S(2)}, u32[]{:S(2)}) collective-permute-start(f32[2,64,256]{2,1,0:T(8,128)S(1)} %get-tuple-element.80.refs_2_), channel_id=1, source_target_pairs={{0,2},{1,5},{2,0},{3,7},{4,6},{5,1},{6,4},{7,3},{8,10},{9,13},{10,... | collective-permute-start | bytes 393224 | tf_op jit(solution)/shard_map/ppermute | solution.py:327
  25.9 1.5 %collective-permute-start.8 = (f32[1,72,256]{2,1,0:T(8,128)S(1)}, f32[1,72,256]{2,1,0:T(8,128)S(1)}, u32[]{:S(2)}, u32[]{:S(2)}) collective-permute-start(f32[1,72,256]{2,1,0:T(8,128)S(1)} %get-tuple-element.82.refs_2_), channel_id=1, source_target_pairs={{0,4},{1,3},{2,6},{3,1},{4,0},{5,7},{6,2},{7,5},{8,12},{9,11},{10,... | collective-permute-start | bytes 221192 | tf_op jit(solution)/shard_map/ppermute | solution.py:327
  27.5 0.1 shard_map.72
  27.6 0.9 %collective-permute-start.14 = (f32[4,128,256]{2,1,0:T(8,128)S(1)}, f32[4,128,256]{2,1,0:T(8,128)S(1)}, u32[]{:S(2)}, u32[]{:S(2)}) collective-permute-start(f32[4,128,256]{2,1,0:T(8,128)S(1)} %get-tuple-element.85.refs_2_), channel_id=1, source_target_pairs={{0,2},{1,5},{2,0},{3,7},{4,6},{5,1},{6,4},{7,3},{8,10},{9,13},{10,... | collective-permute-start | bytes 1572872 | tf_op jit(solution)/shard_map/ppermute | solution.py:327
  28.6 2.4 %collective-permute-start.18 = (f32[2,128,256]{2,1,0:T(8,128)S(1)}, f32[2,128,256]{2,1,0:T(8,128)S(1)}, u32[]{:S(2)}, u32[]{:S(2)}) collective-permute-start(f32[2,128,256]{2,1,0:T(8,128)S(1)} %get-tuple-element.86.refs_2_), channel_id=1, source_target_pairs={{0,8},{1,9},{2,10},{3,11},{4,12},{5,13},{6,14},{7,15},{8,0},{9,1},... | collective-permute-start | bytes 786440 | tf_op jit(solution)/shard_map/ppermute | solution.py:327
  30.9 2.7 %collective-permute-start.11 = (f32[1,72,256]{2,1,0:T(8,128)S(1)}, f32[1,72,256]{2,1,0:T(8,128)S(1)}, u32[]{:S(2)}, u32[]{:S(2)}) collective-permute-start(f32[1,72,256]{2,1,0:T(8,128)S(1)} %shard_map.74.refs_2_.refs_0_), channel_id=1, source_target_pairs={{0,16},{1,17},{2,18},{3,19},{4,20},{5,21},{6,22},{7,23},{8,24},{9,... | collective-permute-start | bytes 221192 | tf_op jit(solution)/shard_map/ppermute | solution.py:327
  33.6 1.8 %collective-permute-start.13 = (f32[1,64,256]{2,1,0:T(8,128)S(1)}, f32[1,64,256]{2,1,0:T(8,128)S(1)}, u32[]{:S(2)}, u32[]{:S(2)}) collective-permute-start(f32[1,64,256]{2,1,0:T(8,128)S(1)} %get-tuple-element.89.refs_2_), channel_id=1, source_target_pairs={{0,4},{1,3},{2,6},{3,1},{4,0},{5,7},{6,2},{7,5},{8,12},{9,11},{10,... | collective-permute-start | bytes 196616 | tf_op jit(solution)/shard_map/ppermute | solution.py:327
  35.5 0.3 collective-permute-start.19
  35.8 2.7 %collective-permute-done.14.refs_1_ = f32[4,128,256]{2,1,0:T(8,128)S(1)} collective-permute-done((f32[4,128,256]{2,1,0:T(8,128)S(1)}, f32[4,128,256]{2,1,0:T(8,128)S(1)}, u32[]{:S(2)}, u32[]{:S(2)}) %collective-permute-start.14) | collective-permute-done | bytes 524320 | tf_op jit(solution)/shard_map/ppermute | solution.py:327
  38.5 1.4 %collective-permute-start.17 = (f32[2,128,256]{2,1,0:T(8,128)S(1)}, f32[2,128,256]{2,1,0:T(8,128)S(1)}, u32[]{:S(2)}, u32[]{:S(2)}) collective-permute-start(f32[2,128,256]{2,1,0:T(8,128)S(1)} %get-tuple-element.93.refs_2_), channel_id=1, source_target_pairs={{0,4},{1,3},{2,6},{3,1},{4,0},{5,7},{6,2},{7,5},{8,12},{9,11},{10,... | collective-permute-start | bytes 786440 | tf_op jit(solution)/shard_map/ppermute | solution.py:327
  39.9 2.8 %collective-permute-start.16 = (f32[1,64,256]{2,1,0:T(8,128)S(1)}, f32[1,64,256]{2,1,0:T(8,128)S(1)}, u32[]{:S(2)}, u32[]{:S(2)}) collective-permute-start(f32[1,64,256]{2,1,0:T(8,128)S(1)} %shard_map.78.refs_2_), channel_id=1, source_target_pairs={{0,16},{1,17},{2,18},{3,19},{4,20},{5,21},{6,22},{7,23},{8,24},{9,... | collective-permute-start | bytes 196616 | tf_op jit(solution)/shard_map/ppermute | solution.py:327
  42.7 0.2 collective-permute-start.24
  43.0 1.0 %collective-permute-start.21 = (f32[1,128,256]{2,1,0:T(8,128)S(1)}, f32[1,128,256]{2,1,0:T(8,128)S(1)}, u32[]{:S(2)}, u32[]{:S(2)}) collective-permute-start(f32[1,128,256]{2,1,0:T(8,128)S(1)} %get-tuple-element.97.refs_2_), channel_id=1, source_target_pairs={{0,4},{1,3},{2,6},{3,1},{4,0},{5,7},{6,2},{7,5},{8,12},{9,11},{10,... | collective-permute-start | bytes 393224 | tf_op jit(solution)/shard_map/ppermute | solution.py:327
  44.0 1.0 %collective-permute-done.17.refs_1_ = f32[2,128,256]{2,1,0:T(8,128)S(1)} collective-permute-done((f32[2,128,256]{2,1,0:T(8,128)S(1)}, f32[2,128,256]{2,1,0:T(8,128)S(1)}, u32[]{:S(2)}, u32[]{:S(2)}) %collective-permute-start.17) | collective-permute-done | bytes 262176 | tf_op jit(solution)/shard_map/ppermute | solution.py:327
  45.0 2.2 %collective-permute-start.23 = (f32[1,128,256]{2,1,0:T(8,128)S(1)}, f32[1,128,256]{2,1,0:T(8,128)S(1)}, u32[]{:S(2)}, u32[]{:S(2)}) collective-permute-start(f32[1,128,256]{2,1,0:T(8,128)S(1)} %get-tuple-element.98.refs_4_), channel_id=1, source_target_pairs={{0,8},{1,9},{2,10},{3,11},{4,12},{5,13},{6,14},{7,15},{8,0},{9,1},... | collective-permute-start | bytes 393224 | tf_op jit(solution)/shard_map/ppermute | solution.py:327
  47.2 0.1 shard_map.82
  47.3 2.1 %collective-permute-start.20 = (f32[1,64,256]{2,1,0:T(8,128)S(1)}, f32[1,64,256]{2,1,0:T(8,128)S(1)}, u32[]{:S(2)}, u32[]{:S(2)}) collective-permute-start(f32[1,64,256]{2,1,0:T(8,128)S(1)} %get-tuple-element.99.refs_0_), channel_id=1, source_target_pairs={{0,4},{1,3},{2,6},{3,1},{4,0},{5,7},{6,2},{7,5},{8,12},{9,11},{10,... | collective-permute-start | bytes 196616 | tf_op jit(solution)/shard_map/ppermute | solution.py:327
  49.4 2.8 %collective-permute-start.26 = (f32[1,128,256]{2,1,0:T(8,128)S(1)}, f32[1,128,256]{2,1,0:T(8,128)S(1)}, u32[]{:S(2)}, u32[]{:S(2)}) collective-permute-start(f32[1,128,256]{2,1,0:T(8,128)S(1)} %shard_map.83.refs_2_.refs_0_), channel_id=1, source_target_pairs={{0,16},{1,17},{2,18},{3,19},{4,20},{5,21},{6,22},{7,23},{8,24},{9,... | collective-permute-start | bytes 393224 | tf_op jit(solution)/shard_map/ppermute | solution.py:327
  52.2 2.8 %collective-permute-start.22 = (f32[2,64,256]{2,1,0:T(8,128)S(1)}, f32[2,64,256]{2,1,0:T(8,128)S(1)}, u32[]{:S(2)}, u32[]{:S(2)}) collective-permute-start(f32[2,64,256]{2,1,0:T(8,128)S(1)} %shard_map.84.refs_4_.refs_0_), channel_id=1, source_target_pairs={{0,8},{1,9},{2,10},{3,11},{4,12},{5,13},{6,14},{7,15},{8,0},{9,1},... | collective-permute-start | bytes 393224 | tf_op jit(solution)/shard_map/ppermute | solution.py:327
  55.0 0.1 shard_map.85
  55.1 1.4 %collective-permute-start.28 = (f32[1,64,256]{2,1,0:T(8,128)S(1)}, f32[1,64,256]{2,1,0:T(8,128)S(1)}, u32[]{:S(2)}, u32[]{:S(2)}) collective-permute-start(f32[1,64,256]{2,1,0:T(8,128)S(1)} %get-tuple-element.107.refs_0_), channel_id=1, source_target_pairs={{0,4},{1,3},{2,6},{3,1},{4,0},{5,7},{6,2},{7,5},{8,12},{9,11},{10,... | collective-permute-start | bytes 196616 | tf_op jit(solution)/shard_map/ppermute | solution.py:327
  56.5 2.2 %collective-permute-start.25 = (f32[1,128,256]{2,1,0:T(8,128)S(1)}, f32[1,128,256]{2,1,0:T(8,128)S(1)}, u32[]{:S(2)}, u32[]{:S(2)}) collective-permute-start(f32[1,128,256]{2,1,0:T(8,128)S(1)} %shard_map.86.refs_4_.refs_0_), channel_id=1, source_target_pairs={{0,16},{1,17},{2,18},{3,19},{4,20},{5,21},{6,22},{7,23},{8,24},{9,... | collective-permute-start | bytes 393224 | tf_op jit(solution)/shard_map/ppermute | solution.py:327
  58.8 0.2 collective-permute-done.26.refs_1_
  59.0 0.1 shard_map.87
  59.1 1.9 %collective-permute-start.27 = (f32[1,64,256]{2,1,0:T(8,128)S(1)}, f32[1,64,256]{2,1,0:T(8,128)S(1)}, u32[]{:S(2)}, u32[]{:S(2)}) collective-permute-start(f32[1,64,256]{2,1,0:T(8,128)S(1)} %get-tuple-element.106.refs_0_), channel_id=1, source_target_pairs={{0,4},{1,3},{2,6},{3,1},{4,0},{5,7},{6,2},{7,5},{8,12},{9,11},{10,... | collective-permute-start | bytes 196616 | tf_op jit(solution)/shard_map/ppermute | solution.py:327
  61.0 3.1 %collective-permute-done.27.refs_1_ = f32[1,64,256]{2,1,0:T(8,128)S(1)} collective-permute-done((f32[1,64,256]{2,1,0:T(8,128)S(1)}, f32[1,64,256]{2,1,0:T(8,128)S(1)}, u32[]{:S(2)}, u32[]{:S(2)}) %collective-permute-start.27) | collective-permute-done | bytes 65568 | tf_op jit(solution)/shard_map/ppermute | solution.py:327
  64.2 1.5 %collective-permute-start.32 = (f32[2,64,256]{2,1,0:T(8,128)S(1)}, f32[2,64,256]{2,1,0:T(8,128)S(1)}, u32[]{:S(2)}, u32[]{:S(2)}) collective-permute-start(f32[2,64,256]{2,1,0:T(8,128)S(1)} %shard_map.89.refs_4_.refs_0_), channel_id=1, source_target_pairs={{0,2},{1,5},{2,0},{3,7},{4,6},{5,1},{6,4},{7,3},{8,10},{9,13},{10,... | collective-permute-start | bytes 393224 | tf_op jit(solution)/shard_map/ppermute | solution.py:327
  65.6 0.1 shard_map.90.refs_2_.refs_0_
  65.7 0.8 collective-permute-start.31
  66.6 0.4 collective-permute-start.29
  67.0 2.2 %collective-permute-done.32.refs_1_ = f32[2,64,256]{2,1,0:T(8,128)S(1)} collective-permute-done((f32[2,64,256]{2,1,0:T(8,128)S(1)}, f32[2,64,256]{2,1,0:T(8,128)S(1)}, u32[]{:S(2)}, u32[]{:S(2)}) %collective-permute-start.32) | collective-permute-done | bytes 131104 | tf_op jit(solution)/shard_map/ppermute | solution.py:327
  69.2 0.5 collective-permute-start.34
  69.8 0.4 collective-permute-done.31.refs_1_
  70.2 1.5 %collective-permute-start.36 = (f32[2,72,256]{2,1,0:T(8,128)S(1)}, f32[2,72,256]{2,1,0:T(8,128)S(1)}, u32[]{:S(2)}, u32[]{:S(2)}) collective-permute-start(f32[2,72,256]{2,1,0:T(8,128)S(1)} %shard_map.93.refs_2_.refs_0_), channel_id=1, source_target_pairs={{0,4},{1,3},{2,6},{3,1},{4,0},{5,7},{6,2},{7,5},{8,12},{9,11},{10,... | collective-permute-start | bytes 442376 | tf_op jit(solution)/shard_map/ppermute | solution.py:327
  71.7 2.0 %collective-permute-start.35 = (f32[4,64,256]{2,1,0:T(8,128)S(1)}, f32[4,64,256]{2,1,0:T(8,128)S(1)}, u32[]{:S(2)}, u32[]{:S(2)}) collective-permute-start(f32[4,64,256]{2,1,0:T(8,128)S(1)} %shard_map.94.refs_2_.refs_0_), channel_id=1, source_target_pairs={{0,2},{1,5},{2,0},{3,7},{4,6},{5,1},{6,4},{7,3},{8,10},{9,13},{10,... | collective-permute-start | bytes 786440 | tf_op jit(solution)/shard_map/ppermute | solution.py:327
  73.9 1.5 %collective-permute-done.36.refs_1_ = f32[2,72,256]{2,1,0:T(8,128)S(1)} collective-permute-done((f32[2,72,256]{2,1,0:T(8,128)S(1)}, f32[2,72,256]{2,1,0:T(8,128)S(1)}, u32[]{:S(2)}, u32[]{:S(2)}) %collective-permute-start.36) | collective-permute-done | bytes 147488 | tf_op jit(solution)/shard_map/ppermute | solution.py:327
  75.4 1.5 %collective-permute-start.39 = (f32[4,72,256]{2,1,0:T(8,128)S(1)}, f32[4,72,256]{2,1,0:T(8,128)S(1)}, u32[]{:S(2)}, u32[]{:S(2)}) collective-permute-start(f32[4,72,256]{2,1,0:T(8,128)S(1)} %shard_map.96.refs_2_.refs_0_), channel_id=1, source_target_pairs={{0,2},{1,5},{2,0},{3,7},{4,6},{5,1},{6,4},{7,3},{8,10},{9,13},{10,... | collective-permute-start | bytes 884744 | tf_op jit(solution)/shard_map/ppermute | solution.py:327
  76.9 1.3 %collective-permute-done.35.refs_1_ = f32[4,64,256]{2,1,0:T(8,128)S(1)} collective-permute-done((f32[4,64,256]{2,1,0:T(8,128)S(1)}, f32[4,64,256]{2,1,0:T(8,128)S(1)}, u32[]{:S(2)}, u32[]{:S(2)}) %collective-permute-start.35) | collective-permute-done | bytes 262176 | tf_op jit(solution)/shard_map/ppermute | solution.py:327
  78.3 0.5 collective-permute-start.38
  78.9 1.1 %shard_map.99 = (f32[2,8,8,32,256]{4,3,2,1,0:T(8,128)}, f32[8,128]{1,0:T(8,128)S(1)}) custom-call(f32[8,64,256]{2,1,0:T(8,128)S(1)} %shard_map.95.refs_2_.refs_0_, f32[8,64,256]{2,1,0:T(8,128)S(1)} %collective-permute-done.33.refs_1_, f32[8,64,256]{2,1,0:T(8,128)S(1)} %shard_map.98.refs_2_.refs_1_), custom_call_target="tpu_custom_call" | custom-call | flops 10000000000 | bytes 1024 | tf_op jit(solution)/shard_map/pallas_call | solution.py:172
  80.0 0.2 collective-permute-done.37.refs_2_
  80.2 1.1 %shard_map.100 = (f32[2,8,8,32,256]{4,3,2,1,0:T(8,128)}, f32[8,128]{1,0:T(8,128)S(1)}) custom-call(f32[2,8,8,32,256]{4,3,2,1,0:T(8,128)} %get-tuple-element.108.refs_0_, f32[8,64,256]{2,1,0:T(8,128)S(1)} %shard_map.97.refs_2_.refs_1_, f32[8,64,256]{2,1,0:T(8,128)S(1)} %collective-permute-done.37.refs_2_, ...), custom_call_target="tpu_custom_call", output_to_operand_aliasing={{0}: (0, {})} | custom-call | flops 10000000000 | bytes 1024 | tf_op jit(solution)/shard_map/pallas_call | solution.py:172
  81.3 0.9 %collective-permute-done.39.refs_1_ = f32[4,72,256]{2,1,0:T(8,128)S(1)} collective-permute-done((f32[4,72,256]{2,1,0:T(8,128)S(1)}, f32[4,72,256]{2,1,0:T(8,128)S(1)}, u32[]{:S(2)}, u32[]{:S(2)}) %collective-permute-start.39) | collective-permute-done | bytes 294944 | tf_op jit(solution)/shard_map/ppermute | solution.py:327
  82.3 1.1 %shard_map.102 = (f32[2,8,8,32,256]{4,3,2,1,0:T(8,128)}, f32[8,128]{1,0:T(8,128)S(1)}) custom-call(f32[2,8,8,32,256]{4,3,2,1,0:T(8,128)} %get-tuple-element.110.refs_0_, f32[8,64,256]{2,1,0:T(8,128)S(1)} %shard_map.98.refs_2_.refs_1_, f32[8,64,256]{2,1,0:T(8,128)S(1)} %collective-permute-done.38.refs_2_, ...), custom_call_target="tpu_custom_call", output_to_operand_aliasing={{0}: (0, {})} | custom-call | flops 10000000000 | bytes 1024 | tf_op jit(solution)/shard_map/pallas_call | solution.py:172
  83.4 0.9 %collective-permute-done.40.refs_2_ = f32[8,72,256]{2,1,0:T(8,128)S(1)} collective-permute-done((f32[8,72,256]{2,1,0:T(8,128)S(1)}, f32[8,72,256]{2,1,0:T(8,128)S(1)}, u32[]{:S(2)}, u32[]{:S(2)}) %collective-permute-start.40) | collective-permute-done | bytes 589856 | tf_op jit(solution)/shard_map/ppermute | solution.py:327
  84.3 1.8 %shard_map.103 = (f32[2,8,8,32,256]{4,3,2,1,0:T(8,128)}, f32[2,64,256]{2,1,0:T(8,128)}) custom-call(f32[2,8,8,32,256]{4,3,2,1,0:T(8,128)} %get-tuple-element.112.refs_0_, f32[8,72,256]{2,1,0:T(8,128)S(1)} %shard_map.101.refs_3_.refs_1_, f32[8,72,256]{2,1,0:T(8,128)S(1)} %collective-permute-done.40.refs_2_, ...), custom_call_target="tpu_custom_call", output_to_operand_aliasing={{0}: (0, {})} | custom-call | flops 10000000000 | bytes 1024 | tf_op jit(solution)/shard_map/pallas_call | solution.py:172
  (63 shorter events, 1.3 us)
Async XLA Ops:
  3.7 3.2 %collective-permute-start = (f32[8,72,256]{2,1,0:T(8,128)S(1)}, f32[8,72,256]{2,1,0:T(8,128)S(1)}, u32[]{:S(2)}, u32[]{:S(2)}) collective-permute-start(f32[8,72,256]{2,1,0:T(8,128)S(1)} %get-tuple-element.60), channel_id=1, source_target_pairs={{0,1},{1,0},{2,3},{3,2},{4,5},{5,4},{6,7},{7,6},{8,9},{9,8},{10,11... | collective-permute-start | bytes 1769480 | tf_op jit(solution)/shard_map/ppermute | solution.py:327
  6.8 4.6 %collective-permute-start.3 = (f32[8,128,256]{2,1,0:T(8,128)S(1)}, f32[8,128,256]{2,1,0:T(8,128)S(1)}, u32[]{:S(2)}, u32[]{:S(2)}) collective-permute-start(f32[8,128,256]{2,1,0:T(8,128)S(1)} %get-tuple-element.63.refs_2_), channel_id=1, source_target_pairs={{0,1},{1,0},{2,3},{3,2},{4,5},{5,4},{6,7},{7,6},{8,9},{9,8},{10,11... | collective-permute-start | bytes 3145736 | tf_op jit(solution)/shard_map/ppermute | solution.py:327
  7.0 10.3 %collective-permute-start.1 = (f32[4,72,256]{2,1,0:T(8,128)S(1)}, f32[4,72,256]{2,1,0:T(8,128)S(1)}, u32[]{:S(2)}, u32[]{:S(2)}) collective-permute-start(f32[4,72,256]{2,1,0:T(8,128)S(1)} %get-tuple-element.65.refs_2_), channel_id=1, source_target_pairs={{0,8},{1,9},{2,10},{3,11},{4,12},{5,13},{6,14},{7,15},{8,0},{9,1},... | collective-permute-start | bytes 884744 | tf_op jit(solution)/shard_map/ppermute | solution.py:327
  11.3 4.6 %collective-permute-start.2 = (f32[8,64,256]{2,1,0:T(8,128)S(1)}, f32[8,64,256]{2,1,0:T(8,128)S(1)}, u32[]{:S(2)}, u32[]{:S(2)}) collective-permute-start(f32[8,64,256]{2,1,0:T(8,128)S(1)} %get-tuple-element.67.refs_2_), channel_id=1, source_target_pairs={{0,1},{1,0},{2,3},{3,2},{4,5},{5,4},{6,7},{7,6},{8,9},{9,8},{10,11... | collective-permute-start | bytes 1572872 | tf_op jit(solution)/shard_map/ppermute | solution.py:327
  11.6 11.0 %collective-permute-start.6 = (f32[4,128,256]{2,1,0:T(8,128)S(1)}, f32[4,128,256]{2,1,0:T(8,128)S(1)}, u32[]{:S(2)}, u32[]{:S(2)}) collective-permute-start(f32[4,128,256]{2,1,0:T(8,128)S(1)} %get-tuple-element.69.refs_2_), channel_id=1, source_target_pairs={{0,2},{1,5},{2,0},{3,7},{4,6},{5,1},{6,4},{7,3},{8,10},{9,13},{10,... | collective-permute-start | bytes 1572872 | tf_op jit(solution)/shard_map/ppermute | solution.py:327
  15.7 3.4 %collective-permute-start.7 = (f32[8,128,256]{2,1,0:T(8,128)S(1)}, f32[8,128,256]{2,1,0:T(8,128)S(1)}, u32[]{:S(2)}, u32[]{:S(2)}) collective-permute-start(f32[8,128,256]{2,1,0:T(8,128)S(1)} %get-tuple-element.70.refs_2_), channel_id=1, source_target_pairs={{0,1},{1,0},{2,3},{3,2},{4,5},{5,4},{6,7},{7,6},{8,9},{9,8},{10,11... | collective-permute-start | bytes 3145736 | tf_op jit(solution)/shard_map/ppermute | solution.py:327
  16.0 8.6 %collective-permute-start.5 = (f32[4,64,256]{2,1,0:T(8,128)S(1)}, f32[4,64,256]{2,1,0:T(8,128)S(1)}, u32[]{:S(2)}, u32[]{:S(2)}) collective-permute-start(f32[4,64,256]{2,1,0:T(8,128)S(1)} %get-tuple-element.71.refs_2_), channel_id=1, source_target_pairs={{0,8},{1,9},{2,10},{3,11},{4,12},{5,13},{6,14},{7,15},{8,0},{9,1},... | collective-permute-start | bytes 786440 | tf_op jit(solution)/shard_map/ppermute | solution.py:327
  17.3 8.6 %collective-permute-start.4 = (f32[2,72,256]{2,1,0:T(8,128)S(1)}, f32[2,72,256]{2,1,0:T(8,128)S(1)}, u32[]{:S(2)}, u32[]{:S(2)}) collective-permute-start(f32[2,72,256]{2,1,0:T(8,128)S(1)} %get-tuple-element.73.refs_2_), channel_id=1, source_target_pairs={{0,2},{1,5},{2,0},{3,7},{4,6},{5,1},{6,4},{7,3},{8,10},{9,13},{10,... | collective-permute-start | bytes 442376 | tf_op jit(solution)/shard_map/ppermute | solution.py:327
  19.2 9.3 %collective-permute-start.9 = (f32[4,128,256]{2,1,0:T(8,128)S(1)}, f32[4,128,256]{2,1,0:T(8,128)S(1)}, u32[]{:S(2)}, u32[]{:S(2)}) collective-permute-start(f32[4,128,256]{2,1,0:T(8,128)S(1)} %get-tuple-element.77.refs_2_), channel_id=1, source_target_pairs={{0,2},{1,5},{2,0},{3,7},{4,6},{5,1},{6,4},{7,3},{8,10},{9,13},{10,... | collective-permute-start | bytes 1572872 | tf_op jit(solution)/shard_map/ppermute | solution.py:327
  22.5 5.0 %collective-permute-start.10 = (f32[8,128,256]{2,1,0:T(8,128)S(1)}, f32[8,128,256]{2,1,0:T(8,128)S(1)}, u32[]{:S(2)}, u32[]{:S(2)}) collective-permute-start(f32[8,128,256]{2,1,0:T(8,128)S(1)} %get-tuple-element.78.refs_2_), channel_id=1, source_target_pairs={{0,1},{1,0},{2,3},{3,2},{4,5},{5,4},{6,7},{7,6},{8,9},{9,8},{10,11... | collective-permute-start | bytes 3145736 | tf_op jit(solution)/shard_map/ppermute | solution.py:327
  22.6 12.8 %collective-permute-start.15 = (f32[2,128,256]{2,1,0:T(8,128)S(1)}, f32[2,128,256]{2,1,0:T(8,128)S(1)}, u32[]{:S(2)}, u32[]{:S(2)}) collective-permute-start(f32[2,128,256]{2,1,0:T(8,128)S(1)} %get-tuple-element.79.refs_2_), channel_id=1, source_target_pairs={{0,8},{1,9},{2,10},{3,11},{4,12},{5,13},{6,14},{7,15},{8,0},{9,1},... | collective-permute-start | bytes 786440 | tf_op jit(solution)/shard_map/ppermute | solution.py:327
  24.6 9.0 %collective-permute-start.12 = (f32[2,64,256]{2,1,0:T(8,128)S(1)}, f32[2,64,256]{2,1,0:T(8,128)S(1)}, u32[]{:S(2)}, u32[]{:S(2)}) collective-permute-start(f32[2,64,256]{2,1,0:T(8,128)S(1)} %get-tuple-element.80.refs_2_), channel_id=1, source_target_pairs={{0,2},{1,5},{2,0},{3,7},{4,6},{5,1},{6,4},{7,3},{8,10},{9,13},{10,... | collective-permute-start | bytes 393224 | tf_op jit(solution)/shard_map/ppermute | solution.py:327
  25.9 5.0 %collective-permute-start.8 = (f32[1,72,256]{2,1,0:T(8,128)S(1)}, f32[1,72,256]{2,1,0:T(8,128)S(1)}, u32[]{:S(2)}, u32[]{:S(2)}) collective-permute-start(f32[1,72,256]{2,1,0:T(8,128)S(1)} %get-tuple-element.82.refs_2_), channel_id=1, source_target_pairs={{0,4},{1,3},{2,6},{3,1},{4,0},{5,7},{6,2},{7,5},{8,12},{9,11},{10,... | collective-permute-start | bytes 221192 | tf_op jit(solution)/shard_map/ppermute | solution.py:327
  27.6 10.9 %collective-permute-start.14 = (f32[4,128,256]{2,1,0:T(8,128)S(1)}, f32[4,128,256]{2,1,0:T(8,128)S(1)}, u32[]{:S(2)}, u32[]{:S(2)}) collective-permute-start(f32[4,128,256]{2,1,0:T(8,128)S(1)} %get-tuple-element.85.refs_2_), channel_id=1, source_target_pairs={{0,2},{1,5},{2,0},{3,7},{4,6},{5,1},{6,4},{7,3},{8,10},{9,13},{10,... | collective-permute-start | bytes 1572872 | tf_op jit(solution)/shard_map/ppermute | solution.py:327
  28.6 14.4 %collective-permute-start.18 = (f32[2,128,256]{2,1,0:T(8,128)S(1)}, f32[2,128,256]{2,1,0:T(8,128)S(1)}, u32[]{:S(2)}, u32[]{:S(2)}) collective-permute-start(f32[2,128,256]{2,1,0:T(8,128)S(1)} %get-tuple-element.86.refs_2_), channel_id=1, source_target_pairs={{0,8},{1,9},{2,10},{3,11},{4,12},{5,13},{6,14},{7,15},{8,0},{9,1},... | collective-permute-start | bytes 786440 | tf_op jit(solution)/shard_map/ppermute | solution.py:327
  30.9 16.3 %collective-permute-start.11 = (f32[1,72,256]{2,1,0:T(8,128)S(1)}, f32[1,72,256]{2,1,0:T(8,128)S(1)}, u32[]{:S(2)}, u32[]{:S(2)}) collective-permute-start(f32[1,72,256]{2,1,0:T(8,128)S(1)} %shard_map.74.refs_2_.refs_0_), channel_id=1, source_target_pairs={{0,16},{1,17},{2,18},{3,19},{4,20},{5,21},{6,22},{7,23},{8,24},{9,... | collective-permute-start | bytes 221192 | tf_op jit(solution)/shard_map/ppermute | solution.py:327
  33.6 6.3 %collective-permute-start.13 = (f32[1,64,256]{2,1,0:T(8,128)S(1)}, f32[1,64,256]{2,1,0:T(8,128)S(1)}, u32[]{:S(2)}, u32[]{:S(2)}) collective-permute-start(f32[1,64,256]{2,1,0:T(8,128)S(1)} %get-tuple-element.89.refs_2_), channel_id=1, source_target_pairs={{0,4},{1,3},{2,6},{3,1},{4,0},{5,7},{6,2},{7,5},{8,12},{9,11},{10,... | collective-permute-start | bytes 196616 | tf_op jit(solution)/shard_map/ppermute | solution.py:327
  35.5 7.3 %collective-permute-start.19 = (f32[1,128,256]{2,1,0:T(8,128)S(1)}, f32[1,128,256]{2,1,0:T(8,128)S(1)}, u32[]{:S(2)}, u32[]{:S(2)}) collective-permute-start(f32[1,128,256]{2,1,0:T(8,128)S(1)} %get-tuple-element.92.refs_2_), channel_id=1, source_target_pairs={{0,4},{1,3},{2,6},{3,1},{4,0},{5,7},{6,2},{7,5},{8,12},{9,11},{10,... | collective-permute-start | bytes 393224 | tf_op jit(solution)/shard_map/ppermute | solution.py:327
  38.5 6.4 %collective-permute-start.17 = (f32[2,128,256]{2,1,0:T(8,128)S(1)}, f32[2,128,256]{2,1,0:T(8,128)S(1)}, u32[]{:S(2)}, u32[]{:S(2)}) collective-permute-start(f32[2,128,256]{2,1,0:T(8,128)S(1)} %get-tuple-element.93.refs_2_), channel_id=1, source_target_pairs={{0,4},{1,3},{2,6},{3,1},{4,0},{5,7},{6,2},{7,5},{8,12},{9,11},{10,... | collective-permute-start | bytes 786440 | tf_op jit(solution)/shard_map/ppermute | solution.py:327
  39.9 7.3 %collective-permute-start.16 = (f32[1,64,256]{2,1,0:T(8,128)S(1)}, f32[1,64,256]{2,1,0:T(8,128)S(1)}, u32[]{:S(2)}, u32[]{:S(2)}) collective-permute-start(f32[1,64,256]{2,1,0:T(8,128)S(1)} %shard_map.78.refs_2_), channel_id=1, source_target_pairs={{0,16},{1,17},{2,18},{3,19},{4,20},{5,21},{6,22},{7,23},{8,24},{9,... | collective-permute-start | bytes 196616 | tf_op jit(solution)/shard_map/ppermute | solution.py:327
  42.7 12.3 %collective-permute-start.24 = (f32[1,128,256]{2,1,0:T(8,128)S(1)}, f32[1,128,256]{2,1,0:T(8,128)S(1)}, u32[]{:S(2)}, u32[]{:S(2)}) collective-permute-start(f32[1,128,256]{2,1,0:T(8,128)S(1)} %shard_map.79.refs_2_.refs_0_), channel_id=1, source_target_pairs={{0,16},{1,17},{2,18},{3,19},{4,20},{5,21},{6,22},{7,23},{8,24},{9,... | collective-permute-start | bytes 393224 | tf_op jit(solution)/shard_map/ppermute | solution.py:327
  43.0 6.3 %collective-permute-start.21 = (f32[1,128,256]{2,1,0:T(8,128)S(1)}, f32[1,128,256]{2,1,0:T(8,128)S(1)}, u32[]{:S(2)}, u32[]{:S(2)}) collective-permute-start(f32[1,128,256]{2,1,0:T(8,128)S(1)} %get-tuple-element.97.refs_2_), channel_id=1, source_target_pairs={{0,4},{1,3},{2,6},{3,1},{4,0},{5,7},{6,2},{7,5},{8,12},{9,11},{10,... | collective-permute-start | bytes 393224 | tf_op jit(solution)/shard_map/ppermute | solution.py:327
  45.0 11.5 %collective-permute-start.23 = (f32[1,128,256]{2,1,0:T(8,128)S(1)}, f32[1,128,256]{2,1,0:T(8,128)S(1)}, u32[]{:S(2)}, u32[]{:S(2)}) collective-permute-start(f32[1,128,256]{2,1,0:T(8,128)S(1)} %get-tuple-element.98.refs_4_), channel_id=1, source_target_pairs={{0,8},{1,9},{2,10},{3,11},{4,12},{5,13},{6,14},{7,15},{8,0},{9,1},... | collective-permute-start | bytes 393224 | tf_op jit(solution)/shard_map/ppermute | solution.py:327
  47.3 4.9 %collective-permute-start.20 = (f32[1,64,256]{2,1,0:T(8,128)S(1)}, f32[1,64,256]{2,1,0:T(8,128)S(1)}, u32[]{:S(2)}, u32[]{:S(2)}) collective-permute-start(f32[1,64,256]{2,1,0:T(8,128)S(1)} %get-tuple-element.99.refs_0_), channel_id=1, source_target_pairs={{0,4},{1,3},{2,6},{3,1},{4,0},{5,7},{6,2},{7,5},{8,12},{9,11},{10,... | collective-permute-start | bytes 196616 | tf_op jit(solution)/shard_map/ppermute | solution.py:327
  49.4 9.6 %collective-permute-start.26 = (f32[1,128,256]{2,1,0:T(8,128)S(1)}, f32[1,128,256]{2,1,0:T(8,128)S(1)}, u32[]{:S(2)}, u32[]{:S(2)}) collective-permute-start(f32[1,128,256]{2,1,0:T(8,128)S(1)} %shard_map.83.refs_2_.refs_0_), channel_id=1, source_target_pairs={{0,16},{1,17},{2,18},{3,19},{4,20},{5,21},{6,22},{7,23},{8,24},{9,... | collective-permute-start | bytes 393224 | tf_op jit(solution)/shard_map/ppermute | solution.py:327
  52.2 14.4 %collective-permute-start.22 = (f32[2,64,256]{2,1,0:T(8,128)S(1)}, f32[2,64,256]{2,1,0:T(8,128)S(1)}, u32[]{:S(2)}, u32[]{:S(2)}) collective-permute-start(f32[2,64,256]{2,1,0:T(8,128)S(1)} %shard_map.84.refs_4_.refs_0_), channel_id=1, source_target_pairs={{0,8},{1,9},{2,10},{3,11},{4,12},{5,13},{6,14},{7,15},{8,0},{9,1},... | collective-permute-start | bytes 393224 | tf_op jit(solution)/shard_map/ppermute | solution.py:327
  55.1 5.8 %collective-permute-start.28 = (f32[1,64,256]{2,1,0:T(8,128)S(1)}, f32[1,64,256]{2,1,0:T(8,128)S(1)}, u32[]{:S(2)}, u32[]{:S(2)}) collective-permute-start(f32[1,64,256]{2,1,0:T(8,128)S(1)} %get-tuple-element.107.refs_0_), channel_id=1, source_target_pairs={{0,4},{1,3},{2,6},{3,1},{4,0},{5,7},{6,2},{7,5},{8,12},{9,11},{10,... | collective-permute-start | bytes 196616 | tf_op jit(solution)/shard_map/ppermute | solution.py:327
  56.5 9.1 %collective-permute-start.25 = (f32[1,128,256]{2,1,0:T(8,128)S(1)}, f32[1,128,256]{2,1,0:T(8,128)S(1)}, u32[]{:S(2)}, u32[]{:S(2)}) collective-permute-start(f32[1,128,256]{2,1,0:T(8,128)S(1)} %shard_map.86.refs_4_.refs_0_), channel_id=1, source_target_pairs={{0,16},{1,17},{2,18},{3,19},{4,20},{5,21},{6,22},{7,23},{8,24},{9,... | collective-permute-start | bytes 393224 | tf_op jit(solution)/shard_map/ppermute | solution.py:327
  59.1 5.1 %collective-permute-start.27 = (f32[1,64,256]{2,1,0:T(8,128)S(1)}, f32[1,64,256]{2,1,0:T(8,128)S(1)}, u32[]{:S(2)}, u32[]{:S(2)}) collective-permute-start(f32[1,64,256]{2,1,0:T(8,128)S(1)} %get-tuple-element.106.refs_0_), channel_id=1, source_target_pairs={{0,4},{1,3},{2,6},{3,1},{4,0},{5,7},{6,2},{7,5},{8,12},{9,11},{10,... | collective-permute-start | bytes 196616 | tf_op jit(solution)/shard_map/ppermute | solution.py:327
  61.0 10.7 %collective-permute-start.30 = (f32[2,64,256]{2,1,0:T(8,128)S(1)}, f32[2,64,256]{2,1,0:T(8,128)S(1)}, u32[]{:S(2)}, u32[]{:S(2)}) collective-permute-start(f32[2,64,256]{2,1,0:T(8,128)S(1)} %shard_map.88.refs_2_.refs_0_), channel_id=1, source_target_pairs={{0,8},{1,9},{2,10},{3,11},{4,12},{5,13},{6,14},{7,15},{8,0},{9,1},... | collective-permute-start | bytes 393224 | tf_op jit(solution)/shard_map/ppermute | solution.py:327
  64.2 5.0 %collective-permute-start.32 = (f32[2,64,256]{2,1,0:T(8,128)S(1)}, f32[2,64,256]{2,1,0:T(8,128)S(1)}, u32[]{:S(2)}, u32[]{:S(2)}) collective-permute-start(f32[2,64,256]{2,1,0:T(8,128)S(1)} %shard_map.89.refs_4_.refs_0_), channel_id=1, source_target_pairs={{0,2},{1,5},{2,0},{3,7},{4,6},{5,1},{6,4},{7,3},{8,10},{9,13},{10,... | collective-permute-start | bytes 393224 | tf_op jit(solution)/shard_map/ppermute | solution.py:327
  65.7 4.4 %collective-permute-start.31 = (f32[1,72,256]{2,1,0:T(8,128)S(1)}, f32[1,72,256]{2,1,0:T(8,128)S(1)}, u32[]{:S(2)}, u32[]{:S(2)}) collective-permute-start(f32[1,72,256]{2,1,0:T(8,128)S(1)} %shard_map.90.refs_2_.refs_0_), channel_id=1, source_target_pairs={{0,8},{1,9},{2,10},{3,11},{4,12},{5,13},{6,14},{7,15},{8,0},{9,1},... | collective-permute-start | bytes 221192 | tf_op jit(solution)/shard_map/ppermute | solution.py:327
  66.6 7.2 %collective-permute-start.29 = (f32[4,64,256]{2,1,0:T(8,128)S(1)}, f32[4,64,256]{2,1,0:T(8,128)S(1)}, u32[]{:S(2)}, u32[]{:S(2)}) collective-permute-start(f32[4,64,256]{2,1,0:T(8,128)S(1)} %shard_map.91.refs_2_.refs_0_), channel_id=1, source_target_pairs={{0,2},{1,5},{2,0},{3,7},{4,6},{5,1},{6,4},{7,3},{8,10},{9,13},{10,... | collective-permute-start | bytes 786440 | tf_op jit(solution)/shard_map/ppermute | solution.py:327
  69.2 9.1 %collective-permute-start.34 = (f32[4,64,256]{2,1,0:T(8,128)S(1)}, f32[4,64,256]{2,1,0:T(8,128)S(1)}, u32[]{:S(2)}, u32[]{:S(2)}) collective-permute-start(f32[4,64,256]{2,1,0:T(8,128)S(1)} %shard_map.92.refs_2_.refs_0_), channel_id=1, source_target_pairs={{0,8},{1,9},{2,10},{3,11},{4,12},{5,13},{6,14},{7,15},{8,0},{9,1},... | collective-permute-start | bytes 786440 | tf_op jit(solution)/shard_map/ppermute | solution.py:327
  70.2 5.2 %collective-permute-start.36 = (f32[2,72,256]{2,1,0:T(8,128)S(1)}, f32[2,72,256]{2,1,0:T(8,128)S(1)}, u32[]{:S(2)}, u32[]{:S(2)}) collective-permute-start(f32[2,72,256]{2,1,0:T(8,128)S(1)} %shard_map.93.refs_2_.refs_0_), channel_id=1, source_target_pairs={{0,4},{1,3},{2,6},{3,1},{4,0},{5,7},{6,2},{7,5},{8,12},{9,11},{10,... | collective-permute-start | bytes 442376 | tf_op jit(solution)/shard_map/ppermute | solution.py:327
  71.7 6.4 %collective-permute-start.35 = (f32[4,64,256]{2,1,0:T(8,128)S(1)}, f32[4,64,256]{2,1,0:T(8,128)S(1)}, u32[]{:S(2)}, u32[]{:S(2)}) collective-permute-start(f32[4,64,256]{2,1,0:T(8,128)S(1)} %shard_map.94.refs_2_.refs_0_), channel_id=1, source_target_pairs={{0,2},{1,5},{2,0},{3,7},{4,6},{5,1},{6,4},{7,3},{8,10},{9,13},{10,... | collective-permute-start | bytes 786440 | tf_op jit(solution)/shard_map/ppermute | solution.py:327
  73.8 5.1 %collective-permute-start.33 = (f32[8,64,256]{2,1,0:T(8,128)S(1)}, f32[8,64,256]{2,1,0:T(8,128)S(1)}, u32[]{:S(2)}, u32[]{:S(2)}) collective-permute-start(f32[8,64,256]{2,1,0:T(8,128)S(1)} %shard_map.95.refs_2_.refs_0_), channel_id=1, source_target_pairs={{0,1},{1,0},{2,3},{3,2},{4,5},{5,4},{6,7},{7,6},{8,9},{9,8},{10,11... | collective-permute-start | bytes 1572872 | tf_op jit(solution)/shard_map/ppermute | solution.py:327
  75.4 6.8 %collective-permute-start.39 = (f32[4,72,256]{2,1,0:T(8,128)S(1)}, f32[4,72,256]{2,1,0:T(8,128)S(1)}, u32[]{:S(2)}, u32[]{:S(2)}) collective-permute-start(f32[4,72,256]{2,1,0:T(8,128)S(1)} %shard_map.96.refs_2_.refs_0_), channel_id=1, source_target_pairs={{0,2},{1,5},{2,0},{3,7},{4,6},{5,1},{6,4},{7,3},{8,10},{9,13},{10,... | collective-permute-start | bytes 884744 | tf_op jit(solution)/shard_map/ppermute | solution.py:327
  78.2 2.0 %collective-permute-start.37 = (f32[8,64,256]{2,1,0:T(8,128)S(1)}, f32[8,64,256]{2,1,0:T(8,128)S(1)}, u32[]{:S(2)}, u32[]{:S(2)}) collective-permute-start(f32[8,64,256]{2,1,0:T(8,128)S(1)} %shard_map.97.refs_2_.refs_1_), channel_id=1, source_target_pairs={{0,1},{1,0},{2,3},{3,2},{4,5},{5,4},{6,7},{7,6},{8,9},{9,8},{10,11... | collective-permute-start | bytes 1572872 | tf_op jit(solution)/shard_map/ppermute | solution.py:327
  78.3 4.0 %collective-permute-start.38 = (f32[8,64,256]{2,1,0:T(8,128)S(1)}, f32[8,64,256]{2,1,0:T(8,128)S(1)}, u32[]{:S(2)}, u32[]{:S(2)}) collective-permute-start(f32[8,64,256]{2,1,0:T(8,128)S(1)} %shard_map.98.refs_2_.refs_1_), channel_id=1, source_target_pairs={{0,1},{1,0},{2,3},{3,2},{4,5},{5,4},{6,7},{7,6},{8,9},{9,8},{10,11... | collective-permute-start | bytes 1572872 | tf_op jit(solution)/shard_map/ppermute | solution.py:327
  82.2 2.1 %collective-permute-start.40 = (f32[8,72,256]{2,1,0:T(8,128)S(1)}, f32[8,72,256]{2,1,0:T(8,128)S(1)}, u32[]{:S(2)}, u32[]{:S(2)}) collective-permute-start(f32[8,72,256]{2,1,0:T(8,128)S(1)} %shard_map.101.refs_3_.refs_1_), channel_id=1, source_target_pairs={{0,1},{1,0},{2,3},{3,2},{4,5},{5,4},{6,7},{7,6},{8,9},{9,8},{10,11... | collective-permute-start | bytes 1769480 | tf_op jit(solution)/shard_map/ppermute | solution.py:327

commit v6 on v5

--- a/solution.py
+++ b/solution.py
@@ -353,7 +353,7 @@
     def histogram(c):
         halves = [f32(plan.items, depth(c), features)] * 2
         if c == 0:
-            blocks = 8
+            blocks = 2
             keep, send, bins, spread = chain(
                 functools.partial(first_kernel, plan, plan.halve[c], sizes[c], blocks),
                 [

time: 86.3 us -> 86.3 us (level)
  no operation moved by 1% of the time
where the time goes in v6:
time: 86.3 us; the launch traced here: 86.1 us
  starting transfers between devices  51.2 us (59%)
  Pallas kernels  18.6 us (22%)
  waiting for transfers between devices  15.4 us (18%)
  between operations  0.93 us (1%)
    ppermute x41, starting transfers between devices, swap(): return lax.ppermute(x, 'dp', [(d, partner(d)) for d in range(devices)])  51.2 us
    pallas_call x45, Pallas kernels, __call__(): pl.pallas_call(run, out_shape=out_shape, in_specs=in_specs, out_specs=out...  18.6 us
    ppermute x41, waiting for transfers between devices, swap(): return lax.ppermute(x, 'dp', [(d, partner(d)) for d in range(devices)])  15.4 us
  transfers between devices with their start and end apart: 41, of which 13 were waited for; matrix products, arithmetic and copies ran while one was open for 0% of the time, Pallas kernels for 16%

profile of v6, /device:TPU:0, one launch (start us, length us, event | category | flops | bytes accessed | tf_op | source)
XLA Modules:
  0.0 86.1 jit_solution(16585460316056592527)
XLA Ops:
  0.6 3.1 %shard_map.59 = (f32[8,72,256]{2,1,0:T(8,128)S(1)}, f32[8,72,256]{2,1,0:T(8,128)S(1)}, bf16[2048,256]{1,0:T(8,128)(2,1)S(1)}, bf16[128,2048]{1,0:T(8,128)(2,1)S(1)}) custom-call(s32[2048,256]{1,0:T(8,128)} %refs_0_.1, s32[1,2048]{1,0:T(1,128)} %bitcast.9, bf16[32,2048]{1,0:T(8,128)(2,1)} %bitcast.7, bf16[32,2048]{1,0:T(8,128)(2,1)} %bitcast.8), custom_call_target="tpu_custom_call" | custom-call | flops 10000000000 | bytes 1024 | tf_op jit(solution)/shard_map/pallas_call | solution.py:172
  3.7 0.5 collective-permute-start
  4.2 2.5 %shard_map.60 = (f32[8,128,256]{2,1,0:T(8,128)S(1)}, f32[8,128,256]{2,1,0:T(8,128)S(1)}) custom-call(bf16[2048,256]{1,0:T(8,128)(2,1)S(1)} %get-tuple-element.61.refs_0_, bf16[128,2048]{1,0:T(8,128)(2,1)S(1)} %get-tuple-element.62.refs_1_.refs_2_, bf16[128,2048]{1,0:T(8,128)(2,1)S(1)} %get-tuple-element.62.refs_1_.refs_2_), custom_call_target="tpu_custom_call" | custom-call | flops 10000000000 | bytes 1024 | tf_op jit(solution)/shard_map/pallas_call | solution.py:172
  6.8 0.1 collective-permute-start.3
  7.0 3.1 %collective-permute-start.1 = (f32[4,72,256]{2,1,0:T(8,128)S(1)}, f32[4,72,256]{2,1,0:T(8,128)S(1)}, u32[]{:S(2)}, u32[]{:S(2)}) collective-permute-start(f32[4,72,256]{2,1,0:T(8,128)S(1)} %get-tuple-element.65.refs_2_), channel_id=1, source_target_pairs={{0,8},{1,9},{2,10},{3,11},{4,12},{5,13},{6,14},{7,15},{8,0},{9,1},... | collective-permute-start | bytes 884744 | tf_op jit(solution)/shard_map/ppermute | solution.py:327
  10.1 1.3 %shard_map.62 = (f32[8,64,256]{2,1,0:T(8,128)S(1)}, f32[8,64,256]{2,1,0:T(8,128)S(1)}) custom-call(bf16[2048,256]{1,0:T(8,128)(2,1)S(1)} %get-tuple-element.61.refs_0_, bf16[128,2048]{1,0:T(8,128)(2,1)S(1)} %get-tuple-element.62.refs_1_.refs_2_, f32[4,72,256]{2,1,0:T(8,128)S(1)} %get-tuple-element.65.refs_2_), custom_call_target="tpu_custom_call" | custom-call | flops 10000000000 | bytes 1024 | tf_op jit(solution)/shard_map/pallas_call | solution.py:172
  11.4 0.1 shard_map.63
  11.5 1.6 %collective-permute-start.6 = (f32[4,128,256]{2,1,0:T(8,128)S(1)}, f32[4,128,256]{2,1,0:T(8,128)S(1)}, u32[]{:S(2)}, u32[]{:S(2)}) collective-permute-start(f32[4,128,256]{2,1,0:T(8,128)S(1)} %get-tuple-element.69.refs_2_), channel_id=1, source_target_pairs={{0,2},{1,5},{2,0},{3,7},{4,6},{5,1},{6,4},{7,3},{8,10},{9,13},{10,... | collective-permute-start | bytes 1572872 | tf_op jit(solution)/shard_map/ppermute | solution.py:327
  13.1 2.5 %shard_map.64 = (f32[8,128,256]{2,1,0:T(8,128)S(1)}, f32[8,128,256]{2,1,0:T(8,128)S(1)}) custom-call(bf16[2048,256]{1,0:T(8,128)(2,1)S(1)} %get-tuple-element.61.refs_0_, bf16[128,2048]{1,0:T(8,128)(2,1)S(1)} %get-tuple-element.62.refs_1_.refs_2_, f32[4,128,256]{2,1,0:T(8,128)S(1)} %get-tuple-element.69.refs_2_), custom_call_target="tpu_custom_call" | custom-call | flops 10000000000 | bytes 1024 | tf_op jit(solution)/shard_map/pallas_call | solution.py:172
  15.6 0.3 collective-permute-start.7
  16.0 0.7 collective-permute-start.5
  16.8 0.5 collective-permute-done.1.refs_1_
  17.3 1.7 %collective-permute-start.4 = (f32[2,72,256]{2,1,0:T(8,128)S(1)}, f32[2,72,256]{2,1,0:T(8,128)S(1)}, u32[]{:S(2)}, u32[]{:S(2)}) collective-permute-start(f32[2,72,256]{2,1,0:T(8,128)S(1)} %get-tuple-element.73.refs_2_), channel_id=1, source_target_pairs={{0,2},{1,5},{2,0},{3,7},{4,6},{5,1},{6,4},{7,3},{8,10},{9,13},{10,... | collective-permute-start | bytes 442376 | tf_op jit(solution)/shard_map/ppermute | solution.py:327
  19.0 0.1 shard_map.67
  19.2 0.8 collective-permute-start.9
  19.9 2.5 %shard_map.68 = (f32[8,128,256]{2,1,0:T(8,128)S(1)}, f32[8,128,256]{2,1,0:T(8,128)S(1)}) custom-call(bf16[2048,256]{1,0:T(8,128)(2,1)S(1)} %get-tuple-element.61.refs_0_, bf16[128,2048]{1,0:T(8,128)(2,1)S(1)} %get-tuple-element.62.refs_1_.refs_2_, f32[4,128,256]{2,1,0:T(8,128)S(1)} %get-tuple-element.77.refs_2_), custom_call_target="tpu_custom_call" | custom-call | flops 10000000000 | bytes 1024 | tf_op jit(solution)/shard_map/pallas_call | solution.py:172
  22.6 1.5 %collective-permute-start.15 = (f32[2,128,256]{2,1,0:T(8,128)S(1)}, f32[2,128,256]{2,1,0:T(8,128)S(1)}, u32[]{:S(2)}, u32[]{:S(2)}) collective-permute-start(f32[2,128,256]{2,1,0:T(8,128)S(1)} %get-tuple-element.79.refs_2_), channel_id=1, source_target_pairs={{0,8},{1,9},{2,10},{3,11},{4,12},{5,13},{6,14},{7,15},{8,0},{9,1},... | collective-permute-start | bytes 786440 | tf_op jit(solution)/shard_map/ppermute | solution.py:327
  24.1 0.5 collective-permute-done.5.refs_1_
  24.6 1.3 %collective-permute-start.12 = (f32[2,64,256]{2,1,0:T(8,128)S(1)}, f32[2,64,256]{2,1,0:T(8,128)S(1)}, u32[]{:S(2)}, u32[]{:S(2)}) collective-permute-start(f32[2,64,256]{2,1,0:T(8,128)S(1)} %get-tuple-element.80.refs_2_), channel_id=1, source_target_pairs={{0,2},{1,5},{2,0},{3,7},{4,6},{5,1},{6,4},{7,3},{8,10},{9,13},{10,... | collective-permute-start | bytes 393224 | tf_op jit(solution)/shard_map/ppermute | solution.py:327
  25.9 1.5 %collective-permute-start.8 = (f32[1,72,256]{2,1,0:T(8,128)S(1)}, f32[1,72,256]{2,1,0:T(8,128)S(1)}, u32[]{:S(2)}, u32[]{:S(2)}) collective-permute-start(f32[1,72,256]{2,1,0:T(8,128)S(1)} %get-tuple-element.82.refs_2_), channel_id=1, source_target_pairs={{0,4},{1,3},{2,6},{3,1},{4,0},{5,7},{6,2},{7,5},{8,12},{9,11},{10,... | collective-permute-start | bytes 221192 | tf_op jit(solution)/shard_map/ppermute | solution.py:327
  27.5 0.1 shard_map.72
  27.6 0.9 %collective-permute-start.14 = (f32[4,128,256]{2,1,0:T(8,128)S(1)}, f32[4,128,256]{2,1,0:T(8,128)S(1)}, u32[]{:S(2)}, u32[]{:S(2)}) collective-permute-start(f32[4,128,256]{2,1,0:T(8,128)S(1)} %get-tuple-element.85.refs_2_), channel_id=1, source_target_pairs={{0,2},{1,5},{2,0},{3,7},{4,6},{5,1},{6,4},{7,3},{8,10},{9,13},{10,... | collective-permute-start | bytes 1572872 | tf_op jit(solution)/shard_map/ppermute | solution.py:327
  28.5 2.4 %collective-permute-start.18 = (f32[2,128,256]{2,1,0:T(8,128)S(1)}, f32[2,128,256]{2,1,0:T(8,128)S(1)}, u32[]{:S(2)}, u32[]{:S(2)}) collective-permute-start(f32[2,128,256]{2,1,0:T(8,128)S(1)} %get-tuple-element.86.refs_2_), channel_id=1, source_target_pairs={{0,8},{1,9},{2,10},{3,11},{4,12},{5,13},{6,14},{7,15},{8,0},{9,1},... | collective-permute-start | bytes 786440 | tf_op jit(solution)/shard_map/ppermute | solution.py:327
  30.9 2.6 %collective-permute-start.11 = (f32[1,72,256]{2,1,0:T(8,128)S(1)}, f32[1,72,256]{2,1,0:T(8,128)S(1)}, u32[]{:S(2)}, u32[]{:S(2)}) collective-permute-start(f32[1,72,256]{2,1,0:T(8,128)S(1)} %shard_map.74.refs_2_.refs_0_), channel_id=1, source_target_pairs={{0,16},{1,17},{2,18},{3,19},{4,20},{5,21},{6,22},{7,23},{8,24},{9,... | collective-permute-start | bytes 221192 | tf_op jit(solution)/shard_map/ppermute | solution.py:327
  33.6 1.8 %collective-permute-start.13 = (f32[1,64,256]{2,1,0:T(8,128)S(1)}, f32[1,64,256]{2,1,0:T(8,128)S(1)}, u32[]{:S(2)}, u32[]{:S(2)}) collective-permute-start(f32[1,64,256]{2,1,0:T(8,128)S(1)} %get-tuple-element.89.refs_2_), channel_id=1, source_target_pairs={{0,4},{1,3},{2,6},{3,1},{4,0},{5,7},{6,2},{7,5},{8,12},{9,11},{10,... | collective-permute-start | bytes 196616 | tf_op jit(solution)/shard_map/ppermute | solution.py:327
  35.5 0.3 collective-permute-start.19
  35.8 2.7 %collective-permute-done.14.refs_1_ = f32[4,128,256]{2,1,0:T(8,128)S(1)} collective-permute-done((f32[4,128,256]{2,1,0:T(8,128)S(1)}, f32[4,128,256]{2,1,0:T(8,128)S(1)}, u32[]{:S(2)}, u32[]{:S(2)}) %collective-permute-start.14) | collective-permute-done | bytes 524320 | tf_op jit(solution)/shard_map/ppermute | solution.py:327
  38.5 1.4 %collective-permute-start.17 = (f32[2,128,256]{2,1,0:T(8,128)S(1)}, f32[2,128,256]{2,1,0:T(8,128)S(1)}, u32[]{:S(2)}, u32[]{:S(2)}) collective-permute-start(f32[2,128,256]{2,1,0:T(8,128)S(1)} %get-tuple-element.93.refs_2_), channel_id=1, source_target_pairs={{0,4},{1,3},{2,6},{3,1},{4,0},{5,7},{6,2},{7,5},{8,12},{9,11},{10,... | collective-permute-start | bytes 786440 | tf_op jit(solution)/shard_map/ppermute | solution.py:327
  39.9 2.8 %collective-permute-start.16 = (f32[1,64,256]{2,1,0:T(8,128)S(1)}, f32[1,64,256]{2,1,0:T(8,128)S(1)}, u32[]{:S(2)}, u32[]{:S(2)}) collective-permute-start(f32[1,64,256]{2,1,0:T(8,128)S(1)} %shard_map.78.refs_2_), channel_id=1, source_target_pairs={{0,16},{1,17},{2,18},{3,19},{4,20},{5,21},{6,22},{7,23},{8,24},{9,... | collective-permute-start | bytes 196616 | tf_op jit(solution)/shard_map/ppermute | solution.py:327
  42.7 0.2 collective-permute-start.24
  43.0 1.0 %collective-permute-start.21 = (f32[1,128,256]{2,1,0:T(8,128)S(1)}, f32[1,128,256]{2,1,0:T(8,128)S(1)}, u32[]{:S(2)}, u32[]{:S(2)}) collective-permute-start(f32[1,128,256]{2,1,0:T(8,128)S(1)} %get-tuple-element.97.refs_2_), channel_id=1, source_target_pairs={{0,4},{1,3},{2,6},{3,1},{4,0},{5,7},{6,2},{7,5},{8,12},{9,11},{10,... | collective-permute-start | bytes 393224 | tf_op jit(solution)/shard_map/ppermute | solution.py:327
  44.0 1.0 %collective-permute-done.17.refs_1_ = f32[2,128,256]{2,1,0:T(8,128)S(1)} collective-permute-done((f32[2,128,256]{2,1,0:T(8,128)S(1)}, f32[2,128,256]{2,1,0:T(8,128)S(1)}, u32[]{:S(2)}, u32[]{:S(2)}) %collective-permute-start.17) | collective-permute-done | bytes 262176 | tf_op jit(solution)/shard_map/ppermute | solution.py:327
  45.0 2.2 %collective-permute-start.23 = (f32[1,128,256]{2,1,0:T(8,128)S(1)}, f32[1,128,256]{2,1,0:T(8,128)S(1)}, u32[]{:S(2)}, u32[]{:S(2)}) collective-permute-start(f32[1,128,256]{2,1,0:T(8,128)S(1)} %get-tuple-element.98.refs_4_), channel_id=1, source_target_pairs={{0,8},{1,9},{2,10},{3,11},{4,12},{5,13},{6,14},{7,15},{8,0},{9,1},... | collective-permute-start | bytes 393224 | tf_op jit(solution)/shard_map/ppermute | solution.py:327
  47.2 0.1 shard_map.82
  47.3 2.1 %collective-permute-start.20 = (f32[1,64,256]{2,1,0:T(8,128)S(1)}, f32[1,64,256]{2,1,0:T(8,128)S(1)}, u32[]{:S(2)}, u32[]{:S(2)}) collective-permute-start(f32[1,64,256]{2,1,0:T(8,128)S(1)} %get-tuple-element.99.refs_0_), channel_id=1, source_target_pairs={{0,4},{1,3},{2,6},{3,1},{4,0},{5,7},{6,2},{7,5},{8,12},{9,11},{10,... | collective-permute-start | bytes 196616 | tf_op jit(solution)/shard_map/ppermute | solution.py:327
  49.4 2.7 %collective-permute-start.26 = (f32[1,128,256]{2,1,0:T(8,128)S(1)}, f32[1,128,256]{2,1,0:T(8,128)S(1)}, u32[]{:S(2)}, u32[]{:S(2)}) collective-permute-start(f32[1,128,256]{2,1,0:T(8,128)S(1)} %shard_map.83.refs_2_.refs_0_), channel_id=1, source_target_pairs={{0,16},{1,17},{2,18},{3,19},{4,20},{5,21},{6,22},{7,23},{8,24},{9,... | collective-permute-start | bytes 393224 | tf_op jit(solution)/shard_map/ppermute | solution.py:327
  52.2 2.8 %collective-permute-start.22 = (f32[2,64,256]{2,1,0:T(8,128)S(1)}, f32[2,64,256]{2,1,0:T(8,128)S(1)}, u32[]{:S(2)}, u32[]{:S(2)}) collective-permute-start(f32[2,64,256]{2,1,0:T(8,128)S(1)} %shard_map.84.refs_4_.refs_0_), channel_id=1, source_target_pairs={{0,8},{1,9},{2,10},{3,11},{4,12},{5,13},{6,14},{7,15},{8,0},{9,1},... | collective-permute-start | bytes 393224 | tf_op jit(solution)/shard_map/ppermute | solution.py:327
  55.0 0.1 shard_map.85
  55.1 1.4 %collective-permute-start.28 = (f32[1,64,256]{2,1,0:T(8,128)S(1)}, f32[1,64,256]{2,1,0:T(8,128)S(1)}, u32[]{:S(2)}, u32[]{:S(2)}) collective-permute-start(f32[1,64,256]{2,1,0:T(8,128)S(1)} %get-tuple-element.107.refs_0_), channel_id=1, source_target_pairs={{0,4},{1,3},{2,6},{3,1},{4,0},{5,7},{6,2},{7,5},{8,12},{9,11},{10,... | collective-permute-start | bytes 196616 | tf_op jit(solution)/shard_map/ppermute | solution.py:327
  56.5 2.2 %collective-permute-start.25 = (f32[1,128,256]{2,1,0:T(8,128)S(1)}, f32[1,128,256]{2,1,0:T(8,128)S(1)}, u32[]{:S(2)}, u32[]{:S(2)}) collective-permute-start(f32[1,128,256]{2,1,0:T(8,128)S(1)} %shard_map.86.refs_4_.refs_0_), channel_id=1, source_target_pairs={{0,16},{1,17},{2,18},{3,19},{4,20},{5,21},{6,22},{7,23},{8,24},{9,... | collective-permute-start | bytes 393224 | tf_op jit(solution)/shard_map/ppermute | solution.py:327
  58.8 0.2 collective-permute-done.26.refs_1_
  59.0 0.1 shard_map.87
  59.1 1.9 %collective-permute-start.27 = (f32[1,64,256]{2,1,0:T(8,128)S(1)}, f32[1,64,256]{2,1,0:T(8,128)S(1)}, u32[]{:S(2)}, u32[]{:S(2)}) collective-permute-start(f32[1,64,256]{2,1,0:T(8,128)S(1)} %get-tuple-element.106.refs_0_), channel_id=1, source_target_pairs={{0,4},{1,3},{2,6},{3,1},{4,0},{5,7},{6,2},{7,5},{8,12},{9,11},{10,... | collective-permute-start | bytes 196616 | tf_op jit(solution)/shard_map/ppermute | solution.py:327
  61.0 3.1 %collective-permute-done.27.refs_1_ = f32[1,64,256]{2,1,0:T(8,128)S(1)} collective-permute-done((f32[1,64,256]{2,1,0:T(8,128)S(1)}, f32[1,64,256]{2,1,0:T(8,128)S(1)}, u32[]{:S(2)}, u32[]{:S(2)}) %collective-permute-start.27) | collective-permute-done | bytes 65568 | tf_op jit(solution)/shard_map/ppermute | solution.py:327
  64.2 1.4 %collective-permute-start.32 = (f32[2,64,256]{2,1,0:T(8,128)S(1)}, f32[2,64,256]{2,1,0:T(8,128)S(1)}, u32[]{:S(2)}, u32[]{:S(2)}) collective-permute-start(f32[2,64,256]{2,1,0:T(8,128)S(1)} %shard_map.89.refs_4_.refs_0_), channel_id=1, source_target_pairs={{0,2},{1,5},{2,0},{3,7},{4,6},{5,1},{6,4},{7,3},{8,10},{9,13},{10,... | collective-permute-start | bytes 393224 | tf_op jit(solution)/shard_map/ppermute | solution.py:327
  65.6 0.1 shard_map.90.refs_2_.refs_0_
  65.7 0.8 collective-permute-start.31
  66.6 0.4 collective-permute-start.29
  67.0 2.2 %collective-permute-done.32.refs_1_ = f32[2,64,256]{2,1,0:T(8,128)S(1)} collective-permute-done((f32[2,64,256]{2,1,0:T(8,128)S(1)}, f32[2,64,256]{2,1,0:T(8,128)S(1)}, u32[]{:S(2)}, u32[]{:S(2)}) %collective-permute-start.32) | collective-permute-done | bytes 131104 | tf_op jit(solution)/shard_map/ppermute | solution.py:327
  69.2 0.5 collective-permute-start.34
  69.8 0.4 collective-permute-done.31.refs_1_
  70.2 1.5 %collective-permute-start.36 = (f32[2,72,256]{2,1,0:T(8,128)S(1)}, f32[2,72,256]{2,1,0:T(8,128)S(1)}, u32[]{:S(2)}, u32[]{:S(2)}) collective-permute-start(f32[2,72,256]{2,1,0:T(8,128)S(1)} %shard_map.93.refs_2_.refs_0_), channel_id=1, source_target_pairs={{0,4},{1,3},{2,6},{3,1},{4,0},{5,7},{6,2},{7,5},{8,12},{9,11},{10,... | collective-permute-start | bytes 442376 | tf_op jit(solution)/shard_map/ppermute | solution.py:327
  71.7 2.0 %collective-permute-start.35 = (f32[4,64,256]{2,1,0:T(8,128)S(1)}, f32[4,64,256]{2,1,0:T(8,128)S(1)}, u32[]{:S(2)}, u32[]{:S(2)}) collective-permute-start(f32[4,64,256]{2,1,0:T(8,128)S(1)} %shard_map.94.refs_2_.refs_0_), channel_id=1, source_target_pairs={{0,2},{1,5},{2,0},{3,7},{4,6},{5,1},{6,4},{7,3},{8,10},{9,13},{10,... | collective-permute-start | bytes 786440 | tf_op jit(solution)/shard_map/ppermute | solution.py:327
  73.9 1.5 %collective-permute-done.36.refs_1_ = f32[2,72,256]{2,1,0:T(8,128)S(1)} collective-permute-done((f32[2,72,256]{2,1,0:T(8,128)S(1)}, f32[2,72,256]{2,1,0:T(8,128)S(1)}, u32[]{:S(2)}, u32[]{:S(2)}) %collective-permute-start.36) | collective-permute-done | bytes 147488 | tf_op jit(solution)/shard_map/ppermute | solution.py:327
  75.4 1.5 %collective-permute-start.39 = (f32[4,72,256]{2,1,0:T(8,128)S(1)}, f32[4,72,256]{2,1,0:T(8,128)S(1)}, u32[]{:S(2)}, u32[]{:S(2)}) collective-permute-start(f32[4,72,256]{2,1,0:T(8,128)S(1)} %shard_map.96.refs_2_.refs_0_), channel_id=1, source_target_pairs={{0,2},{1,5},{2,0},{3,7},{4,6},{5,1},{6,4},{7,3},{8,10},{9,13},{10,... | collective-permute-start | bytes 884744 | tf_op jit(solution)/shard_map/ppermute | solution.py:327
  76.9 1.3 %collective-permute-done.35.refs_1_ = f32[4,64,256]{2,1,0:T(8,128)S(1)} collective-permute-done((f32[4,64,256]{2,1,0:T(8,128)S(1)}, f32[4,64,256]{2,1,0:T(8,128)S(1)}, u32[]{:S(2)}, u32[]{:S(2)}) %collective-permute-start.35) | collective-permute-done | bytes 262176 | tf_op jit(solution)/shard_map/ppermute | solution.py:327
  78.3 0.5 collective-permute-start.38
  78.9 1.1 %shard_map.99 = (f32[2,8,8,32,256]{4,3,2,1,0:T(8,128)}, f32[8,128]{1,0:T(8,128)S(1)}) custom-call(f32[8,64,256]{2,1,0:T(8,128)S(1)} %shard_map.95.refs_2_.refs_0_, f32[8,64,256]{2,1,0:T(8,128)S(1)} %collective-permute-done.33.refs_1_, f32[8,64,256]{2,1,0:T(8,128)S(1)} %shard_map.98.refs_2_.refs_1_), custom_call_target="tpu_custom_call" | custom-call | flops 10000000000 | bytes 1024 | tf_op jit(solution)/shard_map/pallas_call | solution.py:172
  80.0 0.2 collective-permute-done.37.refs_2_
  80.2 1.1 %shard_map.100 = (f32[2,8,8,32,256]{4,3,2,1,0:T(8,128)}, f32[8,128]{1,0:T(8,128)S(1)}) custom-call(f32[2,8,8,32,256]{4,3,2,1,0:T(8,128)} %get-tuple-element.108.refs_0_, f32[8,64,256]{2,1,0:T(8,128)S(1)} %shard_map.97.refs_2_.refs_1_, f32[8,64,256]{2,1,0:T(8,128)S(1)} %collective-permute-done.37.refs_2_, ...), custom_call_target="tpu_custom_call", output_to_operand_aliasing={{0}: (0, {})} | custom-call | flops 10000000000 | bytes 1024 | tf_op jit(solution)/shard_map/pallas_call | solution.py:172
  81.3 0.9 %collective-permute-done.39.refs_1_ = f32[4,72,256]{2,1,0:T(8,128)S(1)} collective-permute-done((f32[4,72,256]{2,1,0:T(8,128)S(1)}, f32[4,72,256]{2,1,0:T(8,128)S(1)}, u32[]{:S(2)}, u32[]{:S(2)}) %collective-permute-start.39) | collective-permute-done | bytes 294944 | tf_op jit(solution)/shard_map/ppermute | solution.py:327
  82.3 1.1 %shard_map.102 = (f32[2,8,8,32,256]{4,3,2,1,0:T(8,128)}, f32[8,128]{1,0:T(8,128)S(1)}) custom-call(f32[2,8,8,32,256]{4,3,2,1,0:T(8,128)} %get-tuple-element.110.refs_0_, f32[8,64,256]{2,1,0:T(8,128)S(1)} %shard_map.98.refs_2_.refs_1_, f32[8,64,256]{2,1,0:T(8,128)S(1)} %collective-permute-done.38.refs_2_, ...), custom_call_target="tpu_custom_call", output_to_operand_aliasing={{0}: (0, {})} | custom-call | flops 10000000000 | bytes 1024 | tf_op jit(solution)/shard_map/pallas_call | solution.py:172
  83.4 0.9 %collective-permute-done.40.refs_2_ = f32[8,72,256]{2,1,0:T(8,128)S(1)} collective-permute-done((f32[8,72,256]{2,1,0:T(8,128)S(1)}, f32[8,72,256]{2,1,0:T(8,128)S(1)}, u32[]{:S(2)}, u32[]{:S(2)}) %collective-permute-start.40) | collective-permute-done | bytes 589856 | tf_op jit(solution)/shard_map/ppermute | solution.py:327
  84.3 1.8 %shard_map.103 = (f32[2,8,8,32,256]{4,3,2,1,0:T(8,128)}, f32[2,64,256]{2,1,0:T(8,128)}) custom-call(f32[2,8,8,32,256]{4,3,2,1,0:T(8,128)} %get-tuple-element.112.refs_0_, f32[8,72,256]{2,1,0:T(8,128)S(1)} %shard_map.101.refs_3_.refs_1_, f32[8,72,256]{2,1,0:T(8,128)S(1)} %collective-permute-done.40.refs_2_, ...), custom_call_target="tpu_custom_call", output_to_operand_aliasing={{0}: (0, {})} | custom-call | flops 10000000000 | bytes 1024 | tf_op jit(solution)/shard_map/pallas_call | solution.py:172
  (63 shorter events, 1.3 us)
Async XLA Ops:
  3.7 3.2 %collective-permute-start = (f32[8,72,256]{2,1,0:T(8,128)S(1)}, f32[8,72,256]{2,1,0:T(8,128)S(1)}, u32[]{:S(2)}, u32[]{:S(2)}) collective-permute-start(f32[8,72,256]{2,1,0:T(8,128)S(1)} %get-tuple-element.60), channel_id=1, source_target_pairs={{0,1},{1,0},{2,3},{3,2},{4,5},{5,4},{6,7},{7,6},{8,9},{9,8},{10,11... | collective-permute-start | bytes 1769480 | tf_op jit(solution)/shard_map/ppermute | solution.py:327
  6.8 4.6 %collective-permute-start.3 = (f32[8,128,256]{2,1,0:T(8,128)S(1)}, f32[8,128,256]{2,1,0:T(8,128)S(1)}, u32[]{:S(2)}, u32[]{:S(2)}) collective-permute-start(f32[8,128,256]{2,1,0:T(8,128)S(1)} %get-tuple-element.63.refs_2_), channel_id=1, source_target_pairs={{0,1},{1,0},{2,3},{3,2},{4,5},{5,4},{6,7},{7,6},{8,9},{9,8},{10,11... | collective-permute-start | bytes 3145736 | tf_op jit(solution)/shard_map/ppermute | solution.py:327
  7.0 10.3 %collective-permute-start.1 = (f32[4,72,256]{2,1,0:T(8,128)S(1)}, f32[4,72,256]{2,1,0:T(8,128)S(1)}, u32[]{:S(2)}, u32[]{:S(2)}) collective-permute-start(f32[4,72,256]{2,1,0:T(8,128)S(1)} %get-tuple-element.65.refs_2_), channel_id=1, source_target_pairs={{0,8},{1,9},{2,10},{3,11},{4,12},{5,13},{6,14},{7,15},{8,0},{9,1},... | collective-permute-start | bytes 884744 | tf_op jit(solution)/shard_map/ppermute | solution.py:327
  11.3 4.6 %collective-permute-start.2 = (f32[8,64,256]{2,1,0:T(8,128)S(1)}, f32[8,64,256]{2,1,0:T(8,128)S(1)}, u32[]{:S(2)}, u32[]{:S(2)}) collective-permute-start(f32[8,64,256]{2,1,0:T(8,128)S(1)} %get-tuple-element.67.refs_2_), channel_id=1, source_target_pairs={{0,1},{1,0},{2,3},{3,2},{4,5},{5,4},{6,7},{7,6},{8,9},{9,8},{10,11... | collective-permute-start | bytes 1572872 | tf_op jit(solution)/shard_map/ppermute | solution.py:327
  11.5 11.0 %collective-permute-start.6 = (f32[4,128,256]{2,1,0:T(8,128)S(1)}, f32[4,128,256]{2,1,0:T(8,128)S(1)}, u32[]{:S(2)}, u32[]{:S(2)}) collective-permute-start(f32[4,128,256]{2,1,0:T(8,128)S(1)} %get-tuple-element.69.refs_2_), channel_id=1, source_target_pairs={{0,2},{1,5},{2,0},{3,7},{4,6},{5,1},{6,4},{7,3},{8,10},{9,13},{10,... | collective-permute-start | bytes 1572872 | tf_op jit(solution)/shard_map/ppermute | solution.py:327
  15.6 3.4 %collective-permute-start.7 = (f32[8,128,256]{2,1,0:T(8,128)S(1)}, f32[8,128,256]{2,1,0:T(8,128)S(1)}, u32[]{:S(2)}, u32[]{:S(2)}) collective-permute-start(f32[8,128,256]{2,1,0:T(8,128)S(1)} %get-tuple-element.70.refs_2_), channel_id=1, source_target_pairs={{0,1},{1,0},{2,3},{3,2},{4,5},{5,4},{6,7},{7,6},{8,9},{9,8},{10,11... | collective-permute-start | bytes 3145736 | tf_op jit(solution)/shard_map/ppermute | solution.py:327
  16.0 8.6 %collective-permute-start.5 = (f32[4,64,256]{2,1,0:T(8,128)S(1)}, f32[4,64,256]{2,1,0:T(8,128)S(1)}, u32[]{:S(2)}, u32[]{:S(2)}) collective-permute-start(f32[4,64,256]{2,1,0:T(8,128)S(1)} %get-tuple-element.71.refs_2_), channel_id=1, source_target_pairs={{0,8},{1,9},{2,10},{3,11},{4,12},{5,13},{6,14},{7,15},{8,0},{9,1},... | collective-permute-start | bytes 786440 | tf_op jit(solution)/shard_map/ppermute | solution.py:327
  17.3 8.6 %collective-permute-start.4 = (f32[2,72,256]{2,1,0:T(8,128)S(1)}, f32[2,72,256]{2,1,0:T(8,128)S(1)}, u32[]{:S(2)}, u32[]{:S(2)}) collective-permute-start(f32[2,72,256]{2,1,0:T(8,128)S(1)} %get-tuple-element.73.refs_2_), channel_id=1, source_target_pairs={{0,2},{1,5},{2,0},{3,7},{4,6},{5,1},{6,4},{7,3},{8,10},{9,13},{10,... | collective-permute-start | bytes 442376 | tf_op jit(solution)/shard_map/ppermute | solution.py:327
  19.2 9.3 %collective-permute-start.9 = (f32[4,128,256]{2,1,0:T(8,128)S(1)}, f32[4,128,256]{2,1,0:T(8,128)S(1)}, u32[]{:S(2)}, u32[]{:S(2)}) collective-permute-start(f32[4,128,256]{2,1,0:T(8,128)S(1)} %get-tuple-element.77.refs_2_), channel_id=1, source_target_pairs={{0,2},{1,5},{2,0},{3,7},{4,6},{5,1},{6,4},{7,3},{8,10},{9,13},{10,... | collective-permute-start | bytes 1572872 | tf_op jit(solution)/shard_map/ppermute | solution.py:327
  22.5 5.0 %collective-permute-start.10 = (f32[8,128,256]{2,1,0:T(8,128)S(1)}, f32[8,128,256]{2,1,0:T(8,128)S(1)}, u32[]{:S(2)}, u32[]{:S(2)}) collective-permute-start(f32[8,128,256]{2,1,0:T(8,128)S(1)} %get-tuple-element.78.refs_2_), channel_id=1, source_target_pairs={{0,1},{1,0},{2,3},{3,2},{4,5},{5,4},{6,7},{7,6},{8,9},{9,8},{10,11... | collective-permute-start | bytes 3145736 | tf_op jit(solution)/shard_map/ppermute | solution.py:327
  22.6 12.8 %collective-permute-start.15 = (f32[2,128,256]{2,1,0:T(8,128)S(1)}, f32[2,128,256]{2,1,0:T(8,128)S(1)}, u32[]{:S(2)}, u32[]{:S(2)}) collective-permute-start(f32[2,128,256]{2,1,0:T(8,128)S(1)} %get-tuple-element.79.refs_2_), channel_id=1, source_target_pairs={{0,8},{1,9},{2,10},{3,11},{4,12},{5,13},{6,14},{7,15},{8,0},{9,1},... | collective-permute-start | bytes 786440 | tf_op jit(solution)/shard_map/ppermute | solution.py:327
  24.6 9.0 %collective-permute-start.12 = (f32[2,64,256]{2,1,0:T(8,128)S(1)}, f32[2,64,256]{2,1,0:T(8,128)S(1)}, u32[]{:S(2)}, u32[]{:S(2)}) collective-permute-start(f32[2,64,256]{2,1,0:T(8,128)S(1)} %get-tuple-element.80.refs_2_), channel_id=1, source_target_pairs={{0,2},{1,5},{2,0},{3,7},{4,6},{5,1},{6,4},{7,3},{8,10},{9,13},{10,... | collective-permute-start | bytes 393224 | tf_op jit(solution)/shard_map/ppermute | solution.py:327
  25.9 5.0 %collective-permute-start.8 = (f32[1,72,256]{2,1,0:T(8,128)S(1)}, f32[1,72,256]{2,1,0:T(8,128)S(1)}, u32[]{:S(2)}, u32[]{:S(2)}) collective-permute-start(f32[1,72,256]{2,1,0:T(8,128)S(1)} %get-tuple-element.82.refs_2_), channel_id=1, source_target_pairs={{0,4},{1,3},{2,6},{3,1},{4,0},{5,7},{6,2},{7,5},{8,12},{9,11},{10,... | collective-permute-start | bytes 221192 | tf_op jit(solution)/shard_map/ppermute | solution.py:327
  27.6 10.9 %collective-permute-start.14 = (f32[4,128,256]{2,1,0:T(8,128)S(1)}, f32[4,128,256]{2,1,0:T(8,128)S(1)}, u32[]{:S(2)}, u32[]{:S(2)}) collective-permute-start(f32[4,128,256]{2,1,0:T(8,128)S(1)} %get-tuple-element.85.refs_2_), channel_id=1, source_target_pairs={{0,2},{1,5},{2,0},{3,7},{4,6},{5,1},{6,4},{7,3},{8,10},{9,13},{10,... | collective-permute-start | bytes 1572872 | tf_op jit(solution)/shard_map/ppermute | solution.py:327
  28.5 14.4 %collective-permute-start.18 = (f32[2,128,256]{2,1,0:T(8,128)S(1)}, f32[2,128,256]{2,1,0:T(8,128)S(1)}, u32[]{:S(2)}, u32[]{:S(2)}) collective-permute-start(f32[2,128,256]{2,1,0:T(8,128)S(1)} %get-tuple-element.86.refs_2_), channel_id=1, source_target_pairs={{0,8},{1,9},{2,10},{3,11},{4,12},{5,13},{6,14},{7,15},{8,0},{9,1},... | collective-permute-start | bytes 786440 | tf_op jit(solution)/shard_map/ppermute | solution.py:327
  30.9 16.3 %collective-permute-start.11 = (f32[1,72,256]{2,1,0:T(8,128)S(1)}, f32[1,72,256]{2,1,0:T(8,128)S(1)}, u32[]{:S(2)}, u32[]{:S(2)}) collective-permute-start(f32[1,72,256]{2,1,0:T(8,128)S(1)} %shard_map.74.refs_2_.refs_0_), channel_id=1, source_target_pairs={{0,16},{1,17},{2,18},{3,19},{4,20},{5,21},{6,22},{7,23},{8,24},{9,... | collective-permute-start | bytes 221192 | tf_op jit(solution)/shard_map/ppermute | solution.py:327
  33.6 6.3 %collective-permute-start.13 = (f32[1,64,256]{2,1,0:T(8,128)S(1)}, f32[1,64,256]{2,1,0:T(8,128)S(1)}, u32[]{:S(2)}, u32[]{:S(2)}) collective-permute-start(f32[1,64,256]{2,1,0:T(8,128)S(1)} %get-tuple-element.89.refs_2_), channel_id=1, source_target_pairs={{0,4},{1,3},{2,6},{3,1},{4,0},{5,7},{6,2},{7,5},{8,12},{9,11},{10,... | collective-permute-start | bytes 196616 | tf_op jit(solution)/shard_map/ppermute | solution.py:327
  35.5 7.3 %collective-permute-start.19 = (f32[1,128,256]{2,1,0:T(8,128)S(1)}, f32[1,128,256]{2,1,0:T(8,128)S(1)}, u32[]{:S(2)}, u32[]{:S(2)}) collective-permute-start(f32[1,128,256]{2,1,0:T(8,128)S(1)} %get-tuple-element.92.refs_2_), channel_id=1, source_target_pairs={{0,4},{1,3},{2,6},{3,1},{4,0},{5,7},{6,2},{7,5},{8,12},{9,11},{10,... | collective-permute-start | bytes 393224 | tf_op jit(solution)/shard_map/ppermute | solution.py:327
  38.5 6.4 %collective-permute-start.17 = (f32[2,128,256]{2,1,0:T(8,128)S(1)}, f32[2,128,256]{2,1,0:T(8,128)S(1)}, u32[]{:S(2)}, u32[]{:S(2)}) collective-permute-start(f32[2,128,256]{2,1,0:T(8,128)S(1)} %get-tuple-element.93.refs_2_), channel_id=1, source_target_pairs={{0,4},{1,3},{2,6},{3,1},{4,0},{5,7},{6,2},{7,5},{8,12},{9,11},{10,... | collective-permute-start | bytes 786440 | tf_op jit(solution)/shard_map/ppermute | solution.py:327
  39.9 7.3 %collective-permute-start.16 = (f32[1,64,256]{2,1,0:T(8,128)S(1)}, f32[1,64,256]{2,1,0:T(8,128)S(1)}, u32[]{:S(2)}, u32[]{:S(2)}) collective-permute-start(f32[1,64,256]{2,1,0:T(8,128)S(1)} %shard_map.78.refs_2_), channel_id=1, source_target_pairs={{0,16},{1,17},{2,18},{3,19},{4,20},{5,21},{6,22},{7,23},{8,24},{9,... | collective-permute-start | bytes 196616 | tf_op jit(solution)/shard_map/ppermute | solution.py:327
  42.7 12.2 %collective-permute-start.24 = (f32[1,128,256]{2,1,0:T(8,128)S(1)}, f32[1,128,256]{2,1,0:T(8,128)S(1)}, u32[]{:S(2)}, u32[]{:S(2)}) collective-permute-start(f32[1,128,256]{2,1,0:T(8,128)S(1)} %shard_map.79.refs_2_.refs_0_), channel_id=1, source_target_pairs={{0,16},{1,17},{2,18},{3,19},{4,20},{5,21},{6,22},{7,23},{8,24},{9,... | collective-permute-start | bytes 393224 | tf_op jit(solution)/shard_map/ppermute | solution.py:327
  43.0 6.4 %collective-permute-start.21 = (f32[1,128,256]{2,1,0:T(8,128)S(1)}, f32[1,128,256]{2,1,0:T(8,128)S(1)}, u32[]{:S(2)}, u32[]{:S(2)}) collective-permute-start(f32[1,128,256]{2,1,0:T(8,128)S(1)} %get-tuple-element.97.refs_2_), channel_id=1, source_target_pairs={{0,4},{1,3},{2,6},{3,1},{4,0},{5,7},{6,2},{7,5},{8,12},{9,11},{10,... | collective-permute-start | bytes 393224 | tf_op jit(solution)/shard_map/ppermute | solution.py:327
  45.0 11.5 %collective-permute-start.23 = (f32[1,128,256]{2,1,0:T(8,128)S(1)}, f32[1,128,256]{2,1,0:T(8,128)S(1)}, u32[]{:S(2)}, u32[]{:S(2)}) collective-permute-start(f32[1,128,256]{2,1,0:T(8,128)S(1)} %get-tuple-element.98.refs_4_), channel_id=1, source_target_pairs={{0,8},{1,9},{2,10},{3,11},{4,12},{5,13},{6,14},{7,15},{8,0},{9,1},... | collective-permute-start | bytes 393224 | tf_op jit(solution)/shard_map/ppermute | solution.py:327
  47.3 4.8 %collective-permute-start.20 = (f32[1,64,256]{2,1,0:T(8,128)S(1)}, f32[1,64,256]{2,1,0:T(8,128)S(1)}, u32[]{:S(2)}, u32[]{:S(2)}) collective-permute-start(f32[1,64,256]{2,1,0:T(8,128)S(1)} %get-tuple-element.99.refs_0_), channel_id=1, source_target_pairs={{0,4},{1,3},{2,6},{3,1},{4,0},{5,7},{6,2},{7,5},{8,12},{9,11},{10,... | collective-permute-start | bytes 196616 | tf_op jit(solution)/shard_map/ppermute | solution.py:327
  49.4 9.6 %collective-permute-start.26 = (f32[1,128,256]{2,1,0:T(8,128)S(1)}, f32[1,128,256]{2,1,0:T(8,128)S(1)}, u32[]{:S(2)}, u32[]{:S(2)}) collective-permute-start(f32[1,128,256]{2,1,0:T(8,128)S(1)} %shard_map.83.refs_2_.refs_0_), channel_id=1, source_target_pairs={{0,16},{1,17},{2,18},{3,19},{4,20},{5,21},{6,22},{7,23},{8,24},{9,... | collective-permute-start | bytes 393224 | tf_op jit(solution)/shard_map/ppermute | solution.py:327
  52.2 14.4 %collective-permute-start.22 = (f32[2,64,256]{2,1,0:T(8,128)S(1)}, f32[2,64,256]{2,1,0:T(8,128)S(1)}, u32[]{:S(2)}, u32[]{:S(2)}) collective-permute-start(f32[2,64,256]{2,1,0:T(8,128)S(1)} %shard_map.84.refs_4_.refs_0_), channel_id=1, source_target_pairs={{0,8},{1,9},{2,10},{3,11},{4,12},{5,13},{6,14},{7,15},{8,0},{9,1},... | collective-permute-start | bytes 393224 | tf_op jit(solution)/shard_map/ppermute | solution.py:327
  55.1 5.8 %collective-permute-start.28 = (f32[1,64,256]{2,1,0:T(8,128)S(1)}, f32[1,64,256]{2,1,0:T(8,128)S(1)}, u32[]{:S(2)}, u32[]{:S(2)}) collective-permute-start(f32[1,64,256]{2,1,0:T(8,128)S(1)} %get-tuple-element.107.refs_0_), channel_id=1, source_target_pairs={{0,4},{1,3},{2,6},{3,1},{4,0},{5,7},{6,2},{7,5},{8,12},{9,11},{10,... | collective-permute-start | bytes 196616 | tf_op jit(solution)/shard_map/ppermute | solution.py:327
  56.5 9.1 %collective-permute-start.25 = (f32[1,128,256]{2,1,0:T(8,128)S(1)}, f32[1,128,256]{2,1,0:T(8,128)S(1)}, u32[]{:S(2)}, u32[]{:S(2)}) collective-permute-start(f32[1,128,256]{2,1,0:T(8,128)S(1)} %shard_map.86.refs_4_.refs_0_), channel_id=1, source_target_pairs={{0,16},{1,17},{2,18},{3,19},{4,20},{5,21},{6,22},{7,23},{8,24},{9,... | collective-permute-start | bytes 393224 | tf_op jit(solution)/shard_map/ppermute | solution.py:327
  59.1 5.1 %collective-permute-start.27 = (f32[1,64,256]{2,1,0:T(8,128)S(1)}, f32[1,64,256]{2,1,0:T(8,128)S(1)}, u32[]{:S(2)}, u32[]{:S(2)}) collective-permute-start(f32[1,64,256]{2,1,0:T(8,128)S(1)} %get-tuple-element.106.refs_0_), channel_id=1, source_target_pairs={{0,4},{1,3},{2,6},{3,1},{4,0},{5,7},{6,2},{7,5},{8,12},{9,11},{10,... | collective-permute-start | bytes 196616 | tf_op jit(solution)/shard_map/ppermute | solution.py:327
  61.0 10.8 %collective-permute-start.30 = (f32[2,64,256]{2,1,0:T(8,128)S(1)}, f32[2,64,256]{2,1,0:T(8,128)S(1)}, u32[]{:S(2)}, u32[]{:S(2)}) collective-permute-start(f32[2,64,256]{2,1,0:T(8,128)S(1)} %shard_map.88.refs_2_.refs_0_), channel_id=1, source_target_pairs={{0,8},{1,9},{2,10},{3,11},{4,12},{5,13},{6,14},{7,15},{8,0},{9,1},... | collective-permute-start | bytes 393224 | tf_op jit(solution)/shard_map/ppermute | solution.py:327
  64.2 5.0 %collective-permute-start.32 = (f32[2,64,256]{2,1,0:T(8,128)S(1)}, f32[2,64,256]{2,1,0:T(8,128)S(1)}, u32[]{:S(2)}, u32[]{:S(2)}) collective-permute-start(f32[2,64,256]{2,1,0:T(8,128)S(1)} %shard_map.89.refs_4_.refs_0_), channel_id=1, source_target_pairs={{0,2},{1,5},{2,0},{3,7},{4,6},{5,1},{6,4},{7,3},{8,10},{9,13},{10,... | collective-permute-start | bytes 393224 | tf_op jit(solution)/shard_map/ppermute | solution.py:327
  65.7 4.4 %collective-permute-start.31 = (f32[1,72,256]{2,1,0:T(8,128)S(1)}, f32[1,72,256]{2,1,0:T(8,128)S(1)}, u32[]{:S(2)}, u32[]{:S(2)}) collective-permute-start(f32[1,72,256]{2,1,0:T(8,128)S(1)} %shard_map.90.refs_2_.refs_0_), channel_id=1, source_target_pairs={{0,8},{1,9},{2,10},{3,11},{4,12},{5,13},{6,14},{7,15},{8,0},{9,1},... | collective-permute-start | bytes 221192 | tf_op jit(solution)/shard_map/ppermute | solution.py:327
  66.6 7.2 %collective-permute-start.29 = (f32[4,64,256]{2,1,0:T(8,128)S(1)}, f32[4,64,256]{2,1,0:T(8,128)S(1)}, u32[]{:S(2)}, u32[]{:S(2)}) collective-permute-start(f32[4,64,256]{2,1,0:T(8,128)S(1)} %shard_map.91.refs_2_.refs_0_), channel_id=1, source_target_pairs={{0,2},{1,5},{2,0},{3,7},{4,6},{5,1},{6,4},{7,3},{8,10},{9,13},{10,... | collective-permute-start | bytes 786440 | tf_op jit(solution)/shard_map/ppermute | solution.py:327
  69.2 9.1 %collective-permute-start.34 = (f32[4,64,256]{2,1,0:T(8,128)S(1)}, f32[4,64,256]{2,1,0:T(8,128)S(1)}, u32[]{:S(2)}, u32[]{:S(2)}) collective-permute-start(f32[4,64,256]{2,1,0:T(8,128)S(1)} %shard_map.92.refs_2_.refs_0_), channel_id=1, source_target_pairs={{0,8},{1,9},{2,10},{3,11},{4,12},{5,13},{6,14},{7,15},{8,0},{9,1},... | collective-permute-start | bytes 786440 | tf_op jit(solution)/shard_map/ppermute | solution.py:327
  70.2 5.2 %collective-permute-start.36 = (f32[2,72,256]{2,1,0:T(8,128)S(1)}, f32[2,72,256]{2,1,0:T(8,128)S(1)}, u32[]{:S(2)}, u32[]{:S(2)}) collective-permute-start(f32[2,72,256]{2,1,0:T(8,128)S(1)} %shard_map.93.refs_2_.refs_0_), channel_id=1, source_target_pairs={{0,4},{1,3},{2,6},{3,1},{4,0},{5,7},{6,2},{7,5},{8,12},{9,11},{10,... | collective-permute-start | bytes 442376 | tf_op jit(solution)/shard_map/ppermute | solution.py:327
  71.7 6.4 %collective-permute-start.35 = (f32[4,64,256]{2,1,0:T(8,128)S(1)}, f32[4,64,256]{2,1,0:T(8,128)S(1)}, u32[]{:S(2)}, u32[]{:S(2)}) collective-permute-start(f32[4,64,256]{2,1,0:T(8,128)S(1)} %shard_map.94.refs_2_.refs_0_), channel_id=1, source_target_pairs={{0,2},{1,5},{2,0},{3,7},{4,6},{5,1},{6,4},{7,3},{8,10},{9,13},{10,... | collective-permute-start | bytes 786440 | tf_op jit(solution)/shard_map/ppermute | solution.py:327
  73.8 5.1 %collective-permute-start.33 = (f32[8,64,256]{2,1,0:T(8,128)S(1)}, f32[8,64,256]{2,1,0:T(8,128)S(1)}, u32[]{:S(2)}, u32[]{:S(2)}) collective-permute-start(f32[8,64,256]{2,1,0:T(8,128)S(1)} %shard_map.95.refs_2_.refs_0_), channel_id=1, source_target_pairs={{0,1},{1,0},{2,3},{3,2},{4,5},{5,4},{6,7},{7,6},{8,9},{9,8},{10,11... | collective-permute-start | bytes 1572872 | tf_op jit(solution)/shard_map/ppermute | solution.py:327
  75.4 6.8 %collective-permute-start.39 = (f32[4,72,256]{2,1,0:T(8,128)S(1)}, f32[4,72,256]{2,1,0:T(8,128)S(1)}, u32[]{:S(2)}, u32[]{:S(2)}) collective-permute-start(f32[4,72,256]{2,1,0:T(8,128)S(1)} %shard_map.96.refs_2_.refs_0_), channel_id=1, source_target_pairs={{0,2},{1,5},{2,0},{3,7},{4,6},{5,1},{6,4},{7,3},{8,10},{9,13},{10,... | collective-permute-start | bytes 884744 | tf_op jit(solution)/shard_map/ppermute | solution.py:327
  78.2 2.0 %collective-permute-start.37 = (f32[8,64,256]{2,1,0:T(8,128)S(1)}, f32[8,64,256]{2,1,0:T(8,128)S(1)}, u32[]{:S(2)}, u32[]{:S(2)}) collective-permute-start(f32[8,64,256]{2,1,0:T(8,128)S(1)} %shard_map.97.refs_2_.refs_1_), channel_id=1, source_target_pairs={{0,1},{1,0},{2,3},{3,2},{4,5},{5,4},{6,7},{7,6},{8,9},{9,8},{10,11... | collective-permute-start | bytes 1572872 | tf_op jit(solution)/shard_map/ppermute | solution.py:327
  78.3 4.0 %collective-permute-start.38 = (f32[8,64,256]{2,1,0:T(8,128)S(1)}, f32[8,64,256]{2,1,0:T(8,128)S(1)}, u32[]{:S(2)}, u32[]{:S(2)}) collective-permute-start(f32[8,64,256]{2,1,0:T(8,128)S(1)} %shard_map.98.refs_2_.refs_1_), channel_id=1, source_target_pairs={{0,1},{1,0},{2,3},{3,2},{4,5},{5,4},{6,7},{7,6},{8,9},{9,8},{10,11... | collective-permute-start | bytes 1572872 | tf_op jit(solution)/shard_map/ppermute | solution.py:327
  82.2 2.1 %collective-permute-start.40 = (f32[8,72,256]{2,1,0:T(8,128)S(1)}, f32[8,72,256]{2,1,0:T(8,128)S(1)}, u32[]{:S(2)}, u32[]{:S(2)}) collective-permute-start(f32[8,72,256]{2,1,0:T(8,128)S(1)} %shard_map.101.refs_3_.refs_1_), channel_id=1, source_target_pairs={{0,1},{1,0},{2,3},{3,2},{4,5},{5,4},{6,7},{7,6},{8,9},{9,8},{10,11... | collective-permute-start | bytes 1769480 | tf_op jit(solution)/shard_map/ppermute | solution.py:327
